TPU v7x, 32 devices: a whole 2x2x4 slice. The times are simulated.
32 devices in a mesh: batch: 8 (over y, x, core), proto: 4 (over z).
Axes of the slice: x: 2, y: 2, z: 4, core: 2. Of those that a mesh axis runs over, the one named last changes fastest.
Arguments:
- features: bfloat16 [2, 8192, 256], P(None, 'batch'), may hold values from -6 to 6
- prototypes: bfloat16 [32768, 256], P('proto'), may hold values from -6 to 6
Outputs:
- grad_features: float32 [2, 8192, 256], P(None, 'batch')
- grad_prototypes: float32 [32768, 256], P('proto')
All inputs are finite; a program needn't handle non-finite values.
Results may differ from a plain program's by a relative error of at most 0.0027.
Values sent between devices are 32-bit elements; how exact they have to be, the bound alone decides.
No kernel may reach another device: no remote copies, remote signals or barrier semaphores. Data moves between devices by JAX's collectives and lax.ppermute only.
A program may use at most 384 MiB of HBM per device.

v0:
```python
import jax
import jax.numpy as jnp
from jax import lax
from jax.sharding import PartitionSpec as P

ITERS = 3


code_temp = 0.05
soft_temp = 0.1


def norm_back(grad, unit, inverse):
    return inverse * (grad - unit * jnp.sum(unit * grad, axis=-1, keepdims=True))


def per_device(features, prototypes):
    rows_here = features.shape[1]
    width = features.shape[2]
    protos_here = prototypes.shape[0]
    feat = features.astype(jnp.float32)
    inv_feat = lax.rsqrt(jnp.sum(feat * feat, axis=-1, keepdims=True) + 1e-06)
    unit_feat = feat * inv_feat
    embed = unit_feat.astype(jnp.bfloat16)
    proto = prototypes.astype(jnp.float32)
    inv_proto = lax.rsqrt(jnp.sum(proto * proto, axis=-1, keepdims=True) + 1e-06)
    unit_proto = proto * inv_proto
    centers = unit_proto.astype(jnp.bfloat16)
    flat_embed = embed.reshape(2 * rows_here, width)
    scores = jnp.dot(flat_embed, centers.T, preferred_element_type=jnp.float32).reshape(
        2, rows_here, protos_here
    )
    base = jnp.exp(scores / code_temp)
    expo = jnp.exp(scores / soft_temp)
    totals = lax.psum(jnp.sum(expo, axis=2), "proto")
    row_scale = jnp.ones((2, rows_here), jnp.float32)
    col_scale = jnp.ones((2, protos_here), jnp.float32)
    for step in range(ITERS):
        col_part = jnp.sum(base * row_scale[:, :, None], axis=1)
        col_scale = 1.0 / lax.psum(col_part, "batch")
        row_part = jnp.sum(base * col_scale[:, None, :], axis=2)
        row_scale = 1.0 / lax.psum(row_part, "proto")
    codes = base * row_scale[:, :, None] * col_scale[:, None, :]
    probs = expo / totals[:, :, None]
    grad_scores = ((probs - codes[::-1]) * (0.5 / soft_temp)).astype(jnp.bfloat16)
    flat_grad = grad_scores.reshape(2 * rows_here, protos_here)
    flat_unit = unit_feat.reshape(2 * rows_here, width)
    flat_inv = inv_feat.reshape(2 * rows_here, 1)
    grad_embed = lax.psum(jnp.dot(flat_grad, centers, preferred_element_type=jnp.float32), "proto")
    grad_features = norm_back(grad_embed, flat_unit, flat_inv)
    grad_features = grad_features.reshape(2, rows_here, width)
    grad_centers = lax.psum(
        lax.dot_general(
            flat_grad, flat_embed, (((0,), (0,)), ((), ())), preferred_element_type=jnp.float32
        ),
        "batch",
    )
    grad_prototypes = norm_back(grad_centers, unit_proto, inv_proto)
    return (grad_features, grad_prototypes)


def solution(mesh):
    return jax.shard_map(
        per_device,
        mesh=mesh,
        in_specs=(P(None, "batch", None), P("proto", None)),
        out_specs=(P(None, "batch", None), P("proto", None)),
        check_vma=False,
    )
```

profile of v0, /device:TPU:0, one launch (start us, length us, event | category | flops | bytes accessed | tf_op | source)
XLA Modules:
  0.0 699.3 jit_solution(4186930797797017289)
XLA Ops:
  7.2 0.0 all-reduce.7.cloned.1.call-start
  7.2 3.3 fusion.8
  10.6 0.0 copy-start.1
  10.6 1.6 fusion.11
  12.2 0.6 fusion.20
  12.8 27.7 %fusion.1 = (f32[2,8192]{1,0:T(2,128)}, f32[2,1024,8192]{2,1,0:T(8,128)}) fusion(f32[8192]{0:T(1024)S(1)} %add_rsqrt_fusion, bf16[8192,256]{1,0:T(8,128)(2,1)} %param.3, f32[2,1024]{1,0:T(2,128)S(1)} %get-tuple-element.7, bf16[2,1024,256]{2,1,0:T(8,128)(2,1)} %param.2), kind=kOutput, calls=%fused_computation.10 | convolution fusion | flops 8631336960 | bytes 72458240 | tf_op jit(solution)/shard_map/dot_general | solution.py:30
  40.4 0.0 copy-done.1
  40.4 0.0 copy-done.3
  40.4 0.0 all-reduce.7.cloned.1.call-update
  40.5 0.0 all-reduce.9.cloned.1.call-start
  40.5 55.3 %all-reduce.7.cloned.1.call-done = f32[2,8192]{1,0:T(2,128)} async-done(((f32[2,8192]{1,0:T(2,128)}), f32[2,8192]{1,0:T(2,128)}) %all-reduce.7.cloned.1.call-update) | async-done | bytes 65552 | tf_op jit(solution)/shard_map/psum | solution.py:40
  95.8 0.9 broadcast_divide_fusion.2
  96.7 25.8 %fusion = (f32[2,1024]{1,0:T(2,128)S(1)}, f32[2,1024]{1,0:T(2,128)S(1)}) fusion(f32[2,1024,8192]{2,1,0:T(8,128)} %get-tuple-element.9, f32[2,8192]{1,0:T(2,128)S(1)} %broadcast_divide_fusion.2), kind=kLoop, calls=%fused_computation.9 | loop fusion | flops 83881984 | bytes 67190784 | tf_op jit(solution)/shard_map/reduce_sum | solution.py:35
  122.5 11.8 %psum.65 = f32[2,1024]{1,0:T(2,128)S(1)} all-reduce(f32[2,1024]{1,0:T(2,128)S(1)} %get-tuple-element.3), channel_id=1, replica_groups=mesh['batch'=8,'proto'=4] {'proto'}, use_global_device_ids=true, to_apply=%region_7.0 | all-reduce | flops 2048 | bytes 16384 | tf_op jit(solution)/shard_map/psum | solution.py:42
  134.4 21.8 %multiply_reduce_fusion.3 = f32[2,8192]{1,0:T(2,128)} fusion(f32[2,1024]{1,0:T(2,128)S(1)} %broadcast_divide_fusion.5, f32[2,1024,8192]{2,1,0:T(8,128)} %get-tuple-element.9), kind=kLoop, calls=%fused_computation.5 | loop fusion | flops 50315264 | bytes 67182592 | tf_op jit(solution)/shard_map/reduce_sum | solution.py:39
  156.2 0.0 all-reduce.9.cloned.1.call-update
  156.2 0.0 all-reduce.11.cloned.1.call-start
  156.3 49.2 %all-reduce.9.cloned.1.call-done = f32[2,8192]{1,0:T(2,128)} async-done(((f32[2,8192]{1,0:T(2,128)}), f32[2,8192]{1,0:T(2,128)}) %all-reduce.9.cloned.1.call-update) | async-done | bytes 65552 | tf_op jit(solution)/shard_map/psum | solution.py:40
  205.5 0.9 broadcast_divide_fusion.1
  206.4 21.3 %multiply_reduce_fusion.2 = f32[2,1024]{1,0:T(2,128)S(1)} fusion(f32[2,8192]{1,0:T(2,128)S(1)} %broadcast_divide_fusion.1, f32[2,1024,8192]{2,1,0:T(8,128)} %get-tuple-element.9), kind=kLoop, calls=%fused_computation.4 | loop fusion | flops 50329600 | bytes 67182592 | tf_op jit(solution)/shard_map/reduce_sum | solution.py:41
  227.7 11.8 %psum.67 = f32[2,1024]{1,0:T(2,128)S(1)} all-reduce(f32[2,1024]{1,0:T(2,128)S(1)} %multiply_reduce_fusion.2), channel_id=1, replica_groups=mesh['batch'=8,'proto'=4] {'proto'}, use_global_device_ids=true, to_apply=%region_11.0 | all-reduce | flops 2048 | bytes 16384 | tf_op jit(solution)/shard_map/psum | solution.py:42
  239.6 21.8 %multiply_reduce_fusion.1 = f32[2,8192]{1,0:T(2,128)} fusion(f32[2,1024]{1,0:T(2,128)S(1)} %broadcast_divide_fusion.4, f32[2,1024,8192]{2,1,0:T(8,128)} %get-tuple-element.9), kind=kLoop, calls=%fused_computation.3 | loop fusion | flops 50315264 | bytes 67182592 | tf_op jit(solution)/shard_map/reduce_sum | solution.py:39
  261.4 0.0 all-reduce.11.cloned.1.call-update
  261.4 0.0 all-reduce.13.cloned.1.call-start
  261.5 49.2 %all-reduce.11.cloned.1.call-done = f32[2,8192]{1,0:T(2,128)} async-done(((f32[2,8192]{1,0:T(2,128)}), f32[2,8192]{1,0:T(2,128)}) %all-reduce.11.cloned.1.call-update) | async-done | bytes 65552 | tf_op jit(solution)/shard_map/psum | solution.py:40
  310.6 0.9 broadcast_divide_fusion
  311.5 21.3 %multiply_reduce_fusion = f32[2,1024]{1,0:T(2,128)S(1)} fusion(f32[2,8192]{1,0:T(2,128)S(1)} %broadcast_divide_fusion, f32[2,1024,8192]{2,1,0:T(8,128)} %get-tuple-element.9), kind=kLoop, calls=%fused_computation.2 | loop fusion | flops 50329600 | bytes 67182592 | tf_op jit(solution)/shard_map/reduce_sum | solution.py:41
  332.8 18.8 %all-reduce = (f32[2,1024]{1,0:T(2,128)S(1)}, f32[2,1024]{1,0:T(2,128)S(1)}) all-reduce(f32[2,1024]{1,0:T(2,128)S(1)} %multiply_reduce_fusion, f32[2,1024]{1,0:T(2,128)S(1)} %get-tuple-element.2), channel_id=1, replica_groups=mesh['batch'=8,'proto'=4] {'proto'}, use_global_device_ids=true, to_apply=%region_15.0 | all-reduce | flops 4096 | bytes 32768 | tf_op jit(solution)/shard_map/psum | solution.py:42
  351.6 43.4 %multiply_multiply_fusion = f32[2,1024,8192]{2,1,0:T(8,128)} fusion(f32[2,1024]{1,0:T(2,128)S(1)} %broadcast_divide_fusion.3, f32[2,8192]{1,0:T(2,128)S(1)} %broadcast_divide_fusion, f32[2,1024,8192]{2,1,0:T(8,128)} %get-tuple-element.9), kind=kLoop, calls=%fused_computation.1 | loop fusion | flops 50331648 | bytes 134291456 | tf_op jit(solution)/shard_map/mul | solution.py:43
  395.0 52.9 %multiply_convert_fusion = bf16[2,1024,8192]{2,1,0:T(8,128)(2,1)} fusion(f32[2,1024,8192]{2,1,0:T(8,128)} %multiply_multiply_fusion, f32[2,1024,8192]{2,1,0:T(8,128)} %get-tuple-element.9, f32[2,1024]{1,0:T(2,128)S(1)} %get-tuple-element.5), kind=kLoop, calls=%fused_computation | loop fusion | flops 83886080 | bytes 167780352 | tf_op jit(solution)/shard_map/convert_element_type | solution.py:45
  447.9 0.0 copy-done.2
  447.9 0.0 copy-start
  447.9 0.0 copy-start.4
  448.0 17.4 %fusion.15 = f32[2048,256]{1,0:T(8,128)} fusion(bf16[2048,8192]{1,0:T(8,128)(2,1)} %bitcast.25, bf16[8192,256]{1,0:T(8,128)(2,1)} %param.3, f32[8192]{0:T(1024)S(1)} %copy-done.2), kind=kOutput, calls=%fused_computation.31 | convolution fusion | flops 8596226048 | bytes 39878656 | tf_op jit(solution)/shard_map/dot_general | solution.py:49
  465.3 0.0 all-reduce.13.cloned.1.call-update
  465.4 0.0 copy-start.5
  465.4 0.3 all-reduce.15.cloned.1.call-start
  465.6 0.0 copy-done
  465.7 0.0 copy-done.4
  465.7 18.4 %convolution_bitcast_fusion = f32[8192,256]{1,0:T(8,128)} fusion(bf16[2,1024,8192]{2,1,0:T(8,128)(2,1)} %multiply_convert_fusion, bf16[2,1024,256]{2,1,0:T(8,128)(2,1)S(1)} %copy-done, f32[2,1024]{1,0:T(2,128)S(1)} %copy-done.4), kind=kOutput, calls=%fused_computation.11 | convolution fusion | flops 8591507456 | bytes 42999808 | tf_op jit(solution)/shard_map/dot_general | solution.py:53
  484.1 0.0 all-reduce.15.cloned.1.call-update
  484.1 0.3 convert_multiply_fusion.2
  484.5 64.2 %all-reduce.13.cloned.1.call-done = f32[2048,256]{1,0:T(8,128)} async-done(((f32[2048,256]{1,0:T(8,128)}), f32[2048,256]{1,0:T(8,128)}) %all-reduce.13.cloned.1.call-update) | async-done | bytes 2097168 | tf_op jit(solution)/shard_map/psum | solution.py:49
  548.7 1.9 fusion.12
  550.6 2.9 fusion.14
  553.5 124.6 %all-reduce.15.cloned.1.call-done = f32[8192,256]{1,0:T(8,128)} async-done(((f32[8192,256]{1,0:T(8,128)}), f32[8192,256]{1,0:T(8,128)}) %all-reduce.15.cloned.1.call-update) | async-done | bytes 8388624 | tf_op jit(solution)/shard_map/psum | solution.py:52
  678.1 5.9 fusion.5
  684.0 8.7 %fusion.7 = f32[8192,256]{1,0:T(8,128)} fusion(f32[8192,256]{1,0:T(8,128)} %all-reduce.15.cloned.1.call-done, bf16[8192,256]{1,0:T(8,128)(2,1)} %param.3, f32[8192]{0:T(1024)S(1)} %fusion.5, f32[8192]{0:T(1024)S(1)} %copy-done.2), kind=kLoop, calls=%fused_computation.19 | loop fusion | flops 10485760 | bytes 21037056 | tf_op jit(solution)/shard_map/mul | solution.py:14
  (8 shorter events, 0.1 us)
Async XLA Ops:
  7.2 88.6 %all-reduce.7.cloned.1.call-start = ((), (), s32[]{:S(2)}) async-start(), calls=%async_computation | async-start | bytes 131072 | tf_op jit(solution)/shard_map/psum | solution.py:40
  10.6 29.9 %copy-start.1 = (f32[8192]{0:T(1024)}, f32[8192]{0:T(1024)S(1)}, u32[]{:S(2)}) copy-start(f32[8192]{0:T(1024)S(1)} %add_rsqrt_fusion) | copy-start | bytes 98308
  12.8 27.7 %copy-start.3 = (f32[2,1024]{1,0:T(2,128)}, f32[2,1024]{1,0:T(2,128)S(1)}, u32[]{:S(2)}) copy-start(f32[2,1024]{1,0:T(2,128)S(1)} %get-tuple-element.7) | copy-start | bytes 24580
  40.5 165.0 %all-reduce.9.cloned.1.call-start = ((), (), s32[]{:S(2)}) async-start(), calls=%async_computation.1 | async-start | bytes 131072 | tf_op jit(solution)/shard_map/psum | solution.py:40
  156.2 154.4 %all-reduce.11.cloned.1.call-start = ((), (), s32[]{:S(2)}) async-start(), calls=%async_computation.2 | async-start | bytes 131072 | tf_op jit(solution)/shard_map/psum | solution.py:40
  261.4 287.3 %all-reduce.13.cloned.1.call-start = ((), (), s32[]{:S(2)}) async-start(), calls=%async_computation.3 | async-start | bytes 4194304 | tf_op jit(solution)/shard_map/psum | solution.py:49
  395.0 52.9 %copy-start.2 = (f32[8192]{0:T(1024)S(1)}, f32[8192]{0:T(1024)}, u32[]{:S(2)}) copy-start(f32[8192]{0:T(1024)} %copy-done.1) | copy-start | bytes 98308
  447.9 17.7 %copy-start = (bf16[2,1024,256]{2,1,0:T(8,128)(2,1)S(1)}, bf16[2,1024,256]{2,1,0:T(8,128)(2,1)}, u32[]{:S(2)}) copy-start(bf16[2,1024,256]{2,1,0:T(8,128)(2,1)} %param.2) | copy-start | bytes 3145732
  447.9 17.7 %copy-start.4 = (f32[2,1024]{1,0:T(2,128)S(1)}, f32[2,1024]{1,0:T(2,128)}, u32[]{:S(2)}) copy-start(f32[2,1024]{1,0:T(2,128)} %copy-done.3) | copy-start | bytes 24580
  465.4 18.8 %copy-start.5 = (f32[1,8,2,128]{3,2,1,0:T(2,128)S(1)}, f32[1,8,2,128]{3,2,1,0:T(2,128)}, u32[]{:S(2)}) copy-start(f32[1,8,2,128]{3,2,1,0:T(2,128)} %get-tuple-element.6) | copy-start | bytes 24580
  465.4 212.8 %all-reduce.15.cloned.1.call-start = ((), (), s32[]{:S(2)}) async-start(), calls=%async_computation.4 | async-start | bytes 16777216 | tf_op jit(solution)/shard_map/psum | solution.py:52
Sparse Core Ops, SparseCore 0:
  40.6 55.1 all-reduce.6
  156.4 49.0 all-reduce.8
  261.5 49.0 all-reduce.10
  465.5 83.1 all-reduce.12
  552.6 125.5 all-reduce.14
where the time goes:
time: 700 us; the launch traced here: 699 us
  waiting for transfers between devices  343 us (49%)
  other arithmetic  236 us (34%)
  matrix products  63.5 us (9%)
  blocking collectives  42.5 us (6%)
  between operations  13.9 us (2%)
    psum x3, waiting for transfers between devices, per_device(): col_scale = 1.0 / lax.psum(col_part, 'batch')  154 us
    psum x1, waiting for transfers between devices, per_device(): lax.psum(lax.dot_general(flat_grad, flat_embed, (((0,), (0,)), ((), ())),...  125 us
    psum x1, waiting for transfers between devices, per_device(): lax.psum(jnp.dot(flat_grad, centers, preferred_element_type=jnp.float32),...  64.2 us
    convert_element_type x1, other arithmetic, per_device(): ((probs - codes[::-1]) * (0.5 / soft_temp)).astype(jnp.bfloat16)  52.9 us
    reduce_sum x2, other arithmetic, per_device(): col_part = jnp.sum(base * row_scale[:, :, None], axis=1)  43.7 us
    mul x1, other arithmetic, per_device(): codes = base * row_scale[:, :, None] * col_scale[:, None, :]  43.4 us
    reduce_sum x2, other arithmetic, per_device(): row_part = jnp.sum(base * col_scale[:, None, :], axis=2)  42.6 us
    psum x3, blocking collectives, per_device(): row_scale = 1.0 / lax.psum(row_part, 'proto')  42.5 us
  transfers between devices with their start and end apart: 5, of which 5 were waited for; matrix products, arithmetic and copies ran while one was open for 3% of the time, Pallas kernels for 0%

commit v1 on v0

v1 whole, which is shorter than its diff:
```python
import jax
import jax.numpy as jnp
from jax import lax
from jax.experimental import pallas as pl
from jax.experimental.pallas import tpu as pltpu
from jax.sharding import PartitionSpec as P

ITERS = 3
LOG2E = 1.4426950408889634
SOFT = 10.0 * LOG2E
GRAD = 5.0
F32 = jnp.float32
BF16 = jnp.bfloat16
NT = (((1,), (1,)), ((), ()))


def tile_of(n, most):
    t = most
    while n % t:
        t //= 2
    return t


def params(mib):
    return pltpu.CompilerParams(vmem_limit_bytes=mib * 2**20)


def lane_fold(x):
    total = x[:, :128]
    for j in range(1, x.shape[1] // 128):
        total = total + x[:, 128 * j : 128 * (j + 1)]
    return total


def sub_fold(x):
    total = x[:8]
    for j in range(1, x.shape[0] // 8):
        total = total + x[8 * j : 8 * (j + 1)]
    return total


def spread(row):
    return jnp.broadcast_to(row, (128, row.shape[1])).T


def unit_of(x):
    inv = lax.rsqrt(jnp.sum(x * x, axis=-1, keepdims=True) + 1e-06)
    return x * inv, inv


def first_kernel(feat_ref, proto_ref, embed_ref, cent_ref, base_ref, col_ref, tot_ref, soft_ref, acc):
    i = pl.program_id(0)
    rows = feat_ref.shape[1]
    kt = proto_ref.shape[0]
    rc = tile_of(rows, 256)

    @pl.when(i == 0)
    def _():
        acc[...] = jnp.zeros_like(acc)
        soft_ref[...] = jnp.zeros_like(soft_ref)
        for v in range(2):
            embed_ref[v] = unit_of(feat_ref[v].astype(F32))[0].astype(BF16)

    cent_ref[...] = unit_of(proto_ref[...].astype(F32))[0].astype(BF16)
    for v in range(2):

        def step(j, col):
            r = pl.ds(pl.multiple_of(j * rc, rc), rc)
            s = lax.dot_general(embed_ref[v, r, :], cent_ref[...], NT, preferred_element_type=F32)
            e = jnp.exp2(s * SOFT)
            acc[v, r, :] += lane_fold(e)
            soft_ref[v, r, :] += jnp.dot(e.astype(BF16), cent_ref[...], preferred_element_type=F32)
            b = e * e
            base_ref[v, r, :] = b.astype(BF16)
            return col + sub_fold(b)

        col = lax.fori_loop(0, rows // rc, step, jnp.zeros((8, kt), F32), unroll=True)
        col_ref[v, pl.ds(i, 1), :] = jnp.sum(col, axis=0, keepdims=True)

    @pl.when(i == pl.num_programs(0) - 1)
    def _():
        for v in range(2):
            tot_ref[v : v + 1, :] = jnp.sum(acc[v].T, axis=0, keepdims=True)


def first(features, prototypes):
    _, rows, width = features.shape
    protos = prototypes.shape[0]
    kt = tile_of(protos, 1024)
    n = protos // kt
    whole = lambda *s: pl.BlockSpec(s, lambda i: (0,) * len(s))
    return pl.pallas_call(
        first_kernel,
        grid=(n,),
        in_specs=[whole(2, rows, width), pl.BlockSpec((kt, width), lambda i: (i, 0))],
        out_specs=[
            whole(2, rows, width),
            pl.BlockSpec((kt, width), lambda i: (i, 0)),
            pl.BlockSpec((2, rows, kt), lambda i: (0, 0, i)),
            whole(2, n, kt),
            whole(2, rows),
            whole(2, rows, width),
        ],
        out_shape=[
            jax.ShapeDtypeStruct((2, rows, width), BF16),
            jax.ShapeDtypeStruct((protos, width), BF16),
            jax.ShapeDtypeStruct((2, rows, protos), BF16),
            jax.ShapeDtypeStruct((2, n, kt), F32),
            jax.ShapeDtypeStruct((2, rows), F32),
            jax.ShapeDtypeStruct((2, rows, width), F32),
        ],
        scratch_shapes=[pltpu.VMEM((2, rows, 128), F32)],
        compiler_params=params(48),
        name="first",
    )(features, prototypes)


def row_kernel(base_ref, *refs):
    *part_refs, out_ref, acc = refs
    i = pl.program_id(0)
    rows = base_ref.shape[1]
    rc = 16

    @pl.when(i == 0)
    def _():
        acc[...] = jnp.zeros_like(acc)

    for v in range(2):
        c = 1.0 / sum(p[v, pl.ds(i, 1), :] for p in part_refs)

        def step(j, carry):
            r = pl.ds(pl.multiple_of(j * rc, rc), rc)
            acc[v, r, :] += lane_fold(base_ref[v, r, :].astype(F32) * c)
            return carry

        lax.fori_loop(0, rows // rc, step, 0, unroll=4)

    @pl.when(i == pl.num_programs(0) - 1)
    def _():
        for v in range(2):
            out_ref[v : v + 1, :] = jnp.sum(acc[v].T, axis=0, keepdims=True)


def row_last_kernel(base_ref, cent_ref, *refs):
    *part_refs, out_ref, code_ref, acc = refs
    i = pl.program_id(0)
    rows = base_ref.shape[1]
    rc = tile_of(rows, 256)

    @pl.when(i == 0)
    def _():
        acc[...] = jnp.zeros_like(acc)
        code_ref[...] = jnp.zeros_like(code_ref)

    for v in range(2):
        c = 1.0 / sum(p[v, pl.ds(i, 1), :] for p in part_refs)

        def step(j, carry):
            r = pl.ds(pl.multiple_of(j * rc, rc), rc)
            w = base_ref[v, r, :].astype(F32) * c
            acc[v, r, :] += lane_fold(w)
            code_ref[v, r, :] += jnp.dot(w.astype(BF16), cent_ref[...], preferred_element_type=F32)
            return carry

        lax.fori_loop(0, rows // rc, step, 0, unroll=True)

    @pl.when(i == pl.num_programs(0) - 1)
    def _():
        for v in range(2):
            out_ref[v : v + 1, :] = jnp.sum(acc[v].T, axis=0, keepdims=True)


def row_pass(base, parts, centers=None):
    _, rows, protos = base.shape
    _, n, kt = parts[0].shape
    whole = lambda *s: pl.BlockSpec(s, lambda i: (0,) * len(s))
    in_specs = [pl.BlockSpec((2, rows, kt), lambda i: (0, 0, i))]
    out_specs = [whole(2, rows)]
    out_shape = [jax.ShapeDtypeStruct((2, rows), F32)]
    args = [base]
    if centers is not None:
        width = centers.shape[1]
        in_specs.append(pl.BlockSpec((kt, width), lambda i: (i, 0)))
        out_specs.append(whole(2, rows, width))
        out_shape.append(jax.ShapeDtypeStruct((2, rows, width), F32))
        args.append(centers)
    return pl.pallas_call(
        row_kernel if centers is None else row_last_kernel,
        grid=(n,),
        in_specs=in_specs + [whole(2, n, kt)] * len(parts),
        out_specs=out_specs,
        out_shape=out_shape,
        scratch_shapes=[pltpu.VMEM((2, rows, 128), F32)],
        compiler_params=params(48),
        name="row_pass" if centers is None else "row_last",
    )(*args, *parts)


def col_kernel(base_ref, total_ref, out_ref, scale):
    i = pl.program_id(0)
    rows, kt = base_ref.shape[1:]
    rc = 16

    @pl.when(i == 0)
    def _():
        for v in range(2):
            scale[v] = spread(1.0 / total_ref[v : v + 1, :])

    for v in range(2):

        def step(j, col):
            r = pl.ds(pl.multiple_of(j * rc, rc), rc)
            w = jnp.concatenate([scale[v, r, :]] * (kt // 128), axis=1)
            return col + sub_fold(base_ref[v, r, :].astype(F32) * w)

        col = lax.fori_loop(0, rows // rc, step, jnp.zeros((8, kt), F32), unroll=4)
        out_ref[v, pl.ds(i, 1), :] = jnp.sum(col, axis=0, keepdims=True)


def col_pass(base, total, n):
    _, rows, protos = base.shape
    kt = protos // n
    whole = lambda *s: pl.BlockSpec(s, lambda i: (0,) * len(s))
    return pl.pallas_call(
        col_kernel,
        grid=(n,),
        in_specs=[pl.BlockSpec((2, rows, kt), lambda i: (0, 0, i)), whole(2, rows)],
        out_specs=whole(2, n, kt),
        out_shape=jax.ShapeDtypeStruct((2, n, kt), F32),
        scratch_shapes=[pltpu.VMEM((2, rows, 128), F32)],
        compiler_params=params(48),
        name="col_pass",
    )(base, total)


def grad_kernel(cent_ref, embed_ref, tot_ref, row_ref, col_ref, out_ref, scale):
    rows = embed_ref.shape[1]
    kt = cent_ref.shape[0]
    rc = tile_of(rows, 512)
    for v in range(2):
        scale[v] = spread(col_ref[v, pl.ds(pl.program_id(0), 1), :])
    cs = [jnp.concatenate([scale[v]] * (rc // 128), axis=1) for v in range(2)]
    total = jnp.zeros(out_ref.shape, F32)
    for j in range(rows // rc):
        r = slice(j * rc, (j + 1) * rc)
        es = []
        for v in range(2):
            s = lax.dot_general(cent_ref[...], embed_ref[v, r, :], NT, preferred_element_type=F32)
            es.append(jnp.exp2(s * SOFT))
        for v in range(2):
            o = 1 - v
            codes = es[o] * es[o] * (GRAD / row_ref[o : o + 1, r]) * cs[o]
            g = (es[v] * (GRAD / tot_ref[v : v + 1, r]) - codes).astype(BF16)
            total = total + jnp.dot(g, embed_ref[v, r, :], preferred_element_type=F32)
    out_ref[...] = total


def grad_pass(centers, embed, tot, row, col):
    protos, width = centers.shape
    rows = embed.shape[1]
    kt = tile_of(protos, 512)
    n = protos // kt
    whole = lambda *s: pl.BlockSpec(s, lambda i: (0,) * len(s))
    return pl.pallas_call(
        grad_kernel,
        grid=(n,),
        in_specs=[
            pl.BlockSpec((kt, width), lambda i: (i, 0)),
            whole(2, rows, width),
            whole(2, rows),
            whole(2, rows),
            whole(2, n, kt),
        ],
        out_specs=pl.BlockSpec((kt, width), lambda i: (i, 0)),
        out_shape=jax.ShapeDtypeStruct((protos, width), F32),
        scratch_shapes=[pltpu.VMEM((2, kt, 128), F32)],
        compiler_params=params(48),
        name="grad_pass",
    )(centers, embed, tot, row, col.reshape(2, n, kt))


def swap(x, axis, n, m):
    return lax.ppermute(x, axis, [(i, i ^ m) for i in range(n)])


def col_exchange(x, n):
    if n > 1:
        x = x + swap(x, "batch", n, 1)
    m = 2
    while n // m > 4:
        x = x + swap(x, "batch", n, m)
        m *= 2
    return [x] + [swap(x, "batch", n, k * m) for k in range(1, n // m)]


def row_exchange(x, n):
    m = 1
    while m < n:
        x = x + swap(x, "proto", n, m)
        m *= 2
    return x


def norm_back(grad, unit, inverse):
    return inverse * (grad - unit * jnp.sum(unit * grad, axis=-1, keepdims=True))


def per_device(nb, npr, features, prototypes):
    embed, centers, base, col, tot, soft = first(features, prototypes)
    n = col.shape[1]
    parts = col_exchange(col, nb)
    tot = row_exchange(tot, npr)
    for step in range(ITERS - 1):
        (row,) = row_pass(base, parts)
        row = row_exchange(row, npr)
        parts = col_exchange(col_pass(base, row, n), nb)
    row, code = row_pass(base, parts, centers)
    row = row_exchange(row, npr)
    col = 1.0 / sum(parts)
    grad_embed = soft * (GRAD / tot)[:, :, None] - (code * (GRAD / row)[:, :, None])[::-1]
    grad_embed = lax.psum(grad_embed, "proto")
    grad_centers = lax.psum(grad_pass(centers, embed, tot, row, col), "batch")
    unit_feat, inv_feat = unit_of(features.astype(F32))
    unit_proto, inv_proto = unit_of(prototypes.astype(F32))
    return (
        norm_back(grad_embed, unit_feat, inv_feat),
        norm_back(grad_centers, unit_proto, inv_proto),
    )


def solution(mesh):
    nb, npr = mesh.shape["batch"], mesh.shape["proto"]
    return jax.shard_map(
        lambda f, p: per_device(nb, npr, f, p),
        mesh=mesh,
        in_specs=(P(None, "batch", None), P("proto", None)),
        out_specs=(P(None, "batch", None), P("proto", None)),
        check_vma=False,
    )
```

time: 700 us -> 406 us (0.58)
  other arithmetic: 236 us -> 33 us
  waiting for transfers between devices: 343 us -> 191 us
  Pallas kernels: 0 us -> 132 us
  matrix products: 63.5 us -> 0 us
  blocking collectives: 42.5 us -> 0 us
  starting transfers between devices: 0.43 us -> 29.1 us
    psum x5 -> x2, waiting for transfers between devices: 342 us -> 166 us  [the longest x1 116 us: per_device(): grad_centers = lax.psum(grad_pass(centers, embed, tot, row, col), 'batch')]
    pallas_call x0 -> x7, Pallas kernels: none -> 132 us  [the longest x3 48.7 us: row_pass(): pl.pallas_call(row_kernel if centers is None else row_last_kernel, grid=(...]
    reduce_sum x7 -> x2, other arithmetic: 117 us -> 3.7 us  [unit_of(): inv = lax.rsqrt(jnp.sum(x * x, axis=-1, keepdims=True) + 1e-06)]
    dot_general x3 -> x0, matrix products: 63.5 us -> none  [the longest x1 27.7 us: per_device(): jnp.dot(flat_embed, centers.T, preferred_element_type=jnp.float32)]
    convert_element_type x1 -> x0, other arithmetic: 52.9 us -> none  [per_device(): ((probs - codes[::-1]) * (0.5 / soft_temp)).astype(jnp.bfloat16)]
    psum x3 -> x0, blocking collectives: 42.5 us -> none  [per_device(): row_scale = 1.0 / lax.psum(row_part, 'proto')]
    mul x2, other arithmetic: 43.7 us -> 14.5 us  [the longest x1 14.2 us: norm_back(): unit * jnp.sum(unit * grad, axis=-1, keepdims=True)]
    ppermute x0 -> x20, starting transfers between devices: none -> 28.9 us  [swap(): return lax.ppermute(x, axis, [(i, i ^ m) for i in range(n)])]
  transfers between devices with their start and end apart: 5 -> 22, of which waited for: 5 -> 18; matrix products, arithmetic and copies ran while one was open for 3% -> 4% of each run, Pallas kernels for 0% -> 11%
where the time goes in v1:
time: 406 us; the launch traced here: 405 us
  waiting for transfers between devices  191 us (47%)
  Pallas kernels  132 us (33%)
  other arithmetic  33 us (8%)
  starting transfers between devices  29.1 us (7%)
  between operations  14.2 us (3%)
  local copies, waits for them, and re-layouts  6.22 us (2%)
    psum x1, waiting for transfers between devices, per_device(): grad_centers = lax.psum(grad_pass(centers, embed, tot, row, col), 'batch')  116 us
    psum x1, waiting for transfers between devices, per_device(): grad_embed = lax.psum(grad_embed, 'proto')  50.1 us
    pallas_call x3, Pallas kernels, row_pass(): pl.pallas_call(row_kernel if centers is None else row_last_kernel, grid=(...  48.7 us
    pallas_call x2, Pallas kernels, col_pass(): pl.pallas_call(col_kernel, grid=(n,), in_specs=[pl.BlockSpec((2, rows, kt...  29.7 us
    ppermute x20, starting transfers between devices, swap(): return lax.ppermute(x, axis, [(i, i ^ m) for i in range(n)])  28.9 us
    pallas_call x1, Pallas kernels, grad_pass(): pl.pallas_call(grad_kernel, grid=(n,), in_specs=[pl.BlockSpec((kt, width)...  27.9 us
    pallas_call x1, Pallas kernels, first(): pl.pallas_call(first_kernel, grid=(n,), in_specs=[whole(2, rows, width),...  25.2 us
    ppermute x20, waiting for transfers between devices, swap(): return lax.ppermute(x, axis, [(i, i ^ m) for i in range(n)])  24.7 us
  transfers between devices with their start and end apart: 22, of which 18 were waited for; matrix products, arithmetic and copies ran while one was open for 4% of the time, Pallas kernels for 11%

profile of v1, /device:TPU:0, one launch (start us, length us, event | category | flops | bytes accessed | tf_op | source)
XLA Modules:
  0.0 404.9 jit_solution(15986330550907707628)
XLA Ops:
  7.2 1.2 copy-done.1
  8.4 25.2 %first.1 = (bf16[2,1024,256]{2,1,0:T(8,128)(2,1)S(1)}, bf16[8192,256]{1,0:T(8,128)(2,1)}, bf16[2,1024,8192]{2,1,0:T(8,128)(2,1)}, f32[2,8,1024]{2,1,0:T(8,128)S(...) custom-call(bf16[2,1024,256]{2,1,0:T(8,128)(2,1)S(1)} %copy-done.1, bf16[8192,256]{1,0:T(8,128)(2,1)} %proto_ref.1), custom_call_target="tpu_custom_call" | custom-call | tf_op jit(solution)/shard_map/first/pallas_call | solution.py:92
  33.7 0.5 collective-permute-start.2
  34.1 0.9 collective-permute-done.2
  35.0 2.9 collective-permute-start.3
  37.9 1.5 collective-permute-start.4
  39.5 0.9 collective-permute-done.3.refs_1_
  40.3 1.9 collective-permute-done.4.refs_2_
  42.2 2.4 collective-permute-done.5.refs_3_
  44.6 15.5 %row_pass.2 = f32[2,1024]{1,0:T(2,128)S(1)} custom-call(bf16[2,1024,8192]{2,1,0:T(8,128)(2,1)} %get-tuple-element.12.base_ref, f32[2,8,1024]{2,1,0:T(8,128)S(1)} %add.72.refs_0_, f32[2,8,1024]{2,1,0:T(8,128)S(1)} %collective-permute-done.3.refs_1_, f32[2,8,1024]{2,1,0:T(8,128)S(1)} %collective-permute-done.4.refs_2_, ...), custom_call_target="tpu_custom_call" | custom-call | tf_op jit(solution)/shard_map/row_pass/pallas_call | solution.py:187
  60.1 1.6 collective-permute-start.6
  61.8 2.1 collective-permute-done.6
  63.8 2.6 collective-permute-start.7
  66.4 2.0 collective-permute-done.7
  68.4 14.9 %col_pass.2 = f32[2,8,1024]{2,1,0:T(8,128)S(1)} custom-call(bf16[2,1024,8192]{2,1,0:T(8,128)(2,1)} %get-tuple-element.12.base_ref, f32[2,1024]{1,0:T(2,128)S(1)} %add.74.total_ref), custom_call_target="tpu_custom_call" | custom-call | tf_op jit(solution)/shard_map/col_pass/pallas_call | solution.py:224
  83.4 1.2 collective-permute-done.8
  84.6 0.6 collective-permute-start.9
  85.6 2.6 collective-permute-start.11
  88.2 0.9 collective-permute-done.9.refs_1_
  89.1 1.3 collective-permute-done.10.refs_2_
  90.8 15.5 %row_pass.3 = f32[2,1024]{1,0:T(2,128)S(1)} custom-call(bf16[2,1024,8192]{2,1,0:T(8,128)(2,1)} %get-tuple-element.12.base_ref, f32[2,8,1024]{2,1,0:T(8,128)S(1)} %add.75.refs_0_, f32[2,8,1024]{2,1,0:T(8,128)S(1)} %collective-permute-done.9.refs_1_, f32[2,8,1024]{2,1,0:T(8,128)S(1)} %collective-permute-done.10.refs_2_, ...), custom_call_target="tpu_custom_call" | custom-call | tf_op jit(solution)/shard_map/row_pass/pallas_call | solution.py:187
  106.3 1.7 collective-permute-start.12
  108.0 2.0 collective-permute-done.12
  110.0 2.8 collective-permute-start.13
  112.8 1.8 collective-permute-done.13
  114.6 14.9 %col_pass.3 = f32[2,8,1024]{2,1,0:T(8,128)S(1)} custom-call(bf16[2,1024,8192]{2,1,0:T(8,128)(2,1)} %get-tuple-element.12.base_ref, f32[2,1024]{1,0:T(2,128)S(1)} %add.77.total_ref), custom_call_target="tpu_custom_call" | custom-call | tf_op jit(solution)/shard_map/col_pass/pallas_call | solution.py:224
  129.6 1.2 collective-permute-done.14
  130.8 1.6 collective-permute-start.15
  132.4 1.5 collective-permute-start.16
  134.4 1.6 collective-permute-start
  136.0 0.7 collective-permute-done.16.refs_2_
  136.7 2.4 collective-permute-done.17.refs_3_
  139.1 17.8 %row_last.1 = (f32[2,1024]{1,0:T(2,128)S(1)}, f32[2,1024,256]{2,1,0:T(8,128)S(1)}) custom-call(bf16[2,1024,8192]{2,1,0:T(8,128)(2,1)} %get-tuple-element.12.base_ref, bf16[8192,256]{1,0:T(8,128)(2,1)} %get-tuple-element.13.cent_ref, f32[2,8,1024]{2,1,0:T(8,128)S(1)} %add.78.refs_0_, f32[2,8,1024]{2,1,0:T(8,128)S(1)} %collective-permute-done.15.refs_1_, ...), custom_call_target="tpu_custom_call" | custom-call | tf_op jit(solution)/shard_map/row_last/pallas_call | solution.py:187
  156.9 1.6 collective-permute-start.18
  158.5 2.7 collective-permute-start.1
  161.2 2.1 collective-permute-start.19
  163.3 2.5 collective-permute-done.19
  166.2 1.7 reverse_subtract_fusion
  168.2 2.2 copy-done
  170.4 27.9 %grad_pass.1 = f32[8192,256]{1,0:T(8,128)} custom-call(bf16[8192,256]{1,0:T(8,128)(2,1)S(1)} %copy-done, bf16[2,1024,256]{2,1,0:T(8,128)(2,1)S(1)} %get-tuple-element.17.embed_ref, f32[2,1024]{1,0:T(2,128)S(1)} %get-tuple-element.19.tot_ref, f32[2,1024]{1,0:T(2,128)S(1)} %get-tuple-element.21.row_ref, f32[2,16,512]{2,1,0:T(8,128)S(1)} %reshape.23.col_ref), custom_call_target="tpu_custom_call" | custom-call | tf_op jit(solution)/shard_map/grad_pass/pallas_call | solution.py:264
  198.3 1.2 copy-done.2
  199.9 3.3 fusion.6
  203.3 50.1 %all-reduce.3.cloned.1.call-done = f32[2,1024,256]{2,1,0:T(8,128)} async-done(((f32[2,1024,256]{2,1,0:T(8,128)}), f32[2,1024,256]{2,1,0:T(8,128)}) %all-reduce.3.cloned.1.call-update) | async-done | bytes 2097168 | tf_op jit(solution)/shard_map/psum | solution.py:321
  253.3 14.2 %fusion.10 = f32[2,1024,256]{2,1,0:T(8,128)} fusion(f32[2,1024,256]{2,1,0:T(8,128)} %all-reduce.3.cloned.1.call-done, bf16[2,1024,256]{2,1,0:T(8,128)(2,1)S(1)} %copy-done.2, f32[2,1024]{1,0:T(2,128)S(1)} %add_rsqrt_fusion.1), kind=kOutput, calls=%fused_computation.14 | output fusion | flops 4196607 | bytes 5251072 | tf_op jit(solution)/shard_map/mul | solution.py:305
  267.5 116.0 %all-reduce.5.cloned.1.call-done = f32[8192,256]{1,0:T(8,128)} async-done(((f32[8192,256]{1,0:T(8,128)}), f32[8192,256]{1,0:T(8,128)}) %all-reduce.5.cloned.1.call-update) | async-done | bytes 8388624 | tf_op jit(solution)/shard_map/psum | solution.py:322
  383.5 6.7 %fusion.3 = f32[8192]{0:T(1024)S(1)} fusion(f32[8192,256]{1,0:T(8,128)} %all-reduce.5.cloned.1.call-done, bf16[8192,256]{1,0:T(8,128)(2,1)} %proto_ref.1, f32[8192]{0:T(1024)S(1)} %add_rsqrt_fusion), kind=kLoop, calls=%fused_computation.5 | loop fusion | flops 8380416 | bytes 12648448 | tf_op jit(solution)/shard_map/reduce_sum | solution.py:305
  390.2 1.6 copy-done.4
  391.8 6.3 %fusion.5 = f32[8192,256]{1,0:T(8,128)} fusion(f32[8192,256]{1,0:T(8,128)S(1)} %copy-done.4, bf16[8192,256]{1,0:T(8,128)(2,1)S(1)} %copy-done.3, f32[8192]{0:T(1024)S(1)} %fusion.3, f32[8192]{0:T(1024)S(1)} %add_rsqrt_fusion), kind=kLoop, calls=%fused_computation.7 | loop fusion | flops 10485760 | bytes 21037056 | tf_op jit(solution)/shard_map/mul | solution.py:305
  (37 shorter events, 2.5 us)
Async XLA Ops:
  7.2 246.2 %all-reduce.3.cloned.1.call-start = ((), (), s32[]{:S(2)}) async-start(), calls=%async_computation | async-start | bytes 4194304 | tf_op jit(solution)/shard_map/psum | solution.py:321
  7.2 1.2 copy-start.1
  33.7 1.4 collective-permute-start.2
  35.0 5.3 %collective-permute-start.3 = (f32[2,8,1024]{2,1,0:T(8,128)S(1)}, f32[2,8,1024]{2,1,0:T(8,128)S(1)}, u32[]{:S(2)}, u32[]{:S(2)}) collective-permute-start(f32[2,8,1024]{2,1,0:T(8,128)S(1)} %add.72.refs_0_), channel_id=1, source_target_pairs={{0,8},{4,12},{8,0},{12,4},{16,24},{20,28},{24,16},{28,20},{1,9},{5... | collective-permute-start | bytes 196616 | tf_op jit(solution)/shard_map/ppermute | solution.py:283
  37.9 4.3 %collective-permute-start.4 = (f32[2,8,1024]{2,1,0:T(8,128)S(1)}, f32[2,8,1024]{2,1,0:T(8,128)S(1)}, u32[]{:S(2)}, u32[]{:S(2)}) collective-permute-start(f32[2,8,1024]{2,1,0:T(8,128)S(1)} %add.72.refs_0_), channel_id=1, source_target_pairs={{0,16},{4,20},{8,24},{12,28},{16,0},{20,4},{24,8},{28,12},{1,17},{... | collective-permute-start | bytes 196616 | tf_op jit(solution)/shard_map/ppermute | solution.py:283
  39.5 5.2 %collective-permute-start.5 = (f32[2,8,1024]{2,1,0:T(8,128)S(1)}, f32[2,8,1024]{2,1,0:T(8,128)S(1)}, u32[]{:S(2)}, u32[]{:S(2)}) collective-permute-start(f32[2,8,1024]{2,1,0:T(8,128)S(1)} %add.72.refs_0_), channel_id=1, source_target_pairs={{0,24},{4,28},{8,16},{12,20},{16,8},{20,12},{24,0},{28,4},{1,25},{... | collective-permute-start | bytes 196616 | tf_op jit(solution)/shard_map/ppermute | solution.py:283
  60.1 3.7 collective-permute-start.6
  63.8 4.5 %collective-permute-start.7 = (f32[2,1024]{1,0:T(2,128)S(1)}, f32[2,1024]{1,0:T(2,128)S(1)}, u32[]{:S(2)}, u32[]{:S(2)}) collective-permute-start(f32[2,1024]{1,0:T(2,128)S(1)} %add.73), channel_id=1, source_target_pairs={{0,2},{1,3},{2,0},{3,1},{4,6},{5,7},{6,4},{7,5},{8,10},{9,11},{10,... | collective-permute-start | bytes 24584 | tf_op jit(solution)/shard_map/ppermute | solution.py:283
  83.3 1.3 collective-permute-start.8
  84.6 4.5 %collective-permute-start.9 = (f32[2,8,1024]{2,1,0:T(8,128)S(1)}, f32[2,8,1024]{2,1,0:T(8,128)S(1)}, u32[]{:S(2)}, u32[]{:S(2)}) collective-permute-start(f32[2,8,1024]{2,1,0:T(8,128)S(1)} %add.75.refs_0_), channel_id=1, source_target_pairs={{0,8},{4,12},{8,0},{12,4},{16,24},{20,28},{24,16},{28,20},{1,9},{5... | collective-permute-start | bytes 196616 | tf_op jit(solution)/shard_map/ppermute | solution.py:283
  85.2 5.2 %collective-permute-start.10 = (f32[2,8,1024]{2,1,0:T(8,128)S(1)}, f32[2,8,1024]{2,1,0:T(8,128)S(1)}, u32[]{:S(2)}, u32[]{:S(2)}) collective-permute-start(f32[2,8,1024]{2,1,0:T(8,128)S(1)} %add.75.refs_0_), channel_id=1, source_target_pairs={{0,16},{4,20},{8,24},{12,28},{16,0},{20,4},{24,8},{28,12},{1,17},{... | collective-permute-start | bytes 196616 | tf_op jit(solution)/shard_map/ppermute | solution.py:283
  85.6 5.2 %collective-permute-start.11 = (f32[2,8,1024]{2,1,0:T(8,128)S(1)}, f32[2,8,1024]{2,1,0:T(8,128)S(1)}, u32[]{:S(2)}, u32[]{:S(2)}) collective-permute-start(f32[2,8,1024]{2,1,0:T(8,128)S(1)} %add.75.refs_0_), channel_id=1, source_target_pairs={{0,24},{4,28},{8,16},{12,20},{16,8},{20,12},{24,0},{28,4},{1,25},{... | collective-permute-start | bytes 196616 | tf_op jit(solution)/shard_map/ppermute | solution.py:283
  106.3 3.7 collective-permute-start.12
  110.0 4.5 %collective-permute-start.13 = (f32[2,1024]{1,0:T(2,128)S(1)}, f32[2,1024]{1,0:T(2,128)S(1)}, u32[]{:S(2)}, u32[]{:S(2)}) collective-permute-start(f32[2,1024]{1,0:T(2,128)S(1)} %add.76), channel_id=1, source_target_pairs={{0,2},{1,3},{2,0},{3,1},{4,6},{5,7},{6,4},{7,5},{8,10},{9,11},{10,... | collective-permute-start | bytes 24584 | tf_op jit(solution)/shard_map/ppermute | solution.py:283
  129.5 1.3 collective-permute-start.14
  130.8 5.2 %collective-permute-start.15 = (f32[2,8,1024]{2,1,0:T(8,128)S(1)}, f32[2,8,1024]{2,1,0:T(8,128)S(1)}, u32[]{:S(2)}, u32[]{:S(2)}) collective-permute-start(f32[2,8,1024]{2,1,0:T(8,128)S(1)} %add.78.refs_0_), channel_id=1, source_target_pairs={{0,8},{4,12},{8,0},{12,4},{16,24},{20,28},{24,16},{28,20},{1,9},{5... | collective-permute-start | bytes 196616 | tf_op jit(solution)/shard_map/ppermute | solution.py:283
  132.4 4.3 %collective-permute-start.16 = (f32[2,8,1024]{2,1,0:T(8,128)S(1)}, f32[2,8,1024]{2,1,0:T(8,128)S(1)}, u32[]{:S(2)}, u32[]{:S(2)}) collective-permute-start(f32[2,8,1024]{2,1,0:T(8,128)S(1)} %add.78.refs_0_), channel_id=1, source_target_pairs={{0,16},{4,20},{8,24},{12,28},{16,0},{20,4},{24,8},{28,12},{1,17},{... | collective-permute-start | bytes 196616 | tf_op jit(solution)/shard_map/ppermute | solution.py:283
  134.0 5.2 %collective-permute-start.17 = (f32[2,8,1024]{2,1,0:T(8,128)S(1)}, f32[2,8,1024]{2,1,0:T(8,128)S(1)}, u32[]{:S(2)}, u32[]{:S(2)}) collective-permute-start(f32[2,8,1024]{2,1,0:T(8,128)S(1)} %add.78.refs_0_), channel_id=1, source_target_pairs={{0,24},{4,28},{8,16},{12,20},{16,8},{20,12},{24,0},{28,4},{1,25},{... | collective-permute-start | bytes 196616 | tf_op jit(solution)/shard_map/ppermute | solution.py:283
  134.4 24.2 %collective-permute-start = (f32[2,1024]{1,0:T(2,128)S(1)}, f32[2,1024]{1,0:T(2,128)S(1)}, u32[]{:S(2)}, u32[]{:S(2)}) collective-permute-start(f32[2,1024]{1,0:T(2,128)S(1)} %get-tuple-element.11), channel_id=1, source_target_pairs={{0,1},{1,0},{2,3},{3,2},{4,5},{5,4},{6,7},{7,6},{8,9},{9,8},{10,11... | collective-permute-start | bytes 24584 | tf_op jit(solution)/shard_map/ppermute | solution.py:283
  156.9 4.3 %collective-permute-start.18 = (f32[2,1024]{1,0:T(2,128)S(1)}, f32[2,1024]{1,0:T(2,128)S(1)}, u32[]{:S(2)}, u32[]{:S(2)}) collective-permute-start(f32[2,1024]{1,0:T(2,128)S(1)} %get-tuple-element.16), channel_id=1, source_target_pairs={{0,1},{1,0},{2,3},{3,2},{4,5},{5,4},{6,7},{7,6},{8,9},{9,8},{10,11... | collective-permute-start | bytes 24584 | tf_op jit(solution)/shard_map/ppermute | solution.py:283
  158.5 4.7 %collective-permute-start.1 = (f32[2,1024]{1,0:T(2,128)S(1)}, f32[2,1024]{1,0:T(2,128)S(1)}, u32[]{:S(2)}, u32[]{:S(2)}) collective-permute-start(f32[2,1024]{1,0:T(2,128)S(1)} %add.70), channel_id=1, source_target_pairs={{0,2},{1,3},{2,0},{3,1},{4,6},{5,7},{6,4},{7,5},{8,10},{9,11},{10,... | collective-permute-start | bytes 24584 | tf_op jit(solution)/shard_map/ppermute | solution.py:283
  161.2 4.6 %collective-permute-start.19 = (f32[2,1024]{1,0:T(2,128)S(1)}, f32[2,1024]{1,0:T(2,128)S(1)}, u32[]{:S(2)}, u32[]{:S(2)}) collective-permute-start(f32[2,1024]{1,0:T(2,128)S(1)} %add.79), channel_id=1, source_target_pairs={{0,2},{1,3},{2,0},{3,1},{4,6},{5,7},{6,4},{7,5},{8,10},{9,11},{10,... | collective-permute-start | bytes 24584 | tf_op jit(solution)/shard_map/ppermute | solution.py:283
  167.9 215.6 %all-reduce.5.cloned.1.call-start = ((), (), s32[]{:S(2)}) async-start(), calls=%async_computation.1 | async-start | bytes 16777216 | tf_op jit(solution)/shard_map/psum | solution.py:322
  168.2 2.2 copy-start
  198.3 1.2 copy-start.2
  383.5 6.7 %copy-start.3 = (bf16[8192,256]{1,0:T(8,128)(2,1)S(1)}, bf16[8192,256]{1,0:T(8,128)(2,1)}, u32[]{:S(2)}) copy-start(bf16[8192,256]{1,0:T(8,128)(2,1)} %proto_ref.1) | copy-start | bytes 12582916
  383.5 8.3 %copy-start.4 = (f32[8192,256]{1,0:T(8,128)S(1)}, f32[8192,256]{1,0:T(8,128)}, u32[]{:S(2)}) copy-start(f32[8192,256]{1,0:T(8,128)} %all-reduce.5.cloned.1.call-done) | copy-start | bytes 25165828
Sparse Core Ops, SparseCore 0:
  168.0 85.2 all-reduce.2
  257.8 125.6 all-reduce.4

commit v2 on v1

--- a/solution.py
+++ b/solution.py
@@ -25,6 +25,10 @@
     return pltpu.CompilerParams(vmem_limit_bytes=mib * 2**20)
 
 
+def cost(flops, nbytes):
+    return pl.CostEstimate(flops=flops, bytes_accessed=nbytes, transcendentals=0)
+
+
 def lane_fold(x):
     total = x[:, :128]
     for j in range(1, x.shape[1] // 128):
@@ -48,7 +52,9 @@
     return x * inv, inv
 
 
-def first_kernel(feat_ref, proto_ref, embed_ref, cent_ref, base_ref, col_ref, tot_ref, soft_ref, acc):
+def first_kernel(
+    feat_ref, proto_ref, lo_ref, hi_ref, cent_ref, base_ref, col_ref, tot_ref, soft_ref, acc, embed_ref
+):
     i = pl.program_id(0)
     rows = feat_ref.shape[1]
     kt = proto_ref.shape[0]
@@ -59,7 +65,10 @@
         acc[...] = jnp.zeros_like(acc)
         soft_ref[...] = jnp.zeros_like(soft_ref)
         for v in range(2):
-            embed_ref[v] = unit_of(feat_ref[v].astype(F32))[0].astype(BF16)
+            e = unit_of(feat_ref[v].astype(F32))[0].astype(BF16)
+            embed_ref[v] = e
+            lo_ref[v] = e[: rows // 2].astype(F32)
+            hi_ref[v] = e[rows // 2 :].astype(F32)
 
     cent_ref[...] = unit_of(proto_ref[...].astype(F32))[0].astype(BF16)
     for v in range(2):
@@ -71,7 +80,7 @@
             acc[v, r, :] += lane_fold(e)
             soft_ref[v, r, :] += jnp.dot(e.astype(BF16), cent_ref[...], preferred_element_type=F32)
             b = e * e
-            base_ref[v, r, :] = b.astype(BF16)
+            base_ref[0, v, r, :] = b.astype(BF16)
             return col + sub_fold(b)
 
         col = lax.fori_loop(0, rows // rc, step, jnp.zeros((8, kt), F32), unroll=True)
@@ -94,23 +103,26 @@
         grid=(n,),
         in_specs=[whole(2, rows, width), pl.BlockSpec((kt, width), lambda i: (i, 0))],
         out_specs=[
-            whole(2, rows, width),
+            whole(2, rows // 2, width),
+            whole(2, rows // 2, width),
             pl.BlockSpec((kt, width), lambda i: (i, 0)),
-            pl.BlockSpec((2, rows, kt), lambda i: (0, 0, i)),
+            pl.BlockSpec((1, 2, rows, kt), lambda i: (i, 0, 0, 0)),
             whole(2, n, kt),
             whole(2, rows),
             whole(2, rows, width),
         ],
         out_shape=[
-            jax.ShapeDtypeStruct((2, rows, width), BF16),
+            jax.ShapeDtypeStruct((2, rows // 2, width), F32),
+            jax.ShapeDtypeStruct((2, rows // 2, width), F32),
             jax.ShapeDtypeStruct((protos, width), BF16),
-            jax.ShapeDtypeStruct((2, rows, protos), BF16),
+            jax.ShapeDtypeStruct((n, 2, rows, kt), BF16),
             jax.ShapeDtypeStruct((2, n, kt), F32),
             jax.ShapeDtypeStruct((2, rows), F32),
             jax.ShapeDtypeStruct((2, rows, width), F32),
         ],
-        scratch_shapes=[pltpu.VMEM((2, rows, 128), F32)],
+        scratch_shapes=[pltpu.VMEM((2, rows, 128), F32), pltpu.VMEM((2, rows, width), BF16)],
         compiler_params=params(48),
+        cost_estimate=cost(16 * rows * protos * width, 4 * rows * protos),
         name="first",
     )(features, prototypes)
 
@@ -118,7 +130,7 @@
 def row_kernel(base_ref, *refs):
     *part_refs, out_ref, acc = refs
     i = pl.program_id(0)
-    rows = base_ref.shape[1]
+    rows = base_ref.shape[2]
     rc = 16
 
     @pl.when(i == 0)
@@ -130,7 +142,7 @@
 
         def step(j, carry):
             r = pl.ds(pl.multiple_of(j * rc, rc), rc)
-            acc[v, r, :] += lane_fold(base_ref[v, r, :].astype(F32) * c)
+            acc[v, r, :] += lane_fold(base_ref[0, v, r, :].astype(F32) * c)
             return carry
 
         lax.fori_loop(0, rows // rc, step, 0, unroll=4)
@@ -144,7 +156,7 @@
 def row_last_kernel(base_ref, cent_ref, *refs):
     *part_refs, out_ref, code_ref, acc = refs
     i = pl.program_id(0)
-    rows = base_ref.shape[1]
+    rows = base_ref.shape[2]
     rc = tile_of(rows, 256)
 
     @pl.when(i == 0)
@@ -157,7 +169,7 @@
 
         def step(j, carry):
             r = pl.ds(pl.multiple_of(j * rc, rc), rc)
-            w = base_ref[v, r, :].astype(F32) * c
+            w = base_ref[0, v, r, :].astype(F32) * c
             acc[v, r, :] += lane_fold(w)
             code_ref[v, r, :] += jnp.dot(w.astype(BF16), cent_ref[...], preferred_element_type=F32)
             return carry
@@ -171,10 +183,9 @@
 
 
 def row_pass(base, parts, centers=None):
-    _, rows, protos = base.shape
-    _, n, kt = parts[0].shape
+    n, _, rows, kt = base.shape
     whole = lambda *s: pl.BlockSpec(s, lambda i: (0,) * len(s))
-    in_specs = [pl.BlockSpec((2, rows, kt), lambda i: (0, 0, i))]
+    in_specs = [pl.BlockSpec((1, 2, rows, kt), lambda i: (i, 0, 0, 0))]
     out_specs = [whole(2, rows)]
     out_shape = [jax.ShapeDtypeStruct((2, rows), F32)]
     args = [base]
@@ -192,13 +203,14 @@
         out_shape=out_shape,
         scratch_shapes=[pltpu.VMEM((2, rows, 128), F32)],
         compiler_params=params(48),
+        cost_estimate=cost(0, 8 * n * rows * kt),
         name="row_pass" if centers is None else "row_last",
     )(*args, *parts)
 
 
 def col_kernel(base_ref, total_ref, out_ref, scale):
     i = pl.program_id(0)
-    rows, kt = base_ref.shape[1:]
+    rows, kt = base_ref.shape[2:]
     rc = 16
 
     @pl.when(i == 0)
@@ -211,53 +223,74 @@
         def step(j, col):
             r = pl.ds(pl.multiple_of(j * rc, rc), rc)
             w = jnp.concatenate([scale[v, r, :]] * (kt // 128), axis=1)
-            return col + sub_fold(base_ref[v, r, :].astype(F32) * w)
+            return col + sub_fold(base_ref[0, v, r, :].astype(F32) * w)
 
         col = lax.fori_loop(0, rows // rc, step, jnp.zeros((8, kt), F32), unroll=4)
         out_ref[v, pl.ds(i, 1), :] = jnp.sum(col, axis=0, keepdims=True)
 
 
-def col_pass(base, total, n):
-    _, rows, protos = base.shape
-    kt = protos // n
+def col_pass(base, total):
+    n, _, rows, kt = base.shape
     whole = lambda *s: pl.BlockSpec(s, lambda i: (0,) * len(s))
     return pl.pallas_call(
         col_kernel,
         grid=(n,),
-        in_specs=[pl.BlockSpec((2, rows, kt), lambda i: (0, 0, i)), whole(2, rows)],
+        in_specs=[pl.BlockSpec((1, 2, rows, kt), lambda i: (i, 0, 0, 0)), whole(2, rows)],
         out_specs=whole(2, n, kt),
         out_shape=jax.ShapeDtypeStruct((2, n, kt), F32),
         scratch_shapes=[pltpu.VMEM((2, rows, 128), F32)],
         compiler_params=params(48),
+        cost_estimate=cost(0, 8 * n * rows * kt),
         name="col_pass",
     )(base, total)
 
 
-def grad_kernel(cent_ref, embed_ref, tot_ref, row_ref, col_ref, out_ref, scale):
-    rows = embed_ref.shape[1]
-    kt = cent_ref.shape[0]
-    rc = tile_of(rows, 512)
+def pack_kernel(*refs):
+    *part_refs, out_ref = refs
+    for j, p in enumerate(part_refs):
+        out_ref[j] = p[...].astype(BF16)
+
+
+def pack(parts):
+    _, rc, width = parts[0].shape
+    m = len(parts)
+    return pl.pallas_call(
+        pack_kernel,
+        grid=(2,),
+        in_specs=[pl.BlockSpec((1, rc, width), lambda v: (v, 0, 0))] * m,
+        out_specs=pl.BlockSpec((m, 1, rc, width), lambda v: (0, v, 0, 0)),
+        out_shape=jax.ShapeDtypeStruct((m, 2, rc, width), BF16),
+        compiler_params=params(32),
+        cost_estimate=cost(0, 12 * m * rc * width),
+        name="pack",
+    )(*parts)
+
+
+def grad_kernel(cent_ref, col_ref, embed, *refs):
+    *row_refs, out_ref, scale = refs
+    m, _, rc, _ = embed.shape
+    i = pl.program_id(0)
     for v in range(2):
-        scale[v] = spread(col_ref[v, pl.ds(pl.program_id(0), 1), :])
-    cs = [jnp.concatenate([scale[v]] * (rc // 128), axis=1) for v in range(2)]
+        scale[v] = spread(col_ref[v, pl.ds(i, 1), :])
     total = jnp.zeros(out_ref.shape, F32)
-    for j in range(rows // rc):
-        r = slice(j * rc, (j + 1) * rc)
+    for j in range(m):
         es = []
         for v in range(2):
-            s = lax.dot_general(cent_ref[...], embed_ref[v, r, :], NT, preferred_element_type=F32)
+            s = lax.dot_general(cent_ref[...], embed[j, v], NT, preferred_element_type=F32)
             es.append(jnp.exp2(s * SOFT))
         for v in range(2):
             o = 1 - v
-            codes = es[o] * es[o] * (GRAD / row_ref[o : o + 1, r]) * cs[o]
-            g = (es[v] * (GRAD / tot_ref[v : v + 1, r]) - codes).astype(BF16)
-            total = total + jnp.dot(g, embed_ref[v, r, :], preferred_element_type=F32)
+            c = jnp.concatenate([scale[o]] * (rc // 128), axis=1)
+            r = slice(j % 2 * rc, (j % 2 + 1) * rc)
+            codes = es[o] * es[o] * (GRAD / row_refs[m // 2 + j // 2][o : o + 1, r]) * c
+            g = (es[v] * (GRAD / row_refs[j // 2][v : v + 1, r]) - codes).astype(BF16)
+            total = total + jnp.dot(g, embed[j, v], preferred_element_type=F32)
     out_ref[...] = total
 
 
-def grad_pass(centers, embed, tot, row, col):
+def grad_pass(centers, embeds, tot, row, col):
     protos, width = centers.shape
-    rows = embed.shape[1]
+    m, _, rc, _ = embeds.shape
     kt = tile_of(protos, 512)
     n = protos // kt
     whole = lambda *s: pl.BlockSpec(s, lambda i: (0,) * len(s))
@@ -266,17 +299,45 @@
         grid=(n,),
         in_specs=[
             pl.BlockSpec((kt, width), lambda i: (i, 0)),
-            whole(2, rows, width),
-            whole(2, rows),
-            whole(2, rows),
             whole(2, n, kt),
-        ],
+            whole(m, 2, rc, width),
+        ]
+        + [whole(2, 2 * rc)] * m,
         out_specs=pl.BlockSpec((kt, width), lambda i: (i, 0)),
         out_shape=jax.ShapeDtypeStruct((protos, width), F32),
         scratch_shapes=[pltpu.VMEM((2, kt, 128), F32)],
         compiler_params=params(48),
+        cost_estimate=cost(8 * protos * m * rc * width, 4 * m * rc * width),
         name="grad_pass",
-    )(centers, embed, tot, row, col.reshape(2, n, kt))
+    )(centers, col.reshape(2, n, kt), embeds, *tot, *row)
+
+
+def place_kernel(at_ref, *refs):
+    m = len(refs) - 2
+    out_ref, sems = refs[m], refs[m + 1]
+    copies = []
+    for j in range(m):
+        size = refs[j].shape[0]
+        where = pl.ds(pl.multiple_of(at_ref[j], 8), size)
+        copies.append(pltpu.make_async_copy(refs[j], out_ref.at[where], sems.at[j]))
+    for c in copies:
+        c.start()
+    for c in copies:
+        c.wait()
+
+
+def place(pieces, at, size):
+    m = len(pieces)
+    return pl.pallas_call(
+        place_kernel,
+        in_specs=[pl.BlockSpec(memory_space=pltpu.SMEM)]
+        + [pl.BlockSpec(memory_space=pltpu.VMEM)] * m,
+        out_specs=pl.BlockSpec(memory_space=pl.ANY),
+        out_shape=jax.ShapeDtypeStruct((size, pieces[0].shape[1]), F32),
+        scratch_shapes=[pltpu.SemaphoreType.DMA((m,))],
+        compiler_params=params(24),
+        name="place",
+    )(jnp.stack(at).astype(jnp.int32), *pieces)
 
 
 def swap(x, axis, n, m):
@@ -301,31 +362,157 @@
     return x
 
 
-def norm_back(grad, unit, inverse):
+def gather_plan(n):
+    bits = [2**j for j in range(1, n.bit_length()) if 2**j < n]
+    plan, keys_a, keys_b = [], [0], [0]
+    for m, w in zip(bits, bits[::-1]):
+        plan += [((k, m), (q, w)) for k, q in zip(keys_a, keys_b)]
+        keys_a, keys_b = keys_a + [k ^ m for k in keys_a], keys_b + [k ^ w for k in keys_b]
+    return plan
+
+
+def send_pair(have, pair, n):
+    for h, (k, m) in zip(have, pair):
+        h[k ^ m] = swap(h[k], "batch", n, m)
+
+
+def gather_rows(x, n):
+    return [x] + [swap(x, "batch", n, k) for k in range(2, n, 2)]
+
+
+def norm_back(grad, given):
+    x = given.astype(F32)
+    inverse = lax.rsqrt(jnp.sum(x * x, axis=-1, keepdims=True) + 1e-06)
+    unit = x * inverse
     return inverse * (grad - unit * jnp.sum(unit * grad, axis=-1, keepdims=True))
 
 
+def cut(x, at, size):
+    return lax.dynamic_slice_in_dim(x, at, size, axis=0)
+
+
+def halve_over_proto(x, n, m=1):
+    size = x.shape[0] // 2
+    side = (lax.axis_index("proto") // m) % 2
+    return cut(x, side * size, size), swap(cut(x, (1 - side) * size, size), "proto", n, m)
+
+
+def home(i, n, size):
+    at = 0 * i
+    for m in bits_of(n):
+        size //= 2
+        at = at + (i // m) % 2 * size
+    return at
+
+
+def spread_out(pieces, n):
+    bits = bits_of(n)[::-1]
+    keys = [0, bits[0]]
+    size = pieces[0].shape[0]
+    x = jnp.concatenate(pieces, axis=0)
+    for m in bits[1:-1]:
+        x = jnp.concatenate([x, swap(x, "proto", n, m)], axis=0)
+        keys = keys + [k ^ m for k in keys]
+    y = swap(x, "proto", n, bits[-1])
+    found = {}
+    for j, k in enumerate(keys):
+        found[k] = x[j * size : (j + 1) * size]
+        found[k ^ bits[-1]] = y[j * size : (j + 1) * size]
+    return found
+
+
+def bits_of(n):
+    return [2**j for j in range(n.bit_length()) if 2**j < n]
+
+
+def shard_back(pair, given, n):
+    x = pair[0] + pair[1]
+    for m in bits_of(n)[2:]:
+        a, b = halve_over_proto(x, n, m)
+        x = a + b
+    at = home(lax.axis_index("proto"), n, given.shape[0])
+    return norm_back(x, cut(given, at, x.shape[0]))
+
+
 def per_device(nb, npr, features, prototypes):
-    embed, centers, base, col, tot, soft = first(features, prototypes)
-    n = col.shape[1]
+    _, rows, width = features.shape
+    protos = prototypes.shape[0]
+    me = lax.axis_index("batch")
+    chip, core = me // 2, me % 2
+    share = protos // (nb // 2)
+
+    lo, hi, centers, base, col, tot, soft = first(features, prototypes)
     parts = col_exchange(col, nb)
     tot = row_exchange(tot, npr)
+    tots = gather_rows(tot, nb)
+    have, plan = [{0: lo}, {0: hi}], gather_plan(nb)
+    have, parts = lax.optimization_barrier((have, parts))
     for step in range(ITERS - 1):
+        if plan:
+            send_pair(have, plan.pop(0), nb)
         (row,) = row_pass(base, parts)
-        row = row_exchange(row, npr)
-        parts = col_exchange(col_pass(base, row, n), nb)
+        col = col_pass(base, row_exchange(row, npr))
+        col, have = lax.optimization_barrier((col, have))
+        parts = col_exchange(col, nb)
+        have, parts = lax.optimization_barrier((have, parts))
+    for pair in plan:
+        send_pair(have, pair, nb)
     row, code = row_pass(base, parts, centers)
     row = row_exchange(row, npr)
-    col = 1.0 / sum(parts)
-    grad_embed = soft * (GRAD / tot)[:, :, None] - (code * (GRAD / row)[:, :, None])[::-1]
-    grad_embed = lax.psum(grad_embed, "proto")
-    grad_centers = lax.psum(grad_pass(centers, embed, tot, row, col), "batch")
-    unit_feat, inv_feat = unit_of(features.astype(F32))
-    unit_proto, inv_proto = unit_of(prototypes.astype(F32))
-    return (
-        norm_back(grad_embed, unit_feat, inv_feat),
-        norm_back(grad_centers, unit_proto, inv_proto),
-    )
+    row, have = lax.optimization_barrier((row, have))
+    rows_all = gather_rows(row, nb)
+    embeds = pack([have[h][k] for k in range(0, nb, 2) for h in range(2)])
+    col = (1.0 / sum(parts)).reshape(2, protos)
+    half = share // 2
+    quarter = half // 2
+
+    def grads(at):
+        c = lax.dynamic_slice_in_dim(col, at, half, axis=1)
+        return grad_pass(cut(centers, at, half), embeds, tots, rows_all, c)
+
+    gf = [
+        soft[v] * (GRAD / tot[v])[:, None] - code[1 - v] * (GRAD / row[1 - v])[:, None]
+        for v in range(2)
+    ]
+    pair = halve_over_proto(gf[0], npr, 1)
+    theirs = grads(chip * share + (1 - core) * half)
+    theirs, pair, late = lax.optimization_barrier((theirs, pair, gf[1]))
+    theirs = swap(theirs, "batch", nb, 1)
+    pair = halve_over_proto(pair[0] + pair[1], npr, 2)
+    pair_late = halve_over_proto(late, npr, 1)
+    mine = grads(chip * share + core * half)
+    mine, theirs, pair, pair_late = lax.optimization_barrier((mine, theirs, pair, pair_late))
+    grad = norm_back(mine + theirs, cut(prototypes, chip * share + core * half, half))
+
+    have, plan = [{0: grad[:quarter]}, {0: grad[quarter:]}], gather_plan(nb)
+    last = bits_of(npr)[-1]
+    send_pair(have, plan.pop(0), nb)
+    shard = shard_back(pair, features[0], npr)
+    near = swap(shard, "proto", npr, last)
+    late = halve_over_proto(pair_late[0] + pair_late[1], npr, 2)
+    have, near, late = lax.optimization_barrier((have, near, late))
+    send_pair(have, plan.pop(0), nb)
+    shards = [spread_out([shard, near], npr), shard_back(late, features[1], npr)]
+    near = swap(shards[1], "proto", npr, last)
+    have, near, first_view = lax.optimization_barrier((have, near, shards[0]))
+    for p in plan:
+        send_pair(have, p, nb)
+    shards = [first_view, spread_out([shards[1], near], npr)]
+    idx = lax.axis_index("proto")
+    out, where = [], []
+    for v in range(2):
+        for k, x in shards[v].items():
+            out.append(x)
+            where.append(home(idx ^ k, npr, rows) + v * rows)
+    grad_features = place(out, where, 2 * rows).reshape(2, rows, width)
+
+    out, where = [], []
+    for k in have[0]:
+        for h in range(2):
+            at = (chip ^ (k // 2)) * share + h * quarter
+            out += [have[h][k], swap(have[h][k], "batch", nb, 1)]
+            where += [at + core * half, at + (1 - core) * half]
+    return grad_features, place(out, where, protos)
 
 
 def solution(mesh):

time: 406 us -> 299 us (0.74)
  waiting for transfers between devices: 191 us -> 84.9 us
  starting transfers between devices: 29.1 us -> 57.3 us
  other arithmetic: 33 us -> 8.44 us
  between operations: 14.2 us -> 1.51 us
  local copies, waits for them, and re-layouts: 6.22 us -> 12.2 us
    psum x2 -> x0, waiting for transfers between devices: 166 us -> none  [the longest x1 116 us: per_device(): grad_centers = lax.psum(grad_pass(centers, embed, tot, row, col), 'batch')]
    ppermute x20 -> x55, waiting for transfers between devices: 24.7 us -> 84.9 us  [swap(): return lax.ppermute(x, axis, [(i, i ^ m) for i in range(n)])]
    ppermute x20 -> x55, starting transfers between devices: 28.9 us -> 57.3 us  [swap(): return lax.ppermute(x, axis, [(i, i ^ m) for i in range(n)])]
    mul x2 -> x0, other arithmetic: 14.5 us -> none  [the longest x1 14.2 us: norm_back(): unit * jnp.sum(unit * grad, axis=-1, keepdims=True)]
    pallas_call x2 -> x5, Pallas kernels: 29.7 us -> 39.6 us  [the longest x2 29.8 us: col_pass(): pl.pallas_call(col_kernel, grid=(n,), in_specs=[pl.BlockSpec((1, 2, rows,...]
    pallas_call x1 -> x2, Pallas kernels: 27.9 us -> 20.5 us  [grad_pass(): pl.pallas_call(grad_kernel, grid=(n,), in_specs=[pl.BlockSpec((kt, width)...]
    reduce_sum x1 -> x3, other arithmetic: 6.69 us -> 1.86 us  [norm_back(): jnp.sum(unit * grad, axis=-1, keepdims=True)]
    mul x1 -> x3, other arithmetic: 6.29 us -> 1.69 us  [norm_back(): inverse * (grad - unit * jnp.sum(unit * grad, axis=-1, keepdims=True))]
  transfers between devices with their start and end apart: 22 -> 55, of which waited for: 18 -> 23; matrix products, arithmetic and copies ran while one was open for 4% -> 5% of each run, Pallas kernels for 11% -> 35%
where the time goes in v2:
time: 299 us; the launch traced here: 298 us
  Pallas kernels  134 us (45%)
  waiting for transfers between devices  84.9 us (28%)
  starting transfers between devices  57.3 us (19%)
  local copies, waits for them, and re-layouts  12.2 us (4%)
  other arithmetic  8.44 us (3%)
    ppermute x55, waiting for transfers between devices, swap(): return lax.ppermute(x, axis, [(i, i ^ m) for i in range(n)])  84.9 us
    ppermute x55, starting transfers between devices, swap(): return lax.ppermute(x, axis, [(i, i ^ m) for i in range(n)])  57.3 us
    pallas_call x3, Pallas kernels, row_pass(): pl.pallas_call(row_kernel if centers is None else row_last_kernel, grid=(...  48.7 us
    pallas_call x2, Pallas kernels, col_pass(): pl.pallas_call(col_kernel, grid=(n,), in_specs=[pl.BlockSpec((1, 2, rows,...  29.8 us
    pallas_call x1, Pallas kernels, first(): pl.pallas_call(first_kernel, grid=(n,), in_specs=[whole(2, rows, width),...  25.2 us
    pallas_call x2, Pallas kernels, grad_pass(): pl.pallas_call(grad_kernel, grid=(n,), in_specs=[pl.BlockSpec((kt, width)...  20.5 us
    pallas_call x2, Pallas kernels, place(): pl.pallas_call(place_kernel, in_specs=[pl.BlockSpec(memory_space=pltpu.SM...  7.82 us
    unnamed x47, local copies, waits for them, and re-layouts  7.04 us
  transfers between devices with their start and end apart: 55, of which 23 were waited for; matrix products, arithmetic and copies ran while one was open for 5% of the time, Pallas kernels for 35%

profile of v2, /device:TPU:0, one launch (start us, length us, event | category | flops | bytes accessed | tf_op | source)
XLA Modules:
  0.0 298.4 jit_solution(8316666620443888124)
XLA Ops:
  1.9 25.2 %first.1 = (f32[2,512,256]{2,1,0:T(8,128)S(1)}, f32[2,512,256]{2,1,0:T(8,128)S(1)}, bf16[8192,256]{1,0:T(8,128)(2,1)}, bf16[8,2,1024,1024]{3,2,1,0:T(8,128)(2,1)...) custom-call(bf16[2,1024,256]{2,1,0:T(8,128)(2,1)S(1)} %copy-done.11, ...), custom_call_target="tpu_custom_call" | custom-call | flops 34359738368 | bytes 33554432 | tf_op jit(solution)/shard_map/first/pallas_call | solution.py:101
  28.4 2.9 collective-permute-start.1
  31.3 1.5 collective-permute-start.2
  33.7 1.9 collective-permute-done.2.refs_2_
  35.6 2.4 collective-permute-done.3.refs_3_
  38.9 15.5 %row_pass.2 = f32[2,1024]{1,0:T(2,128)S(1)} custom-call(bf16[8,2,1024,1024]{3,2,1,0:T(8,128)(2,1)} %get-tuple-element.85.base_ref, f32[2,8,1024]{2,1,0:T(8,128)S(1)} %add.278.refs_0_, f32[2,8,1024]{2,1,0:T(8,128)S(1)} %collective-permute-done.1.refs_1_, f32[2,8,1024]{2,1,0:T(8,128)S(1)} %collective-permute-done.2.refs_2_, ...), custom_call_target="tpu_custom_call" | custom-call | bytes 67108864 | tf_op jit(solution)/shard_map/row_pass/pallas_call | solution.py:198
  54.4 1.7 collective-permute-start.4
  56.2 2.0 collective-permute-done.4
  58.2 2.7 collective-permute-start.5
  60.9 1.9 collective-permute-done.5
  62.7 14.9 %col_pass.2 = f32[2,8,1024]{2,1,0:T(8,128)S(1)} custom-call(bf16[8,2,1024,1024]{3,2,1,0:T(8,128)(2,1)} %get-tuple-element.85.base_ref, f32[2,1024]{1,0:T(2,128)S(1)} %add.280.total_ref), custom_call_target="tpu_custom_call" | custom-call | bytes 67108864 | tf_op jit(solution)/shard_map/col_pass/pallas_call | solution.py:235
  79.0 1.7 collective-permute-start.10
  83.3 3.1 %collective-permute-done.11.refs_3_ = f32[2,8,1024]{2,1,0:T(8,128)S(1)} collective-permute-done((f32[2,8,1024]{2,1,0:T(8,128)S(1)}, f32[2,8,1024]{2,1,0:T(8,128)S(1)}, u32[]{:S(2)}, u32[]{:S(2)}) %collective-permute-start.11) | collective-permute-done | bytes 65568 | tf_op jit(solution)/shard_map/ppermute | solution.py:344
  86.4 1.5 collective-permute-start.14
  88.9 15.5 %row_pass.3 = f32[2,1024]{1,0:T(2,128)S(1)} custom-call(bf16[8,2,1024,1024]{3,2,1,0:T(8,128)(2,1)} %get-tuple-element.85.base_ref, f32[2,8,1024]{2,1,0:T(8,128)S(1)} %add.281.refs_0_, f32[2,8,1024]{2,1,0:T(8,128)S(1)} %collective-permute-done.9.refs_1_, f32[2,8,1024]{2,1,0:T(8,128)S(1)} %collective-permute-done.10.refs_2_, ...), custom_call_target="tpu_custom_call" | custom-call | bytes 67108864 | tf_op jit(solution)/shard_map/row_pass/pallas_call | solution.py:198
  104.4 1.6 collective-permute-start.12
  106.1 2.1 collective-permute-done.12
  108.1 2.6 collective-permute-start.13
  110.7 2.0 collective-permute-done.13
  112.7 15.0 %col_pass.3 = f32[2,8,1024]{2,1,0:T(8,128)S(1)} custom-call(bf16[8,2,1024,1024]{3,2,1,0:T(8,128)(2,1)} %get-tuple-element.85.base_ref, f32[2,1024]{1,0:T(2,128)S(1)} %add.283.total_ref), custom_call_target="tpu_custom_call" | custom-call | bytes 67108864 | tf_op jit(solution)/shard_map/col_pass/pallas_call | solution.py:235
  129.7 1.6 collective-permute-start.24
  132.9 1.9 collective-permute-start.19
  141.7 2.7 collective-permute-start.25
  144.3 2.3 constant_dynamic-slice_fusion.9
  148.3 17.7 %row_last.1 = (f32[2,1024]{1,0:T(2,128)S(1)}, f32[2,1024,256]{2,1,0:T(8,128)S(1)}) custom-call(bf16[8,2,1024,1024]{3,2,1,0:T(8,128)(2,1)} %get-tuple-element.85.base_ref, bf16[8192,256]{1,0:T(8,128)(2,1)} %get-tuple-element.84.cent_ref, f32[2,8,1024]{2,1,0:T(8,128)S(1)} %add.284.refs_0_, f32[2,8,1024]{2,1,0:T(8,128)S(1)} %collective-permute-done.17.refs_1_, ...), custom_call_target="tpu_custom_call" | custom-call | bytes 67108864 | tf_op jit(solution)/shard_map/row_last/pallas_call | solution.py:198
  168.7 2.3 collective-permute-done.20
  171.0 2.2 collective-permute-start.21
  173.2 2.3 collective-permute-done.21
  175.5 1.9 collective-permute-start.28
  179.1 2.2 fusion.6
  181.3 2.0 collective-permute-start.31
  183.4 2.0 pack.1.embed
  186.8 10.3 %grad_pass.3 = f32[1024,256]{1,0:T(8,128)S(1)} custom-call(bf16[1024,256]{1,0:T(8,128)(2,1)S(1)} %copy-done.20, f32[2,2,512]{2,1,0:T(2,128)S(1)} %reshape.73.col_ref, bf16[8,2,512,256]{3,2,1,0:T(8,128)(2,1)S(1)} %pack.1.embed, f32[2,1024]{1,0:T(2,128)S(1)} %add.291.refs_0_, f32[2,1024]{1,0:T(2,128)S(1)} %collective-permute-done.26.refs_1_, ...), custom_call_target="tpu_custom_call" | custom-call | flops 8589934592 | bytes 4194304 | tf_op jit(solution)/shard_map/grad_pass/pallas_call | solution.py:297
  197.3 2.2 collective-permute-start.34
  200.5 10.3 %grad_pass.2 = f32[1024,256]{1,0:T(8,128)S(1)} custom-call(bf16[1024,256]{1,0:T(8,128)(2,1)S(1)} %copy-done.19, f32[2,2,512]{2,1,0:T(2,128)S(1)} %reshape.72.col_ref, bf16[8,2,512,256]{3,2,1,0:T(8,128)(2,1)S(1)} %pack.1.embed, f32[2,1024]{1,0:T(2,128)S(1)} %add.291.refs_0_, f32[2,1024]{1,0:T(2,128)S(1)} %collective-permute-done.26.refs_1_, ...), custom_call_target="tpu_custom_call" | custom-call | flops 8589934592 | bytes 4194304 | tf_op jit(solution)/shard_map/grad_pass/pallas_call | solution.py:297
  210.8 1.9 collective-permute-done.34
  212.7 6.3 %collective-permute-done.35 = f32[512,256]{1,0:T(8,128)S(1)} collective-permute-done((f32[512,256]{1,0:T(8,128)S(1)}, f32[512,256]{1,0:T(8,128)S(1)}, u32[]{:S(2)}, u32[]{:S(2)}) %collective-permute-start.35) | collective-permute-done | bytes 524320 | tf_op jit(solution)/shard_map/ppermute | solution.py:344
  219.3 1.5 fusion.2
  224.5 2.3 collective-permute-start.38
  226.9 12.4 %collective-permute-done.39 = f32[256,256]{1,0:T(8,128)S(1)} collective-permute-done((f32[256,256]{1,0:T(8,128)S(1)}, f32[256,256]{1,0:T(8,128)S(1)}, u32[]{:S(2)}, u32[]{:S(2)}) %collective-permute-start.39) | collective-permute-done | bytes 262176 | tf_op jit(solution)/shard_map/ppermute | solution.py:344
  239.3 5.3 %collective-permute-done.38.refs_2_ = f32[256,256]{1,0:T(8,128)S(1)} collective-permute-done((f32[256,256]{1,0:T(8,128)S(1)}, f32[256,256]{1,0:T(8,128)S(1)}, u32[]{:S(2)}, u32[]{:S(2)}) %collective-permute-start.38) | collective-permute-done | bytes 262176 | tf_op jit(solution)/shard_map/ppermute | solution.py:344
  246.4 2.5 collective-permute-start.42
  248.8 15.2 %collective-permute-done.43 = f32[512,256]{1,0:T(8,128)S(1)} collective-permute-done((f32[512,256]{1,0:T(8,128)S(1)}, f32[512,256]{1,0:T(8,128)S(1)}, u32[]{:S(2)}, u32[]{:S(2)}) %collective-permute-start.43) | collective-permute-done | bytes 524320 | tf_op jit(solution)/shard_map/ppermute | solution.py:344
  265.7 11.3 %collective-permute-done.51.refs_12_ = f32[512,256]{1,0:T(8,128)} collective-permute-done((f32[512,256]{1,0:T(8,128)S(1)}, f32[512,256]{1,0:T(8,128)}, u32[]{:S(2)}, u32[]{:S(2)}) %collective-permute-start.51) | collective-permute-done | bytes 524320 | tf_op jit(solution)/shard_map/ppermute | solution.py:344
  277.6 1.6 collective-permute-done.53.refs_14_
  282.6 6.3 %collective-permute-done.44 = f32[512,256]{1,0:T(8,128)} collective-permute-done((f32[512,256]{1,0:T(8,128)S(1)}, f32[512,256]{1,0:T(8,128)}, u32[]{:S(2)}, u32[]{:S(2)}) %collective-permute-start.44) | collective-permute-done | bytes 524320 | tf_op jit(solution)/shard_map/ppermute | solution.py:344
  290.3 1.9 place.2
  292.3 5.9 %place.3 = f32[8192,256]{1,0:T(8,128)} custom-call(s32[16]{0:T(128)S(1)} %stack.103.at_ref, f32[512,256]{1,0:T(8,128)S(1)} %get-tuple-element.160.refs_0_, f32[512,256]{1,0:T(8,128)S(1)} %copy-done.16, f32[512,256]{1,0:T(8,128)S(1)} %get-tuple-element.161.refs_2_, f32[512,256]{1,0:T(8,128)S(1)} %copy-done.18, ...), custom_call_target="tpu_custom_call" | custom-call | tf_op jit(solution)/shard_map/place/pallas_call | solution.py:331
  (165 shorter events, 41.3 us)
Async XLA Ops:
  28.4 5.3 %collective-permute-start.1 = (f32[2,8,1024]{2,1,0:T(8,128)S(1)}, f32[2,8,1024]{2,1,0:T(8,128)S(1)}, u32[]{:S(2)}, u32[]{:S(2)}) collective-permute-start(f32[2,8,1024]{2,1,0:T(8,128)S(1)} %add.278.refs_0_), channel_id=1, source_target_pairs={{0,8},{4,12},{8,0},{12,4},{16,24},{20,28},{24,16},{28,20},{1,9},{5... | collective-permute-start | bytes 196616 | tf_op jit(solution)/shard_map/ppermute | solution.py:344
  31.3 4.3 %collective-permute-start.2 = (f32[2,8,1024]{2,1,0:T(8,128)S(1)}, f32[2,8,1024]{2,1,0:T(8,128)S(1)}, u32[]{:S(2)}, u32[]{:S(2)}) collective-permute-start(f32[2,8,1024]{2,1,0:T(8,128)S(1)} %add.278.refs_0_), channel_id=1, source_target_pairs={{0,16},{4,20},{8,24},{12,28},{16,0},{20,4},{24,8},{28,12},{1,17},{... | collective-permute-start | bytes 196616 | tf_op jit(solution)/shard_map/ppermute | solution.py:344
  32.8 5.2 %collective-permute-start.3 = (f32[2,8,1024]{2,1,0:T(8,128)S(1)}, f32[2,8,1024]{2,1,0:T(8,128)S(1)}, u32[]{:S(2)}, u32[]{:S(2)}) collective-permute-start(f32[2,8,1024]{2,1,0:T(8,128)S(1)} %add.278.refs_0_), channel_id=1, source_target_pairs={{0,24},{4,28},{8,16},{12,20},{16,8},{20,12},{24,0},{28,4},{1,25},{... | collective-permute-start | bytes 196616 | tf_op jit(solution)/shard_map/ppermute | solution.py:344
  38.0 39.6 %collective-permute-start.6 = (f32[2,512,256]{2,1,0:T(8,128)S(1)}, f32[2,512,256]{2,1,0:T(8,128)S(1)}, u32[]{:S(2)}, u32[]{:S(2)}) collective-permute-start(f32[2,512,256]{2,1,0:T(8,128)S(1)} %get-tuple-element.126.refs_0_), channel_id=1, source_target_pairs={{0,8},{4,12},{8,0},{12,4},{16,24},{20,28},{24,16},{28,20},{1,9},{5... | collective-permute-start | bytes 3145736 | tf_op jit(solution)/shard_map/ppermute | solution.py:344
  38.5 39.1 %collective-permute-start.7 = (f32[2,512,256]{2,1,0:T(8,128)S(1)}, f32[2,512,256]{2,1,0:T(8,128)S(1)}, u32[]{:S(2)}, u32[]{:S(2)}) collective-permute-start(f32[2,512,256]{2,1,0:T(8,128)S(1)} %get-tuple-element.127.refs_1_), channel_id=1, source_target_pairs={{0,16},{4,20},{8,24},{12,28},{16,0},{20,4},{24,8},{28,12},{1,17},{... | collective-permute-start | bytes 3145736 | tf_op jit(solution)/shard_map/ppermute | solution.py:344
  58.2 4.5 %collective-permute-start.5 = (f32[2,1024]{1,0:T(2,128)S(1)}, f32[2,1024]{1,0:T(2,128)S(1)}, u32[]{:S(2)}, u32[]{:S(2)}) collective-permute-start(f32[2,1024]{1,0:T(2,128)S(1)} %add.279), channel_id=1, source_target_pairs={{0,2},{1,3},{2,0},{3,1},{4,6},{5,7},{6,4},{7,5},{8,10},{9,11},{10,... | collective-permute-start | bytes 24584 | tf_op jit(solution)/shard_map/ppermute | solution.py:344
  79.0 4.3 %collective-permute-start.10 = (f32[2,8,1024]{2,1,0:T(8,128)S(1)}, f32[2,8,1024]{2,1,0:T(8,128)S(1)}, u32[]{:S(2)}, u32[]{:S(2)}) collective-permute-start(f32[2,8,1024]{2,1,0:T(8,128)S(1)} %add.281.refs_0_), channel_id=1, source_target_pairs={{0,16},{4,20},{8,24},{12,28},{16,0},{20,4},{24,8},{28,12},{1,17},{... | collective-permute-start | bytes 196616 | tf_op jit(solution)/shard_map/ppermute | solution.py:344
  80.7 5.7 %collective-permute-start.11 = (f32[2,8,1024]{2,1,0:T(8,128)S(1)}, f32[2,8,1024]{2,1,0:T(8,128)S(1)}, u32[]{:S(2)}, u32[]{:S(2)}) collective-permute-start(f32[2,8,1024]{2,1,0:T(8,128)S(1)} %add.281.refs_0_), channel_id=1, source_target_pairs={{0,24},{4,28},{8,16},{12,20},{16,8},{20,12},{24,0},{28,4},{1,25},{... | collective-permute-start | bytes 196616 | tf_op jit(solution)/shard_map/ppermute | solution.py:344
  82.1 4.3 %collective-permute-start.9 = (f32[2,8,1024]{2,1,0:T(8,128)S(1)}, f32[2,8,1024]{2,1,0:T(8,128)S(1)}, u32[]{:S(2)}, u32[]{:S(2)}) collective-permute-start(f32[2,8,1024]{2,1,0:T(8,128)S(1)} %add.281.refs_0_), channel_id=1, source_target_pairs={{0,8},{4,12},{8,0},{12,4},{16,24},{20,28},{24,16},{28,20},{1,9},{5... | collective-permute-start | bytes 196616 | tf_op jit(solution)/shard_map/ppermute | solution.py:344
  86.4 41.3 %collective-permute-start.14 = (f32[2,512,256]{2,1,0:T(8,128)S(1)}, f32[2,512,256]{2,1,0:T(8,128)S(1)}, u32[]{:S(2)}, u32[]{:S(2)}) collective-permute-start(f32[2,512,256]{2,1,0:T(8,128)S(1)} %get-tuple-element.126.refs_0_), channel_id=1, source_target_pairs={{0,16},{4,20},{8,24},{12,28},{16,0},{20,4},{24,8},{28,12},{1,17},{... | collective-permute-start | bytes 3145736 | tf_op jit(solution)/shard_map/ppermute | solution.py:344
  87.9 40.8 %collective-permute-start.15 = (f32[2,512,256]{2,1,0:T(8,128)S(1)}, f32[2,512,256]{2,1,0:T(8,128)S(1)}, u32[]{:S(2)}, u32[]{:S(2)}) collective-permute-start(f32[2,512,256]{2,1,0:T(8,128)S(1)} %get-tuple-element.127.refs_1_), channel_id=1, source_target_pairs={{0,8},{4,12},{8,0},{12,4},{16,24},{20,28},{24,16},{28,20},{1,9},{5... | collective-permute-start | bytes 3145736 | tf_op jit(solution)/shard_map/ppermute | solution.py:344
  108.1 4.5 %collective-permute-start.13 = (f32[2,1024]{1,0:T(2,128)S(1)}, f32[2,1024]{1,0:T(2,128)S(1)}, u32[]{:S(2)}, u32[]{:S(2)}) collective-permute-start(f32[2,1024]{1,0:T(2,128)S(1)} %add.282), channel_id=1, source_target_pairs={{0,2},{1,3},{2,0},{3,1},{4,6},{5,7},{6,4},{7,5},{8,10},{9,11},{10,... | collective-permute-start | bytes 24584 | tf_op jit(solution)/shard_map/ppermute | solution.py:344
  129.7 11.9 %collective-permute-start.24 = (f32[2,1024]{1,0:T(2,128)S(1)}, f32[2,1024]{1,0:T(2,128)S(1)}, u32[]{:S(2)}, u32[]{:S(2)}) collective-permute-start(f32[2,1024]{1,0:T(2,128)S(1)} %get-tuple-element.134), channel_id=1, source_target_pairs={{0,1},{1,0},{2,3},{3,2},{4,5},{5,4},{6,7},{7,6},{8,9},{9,8},{10,11... | collective-permute-start | bytes 24584 | tf_op jit(solution)/shard_map/ppermute | solution.py:344
  131.3 5.9 %collective-permute-start.17 = (f32[2,8,1024]{2,1,0:T(8,128)S(1)}, f32[2,8,1024]{2,1,0:T(8,128)S(1)}, u32[]{:S(2)}, u32[]{:S(2)}) collective-permute-start(f32[2,8,1024]{2,1,0:T(8,128)S(1)} %add.284.refs_0_), channel_id=1, source_target_pairs={{0,8},{4,12},{8,0},{12,4},{16,24},{20,28},{24,16},{28,20},{1,9},{5... | collective-permute-start | bytes 196616 | tf_op jit(solution)/shard_map/ppermute | solution.py:344
  132.4 5.0 %collective-permute-start.18 = (f32[2,8,1024]{2,1,0:T(8,128)S(1)}, f32[2,8,1024]{2,1,0:T(8,128)S(1)}, u32[]{:S(2)}, u32[]{:S(2)}) collective-permute-start(f32[2,8,1024]{2,1,0:T(8,128)S(1)} %add.284.refs_0_), channel_id=1, source_target_pairs={{0,16},{4,20},{8,24},{12,28},{16,0},{20,4},{24,8},{28,12},{1,17},{... | collective-permute-start | bytes 196616 | tf_op jit(solution)/shard_map/ppermute | solution.py:344
  132.9 5.2 %collective-permute-start.19 = (f32[2,8,1024]{2,1,0:T(8,128)S(1)}, f32[2,8,1024]{2,1,0:T(8,128)S(1)}, u32[]{:S(2)}, u32[]{:S(2)}) collective-permute-start(f32[2,8,1024]{2,1,0:T(8,128)S(1)} %add.284.refs_0_), channel_id=1, source_target_pairs={{0,24},{4,28},{8,16},{12,20},{16,8},{20,12},{24,0},{28,4},{1,25},{... | collective-permute-start | bytes 196616 | tf_op jit(solution)/shard_map/ppermute | solution.py:344
  138.1 39.4 %collective-permute-start.22 = (f32[2,512,256]{2,1,0:T(8,128)}, f32[2,512,256]{2,1,0:T(8,128)}, u32[]{:S(2)}, u32[]{:S(2)}) collective-permute-start(f32[2,512,256]{2,1,0:T(8,128)} %copy-done.3), channel_id=1, source_target_pairs={{0,16},{4,20},{8,24},{12,28},{16,0},{20,4},{24,8},{28,12},{1,17},{... | collective-permute-start | bytes 3145736 | tf_op jit(solution)/shard_map/ppermute | solution.py:344
  139.6 37.9 %collective-permute-start.23 = (f32[2,512,256]{2,1,0:T(8,128)}, f32[2,512,256]{2,1,0:T(8,128)}, u32[]{:S(2)}, u32[]{:S(2)}) collective-permute-start(f32[2,512,256]{2,1,0:T(8,128)} %copy-done.5), channel_id=1, source_target_pairs={{0,8},{4,12},{8,0},{12,4},{16,24},{20,28},{24,16},{28,20},{1,9},{5... | collective-permute-start | bytes 3145736 | tf_op jit(solution)/shard_map/ppermute | solution.py:344
  141.7 5.0 %collective-permute-start.25 = (f32[2,1024]{1,0:T(2,128)S(1)}, f32[2,1024]{1,0:T(2,128)S(1)}, u32[]{:S(2)}, u32[]{:S(2)}) collective-permute-start(f32[2,1024]{1,0:T(2,128)S(1)} %add.290), channel_id=1, source_target_pairs={{0,2},{1,3},{2,0},{3,1},{4,6},{5,7},{6,4},{7,5},{8,10},{9,11},{10,... | collective-permute-start | bytes 24584 | tf_op jit(solution)/shard_map/ppermute | solution.py:344
  146.6 34.7 %collective-permute-start.26 = (f32[2,1024]{1,0:T(2,128)S(1)}, f32[2,1024]{1,0:T(2,128)S(1)}, u32[]{:S(2)}, u32[]{:S(2)}) collective-permute-start(f32[2,1024]{1,0:T(2,128)S(1)} %add.291.refs_0_), channel_id=1, source_target_pairs={{0,8},{4,12},{8,0},{12,4},{16,24},{20,28},{24,16},{28,20},{1,9},{5... | collective-permute-start | bytes 24584 | tf_op jit(solution)/shard_map/ppermute | solution.py:344
  147.7 37.7 %collective-permute-start.27 = (f32[2,1024]{1,0:T(2,128)S(1)}, f32[2,1024]{1,0:T(2,128)S(1)}, u32[]{:S(2)}, u32[]{:S(2)}) collective-permute-start(f32[2,1024]{1,0:T(2,128)S(1)} %add.291.refs_0_), channel_id=1, source_target_pairs={{0,16},{4,20},{8,24},{12,28},{16,0},{20,4},{24,8},{28,12},{1,17},{... | collective-permute-start | bytes 24584 | tf_op jit(solution)/shard_map/ppermute | solution.py:344
  171.0 4.5 %collective-permute-start.21 = (f32[2,1024]{1,0:T(2,128)S(1)}, f32[2,1024]{1,0:T(2,128)S(1)}, u32[]{:S(2)}, u32[]{:S(2)}) collective-permute-start(f32[2,1024]{1,0:T(2,128)S(1)} %add.288), channel_id=1, source_target_pairs={{0,2},{1,3},{2,0},{3,1},{4,6},{5,7},{6,4},{7,5},{8,10},{9,11},{10,... | collective-permute-start | bytes 24584 | tf_op jit(solution)/shard_map/ppermute | solution.py:344
  175.5 11.3 %collective-permute-start.28 = (f32[2,1024]{1,0:T(2,128)S(1)}, f32[2,1024]{1,0:T(2,128)S(1)}, u32[]{:S(2)}, u32[]{:S(2)}) collective-permute-start(f32[2,1024]{1,0:T(2,128)S(1)} %add.291.refs_0_), channel_id=1, source_target_pairs={{0,24},{4,28},{8,16},{12,20},{16,8},{20,12},{24,0},{28,4},{1,25},{... | collective-permute-start | bytes 24584 | tf_op jit(solution)/shard_map/ppermute | solution.py:344
  177.5 9.3 %collective-permute-start.29 = (f32[2,1024]{1,0:T(2,128)S(1)}, f32[2,1024]{1,0:T(2,128)S(1)}, u32[]{:S(2)}, u32[]{:S(2)}) collective-permute-start(f32[2,1024]{1,0:T(2,128)S(1)} %add.289.refs_4_), channel_id=1, source_target_pairs={{0,8},{4,12},{8,0},{12,4},{16,24},{20,28},{24,16},{28,20},{1,9},{5... | collective-permute-start | bytes 24584 | tf_op jit(solution)/shard_map/ppermute | solution.py:344
  178.6 8.2 %collective-permute-start.30 = (f32[2,1024]{1,0:T(2,128)S(1)}, f32[2,1024]{1,0:T(2,128)S(1)}, u32[]{:S(2)}, u32[]{:S(2)}) collective-permute-start(f32[2,1024]{1,0:T(2,128)S(1)} %add.289.refs_4_), channel_id=1, source_target_pairs={{0,16},{4,20},{8,24},{12,28},{16,0},{20,4},{24,8},{28,12},{1,17},{... | collective-permute-start | bytes 24584 | tf_op jit(solution)/shard_map/ppermute | solution.py:344
  181.3 5.5 %collective-permute-start.31 = (f32[2,1024]{1,0:T(2,128)S(1)}, f32[2,1024]{1,0:T(2,128)S(1)}, u32[]{:S(2)}, u32[]{:S(2)}) collective-permute-start(f32[2,1024]{1,0:T(2,128)S(1)} %add.289.refs_4_), channel_id=1, source_target_pairs={{0,24},{4,28},{8,16},{12,20},{16,8},{20,12},{24,0},{28,4},{1,25},{... | collective-permute-start | bytes 24584 | tf_op jit(solution)/shard_map/ppermute | solution.py:344
  185.5 11.7 %collective-permute-start.32 = (f32[512,256]{1,0:T(8,128)S(1)}, f32[512,256]{1,0:T(8,128)S(1)}, u32[]{:S(2)}, u32[]{:S(2)}) collective-permute-start(f32[512,256]{1,0:T(8,128)S(1)} %get-tuple-element.182), channel_id=1, source_target_pairs={{0,1},{1,0},{2,3},{3,2},{4,5},{5,4},{6,7},{7,6},{8,9},{9,8},{10,11... | collective-permute-start | bytes 1572872 | tf_op jit(solution)/shard_map/ppermute | solution.py:344
  197.1 21.9 %collective-permute-start.33 = (f32[1024,256]{1,0:T(8,128)S(1)}, f32[1024,256]{1,0:T(8,128)S(1)}, u32[]{:S(2)}, u32[]{:S(2)}) collective-permute-start(f32[1024,256]{1,0:T(8,128)S(1)} %grad_pass.3), channel_id=1, source_target_pairs={{0,4},{4,0},{8,12},{12,8},{16,20},{20,16},{24,28},{28,24},{1,5},{5... | collective-permute-start | bytes 3145736 | tf_op jit(solution)/shard_map/ppermute | solution.py:344
  197.3 15.4 %collective-permute-start.34 = (f32[256,256]{1,0:T(8,128)S(1)}, f32[256,256]{1,0:T(8,128)S(1)}, u32[]{:S(2)}, u32[]{:S(2)}) collective-permute-start(f32[256,256]{1,0:T(8,128)S(1)} %get-tuple-element.190), channel_id=1, source_target_pairs={{0,2},{1,3},{2,0},{3,1},{4,6},{5,7},{6,4},{7,5},{8,10},{9,11},{10,... | collective-permute-start | bytes 786440 | tf_op jit(solution)/shard_map/ppermute | solution.py:344
  199.6 19.4 %collective-permute-start.35 = (f32[512,256]{1,0:T(8,128)S(1)}, f32[512,256]{1,0:T(8,128)S(1)}, u32[]{:S(2)}, u32[]{:S(2)}) collective-permute-start(f32[512,256]{1,0:T(8,128)S(1)} %get-tuple-element.180), channel_id=1, source_target_pairs={{0,1},{1,0},{2,3},{3,2},{4,5},{5,4},{6,7},{7,6},{8,9},{9,8},{10,11... | collective-permute-start | bytes 1572872 | tf_op jit(solution)/shard_map/ppermute | solution.py:344
  219.2 20.1 %collective-permute-start.39 = (f32[256,256]{1,0:T(8,128)S(1)}, f32[256,256]{1,0:T(8,128)S(1)}, u32[]{:S(2)}, u32[]{:S(2)}) collective-permute-start(f32[256,256]{1,0:T(8,128)S(1)} %get-tuple-element.188), channel_id=1, source_target_pairs={{0,2},{1,3},{2,0},{3,1},{4,6},{5,7},{6,4},{7,5},{8,10},{9,11},{10,... | collective-permute-start | bytes 786440 | tf_op jit(solution)/shard_map/ppermute | solution.py:344
  222.3 22.4 %collective-permute-start.36 = (f32[512,256]{1,0:T(8,128)S(1)}, f32[512,256]{1,0:T(8,128)S(1)}, u32[]{:S(2)}, u32[]{:S(2)}) collective-permute-start(f32[512,256]{1,0:T(8,128)S(1)} %get-tuple-element.160.refs_0_), channel_id=1, source_target_pairs={{0,8},{4,12},{8,0},{12,4},{16,24},{20,28},{24,16},{28,20},{1,9},{5... | collective-permute-start | bytes 1572872 | tf_op jit(solution)/shard_map/ppermute | solution.py:344
  223.3 21.3 %collective-permute-start.37 = (f32[512,256]{1,0:T(8,128)S(1)}, f32[512,256]{1,0:T(8,128)}, u32[]{:S(2)}, u32[]{:S(2)}) collective-permute-start(f32[512,256]{1,0:T(8,128)S(1)} %get-tuple-element.161.refs_2_), channel_id=1, source_target_pairs={{0,16},{4,20},{8,24},{12,28},{16,0},{20,4},{24,8},{28,12},{1,17},{... | collective-permute-start | bytes 1572872 | tf_op jit(solution)/shard_map/ppermute | solution.py:344
  224.5 20.1 %collective-permute-start.38 = (f32[256,256]{1,0:T(8,128)S(1)}, f32[256,256]{1,0:T(8,128)S(1)}, u32[]{:S(2)}, u32[]{:S(2)}) collective-permute-start(f32[256,256]{1,0:T(8,128)S(1)} %fusion.17.refs_0_), channel_id=1, source_target_pairs={{0,2},{1,3},{2,0},{3,1},{4,6},{5,7},{6,4},{7,5},{8,10},{9,11},{10,... | collective-permute-start | bytes 786440 | tf_op jit(solution)/shard_map/ppermute | solution.py:344
  244.7 19.3 %collective-permute-start.43 = (f32[512,256]{1,0:T(8,128)S(1)}, f32[512,256]{1,0:T(8,128)S(1)}, u32[]{:S(2)}, u32[]{:S(2)}) collective-permute-start(f32[512,256]{1,0:T(8,128)S(1)} %pad_maximum_fusion), channel_id=1, source_target_pairs={{0,1},{1,0},{2,3},{3,2},{4,5},{5,4},{6,7},{7,6},{8,9},{9,8},{10,11... | collective-permute-start | bytes 1572872 | tf_op jit(solution)/shard_map/ppermute | solution.py:344
  244.8 19.3 %collective-permute-start.40 = (f32[512,256]{1,0:T(8,128)S(1)}, f32[512,256]{1,0:T(8,128)}, u32[]{:S(2)}, u32[]{:S(2)}) collective-permute-start(f32[512,256]{1,0:T(8,128)S(1)} %get-tuple-element.160.refs_0_), channel_id=1, source_target_pairs={{0,16},{4,20},{8,24},{12,28},{16,0},{20,4},{24,8},{28,12},{1,17},{... | collective-permute-start | bytes 1572872 | tf_op jit(solution)/shard_map/ppermute | solution.py:344
  245.5 18.6 %collective-permute-start.41 = (f32[512,256]{1,0:T(8,128)S(1)}, f32[512,256]{1,0:T(8,128)}, u32[]{:S(2)}, u32[]{:S(2)}) collective-permute-start(f32[512,256]{1,0:T(8,128)S(1)} %get-tuple-element.161.refs_2_), channel_id=1, source_target_pairs={{0,8},{4,12},{8,0},{12,4},{16,24},{20,28},{24,16},{28,20},{1,9},{5... | collective-permute-start | bytes 1572872 | tf_op jit(solution)/shard_map/ppermute | solution.py:344
  246.4 17.7 %collective-permute-start.42 = (f32[256,256]{1,0:T(8,128)S(1)}, f32[256,256]{1,0:T(8,128)S(1)}, u32[]{:S(2)}, u32[]{:S(2)}) collective-permute-start(f32[256,256]{1,0:T(8,128)S(1)} %fusion.14.refs_4_), channel_id=1, source_target_pairs={{0,2},{1,3},{2,0},{3,1},{4,6},{5,7},{6,4},{7,5},{8,10},{9,11},{10,... | collective-permute-start | bytes 786440 | tf_op jit(solution)/shard_map/ppermute | solution.py:344
  264.0 12.9 %collective-permute-start.51 = (f32[512,256]{1,0:T(8,128)S(1)}, f32[512,256]{1,0:T(8,128)}, u32[]{:S(2)}, u32[]{:S(2)}) collective-permute-start(f32[512,256]{1,0:T(8,128)S(1)} %collective-permute-done.36.refs_4_), channel_id=1, source_target_pairs={{0,16},{4,20},{8,24},{12,28},{16,0},{20,4},{24,8},{28,12},{1,17},{... | collective-permute-start | bytes 1572872 | tf_op jit(solution)/shard_map/ppermute | solution.py:344
  264.5 16.8 %collective-permute-start.47 = (f32[512,256]{1,0:T(8,128)S(1)}, f32[512,256]{1,0:T(8,128)S(1)}, u32[]{:S(2)}, u32[]{:S(2)}) collective-permute-start(f32[512,256]{1,0:T(8,128)S(1)} %collective-permute-done.36.refs_4_), channel_id=1, source_target_pairs={{0,4},{4,0},{8,12},{12,8},{16,20},{20,16},{24,28},{28,24},{1,5},{5... | collective-permute-start | bytes 1572872 | tf_op jit(solution)/shard_map/ppermute | solution.py:344
  264.5 14.7 %collective-permute-start.53 = (f32[512,256]{1,0:T(8,128)}, f32[512,256]{1,0:T(8,128)}, u32[]{:S(2)}, u32[]{:S(2)}) collective-permute-start(f32[512,256]{1,0:T(8,128)} %collective-permute-done.37.refs_10_), channel_id=1, source_target_pairs={{0,8},{4,12},{8,0},{12,4},{16,24},{20,28},{24,16},{28,20},{1,9},{5... | collective-permute-start | bytes 1572872 | tf_op jit(solution)/shard_map/ppermute | solution.py:344
  265.2 14.0 %collective-permute-start.45 = (f32[512,256]{1,0:T(8,128)S(1)}, f32[512,256]{1,0:T(8,128)S(1)}, u32[]{:S(2)}, u32[]{:S(2)}) collective-permute-start(f32[512,256]{1,0:T(8,128)S(1)} %get-tuple-element.160.refs_0_), channel_id=1, source_target_pairs={{0,4},{4,0},{8,12},{12,8},{16,20},{20,16},{24,28},{28,24},{1,5},{5... | collective-permute-start | bytes 1572872 | tf_op jit(solution)/shard_map/ppermute | solution.py:344
  265.3 15.2 %collective-permute-start.46 = (f32[512,256]{1,0:T(8,128)S(1)}, f32[512,256]{1,0:T(8,128)S(1)}, u32[]{:S(2)}, u32[]{:S(2)}) collective-permute-start(f32[512,256]{1,0:T(8,128)S(1)} %get-tuple-element.161.refs_2_), channel_id=1, source_target_pairs={{0,4},{4,0},{8,12},{12,8},{16,20},{20,16},{24,28},{28,24},{1,5},{5... | collective-permute-start | bytes 1572872 | tf_op jit(solution)/shard_map/ppermute | solution.py:344
  277.0 11.9 %collective-permute-start.44 = (f32[512,256]{1,0:T(8,128)S(1)}, f32[512,256]{1,0:T(8,128)}, u32[]{:S(2)}, u32[]{:S(2)}) collective-permute-start(f32[512,256]{1,0:T(8,128)S(1)} %pad_maximum_fusion.1), channel_id=1, source_target_pairs={{0,1},{1,0},{2,3},{3,2},{4,5},{5,4},{6,7},{7,6},{8,9},{9,8},{10,11... | collective-permute-start | bytes 1572872 | tf_op jit(solution)/shard_map/ppermute | solution.py:344
  279.2 13.1 %collective-permute-start.50 = (f32[512,256]{1,0:T(8,128)}, f32[512,256]{1,0:T(8,128)}, u32[]{:S(2)}, u32[]{:S(2)}) collective-permute-start(f32[512,256]{1,0:T(8,128)} %collective-permute-done.37.refs_10_), channel_id=1, source_target_pairs={{0,4},{4,0},{8,12},{12,8},{16,20},{20,16},{24,28},{28,24},{1,5},{5... | collective-permute-start | bytes 1572872 | tf_op jit(solution)/shard_map/ppermute | solution.py:344
  280.0 12.2 %collective-permute-start.48 = (f32[512,256]{1,0:T(8,128)}, f32[512,256]{1,0:T(8,128)}, u32[]{:S(2)}, u32[]{:S(2)}) collective-permute-start(f32[512,256]{1,0:T(8,128)} %collective-permute-done.41.refs_6_), channel_id=1, source_target_pairs={{0,4},{4,0},{8,12},{12,8},{16,20},{20,16},{24,28},{28,24},{1,5},{5... | collective-permute-start | bytes 1572872 | tf_op jit(solution)/shard_map/ppermute | solution.py:344
  281.3 10.9 %collective-permute-start.49 = (f32[512,256]{1,0:T(8,128)}, f32[512,256]{1,0:T(8,128)}, u32[]{:S(2)}, u32[]{:S(2)}) collective-permute-start(f32[512,256]{1,0:T(8,128)} %collective-permute-done.40.refs_8_), channel_id=1, source_target_pairs={{0,4},{4,0},{8,12},{12,8},{16,20},{20,16},{24,28},{28,24},{1,5},{5... | collective-permute-start | bytes 1572872 | tf_op jit(solution)/shard_map/ppermute | solution.py:344
  282.1 10.1 %collective-permute-start.52 = (f32[512,256]{1,0:T(8,128)}, f32[512,256]{1,0:T(8,128)}, u32[]{:S(2)}, u32[]{:S(2)}) collective-permute-start(f32[512,256]{1,0:T(8,128)} %collective-permute-done.51.refs_12_), channel_id=1, source_target_pairs={{0,4},{4,0},{8,12},{12,8},{16,20},{20,16},{24,28},{28,24},{1,5},{5... | collective-permute-start | bytes 1572872 | tf_op jit(solution)/shard_map/ppermute | solution.py:344
  (30 other events, 212.5 us)

commit v3 on v2

--- a/solution.py
+++ b/solution.py
@@ -52,13 +52,21 @@
     return x * inv, inv
 
 
-def first_kernel(
-    feat_ref, proto_ref, lo_ref, hi_ref, cent_ref, base_ref, col_ref, tot_ref, soft_ref, acc, embed_ref
-):
+def two_terms(x):
+    high = x.astype(BF16)
+    return high, (x - high.astype(F32)).astype(BF16)
+
+
+def in_vmem():
+    return pl.BlockSpec(memory_space=pltpu.VMEM)
+
+
+def first_kernel(feat_ref, proto_ref, lo_ref, hi_ref, cent_ref, col_ref, tot_ref, soft_ref, *refs):
+    *base_refs, acc, embed_ref = refs
     i = pl.program_id(0)
     rows = feat_ref.shape[1]
     kt = proto_ref.shape[0]
-    rc = tile_of(rows, 256)
+    rc = base_refs[0].shape[1]
 
     @pl.when(i == 0)
     def _():
@@ -72,18 +80,16 @@
 
     cent_ref[...] = unit_of(proto_ref[...].astype(F32))[0].astype(BF16)
     for v in range(2):
-
-        def step(j, col):
-            r = pl.ds(pl.multiple_of(j * rc, rc), rc)
+        col = jnp.zeros((8, kt), F32)
+        for j in range(rows // rc):
+            r = slice(j * rc, (j + 1) * rc)
             s = lax.dot_general(embed_ref[v, r, :], cent_ref[...], NT, preferred_element_type=F32)
             e = jnp.exp2(s * SOFT)
             acc[v, r, :] += lane_fold(e)
             soft_ref[v, r, :] += jnp.dot(e.astype(BF16), cent_ref[...], preferred_element_type=F32)
             b = e * e
-            base_ref[0, v, r, :] = b.astype(BF16)
-            return col + sub_fold(b)
-
-        col = lax.fori_loop(0, rows // rc, step, jnp.zeros((8, kt), F32), unroll=True)
+            base_refs[v * (rows // rc) + j][i] = b.astype(BF16)
+            col = col + sub_fold(b)
         col_ref[v, pl.ds(i, 1), :] = jnp.sum(col, axis=0, keepdims=True)
 
     @pl.when(i == pl.num_programs(0) - 1)
@@ -97,152 +103,156 @@
     protos = prototypes.shape[0]
     kt = tile_of(protos, 1024)
     n = protos // kt
-    whole = lambda *s: pl.BlockSpec(s, lambda i: (0,) * len(s))
-    return pl.pallas_call(
+    rc = tile_of(rows, 256)
+    m = 2 * rows // rc
+    outs = pl.pallas_call(
         first_kernel,
         grid=(n,),
-        in_specs=[whole(2, rows, width), pl.BlockSpec((kt, width), lambda i: (i, 0))],
+        in_specs=[in_vmem(), pl.BlockSpec((kt, width), lambda i: (i, 0))],
         out_specs=[
-            whole(2, rows // 2, width),
-            whole(2, rows // 2, width),
+            in_vmem(),
+            in_vmem(),
             pl.BlockSpec((kt, width), lambda i: (i, 0)),
-            pl.BlockSpec((1, 2, rows, kt), lambda i: (i, 0, 0, 0)),
-            whole(2, n, kt),
-            whole(2, rows),
-            whole(2, rows, width),
-        ],
+            in_vmem(),
+            in_vmem(),
+            in_vmem(),
+        ]
+        + [in_vmem()] * m,
         out_shape=[
             jax.ShapeDtypeStruct((2, rows // 2, width), F32),
             jax.ShapeDtypeStruct((2, rows // 2, width), F32),
             jax.ShapeDtypeStruct((protos, width), BF16),
-            jax.ShapeDtypeStruct((n, 2, rows, kt), BF16),
             jax.ShapeDtypeStruct((2, n, kt), F32),
             jax.ShapeDtypeStruct((2, rows), F32),
             jax.ShapeDtypeStruct((2, rows, width), F32),
-        ],
+        ]
+        + [pltpu.VMEM((n, rc, kt), BF16)] * m,
         scratch_shapes=[pltpu.VMEM((2, rows, 128), F32), pltpu.VMEM((2, rows, width), BF16)],
-        compiler_params=params(48),
-        cost_estimate=cost(16 * rows * protos * width, 4 * rows * protos),
+        compiler_params=params(16),
+        cost_estimate=cost(16 * rows * protos * width, 0),
         name="first",
     )(features, prototypes)
-
-
-def row_kernel(base_ref, *refs):
-    *part_refs, out_ref, acc = refs
-    i = pl.program_id(0)
-    rows = base_ref.shape[2]
-    rc = 16
-
-    @pl.when(i == 0)
-    def _():
-        acc[...] = jnp.zeros_like(acc)
-
+    return outs[:6], outs[6:]
+
+
+def load_scales(part_refs, rows_ref, cols_ref, v):
+    n, kt = rows_ref.shape
+    half = kt // 2
+    for i in range(n):
+        c = 1.0 / sum(p[v, i : i + 1, :] for p in part_refs)
+        rows_ref[i : i + 1, :] = c
+        high, low = two_terms(c[:, half:])
+        cols_ref[i] = jnp.concatenate([high, low, jnp.zeros((126, half), BF16)], axis=0).T
+
+
+def block_sum(base_ref, rows_ref, cols_ref, acc):
+    n, rc, kt = base_ref.shape
+    half = kt // 2
+    total = jnp.dot(base_ref[0, :, half:], cols_ref[0], preferred_element_type=F32)
+    for i in range(1, n):
+        total = total + jnp.dot(base_ref[i, :, half:], cols_ref[i], preferred_element_type=F32)
+    acc[...] = total
+    step = 32
+    for j in range(0, rc, step):
+        r = slice(j, j + step)
+        part = acc[r]
+        for i in range(n):
+            part = part + lane_fold(base_ref[i, r, :half].astype(F32) * rows_ref[i : i + 1, :half])
+        acc[r] = part
+    return jnp.sum(acc[...].T, axis=0, keepdims=True)
+
+
+def row_kernel(m, *refs):
+    base_refs, part_refs = refs[:m], refs[m:-4]
+    out_ref, rows_ref, cols_ref, acc = refs[-4:]
+    rc = base_refs[0].shape[1]
     for v in range(2):
-        c = 1.0 / sum(p[v, pl.ds(i, 1), :] for p in part_refs)
-
-        def step(j, carry):
-            r = pl.ds(pl.multiple_of(j * rc, rc), rc)
-            acc[v, r, :] += lane_fold(base_ref[0, v, r, :].astype(F32) * c)
-            return carry
-
-        lax.fori_loop(0, rows // rc, step, 0, unroll=4)
-
-    @pl.when(i == pl.num_programs(0) - 1)
-    def _():
-        for v in range(2):
-            out_ref[v : v + 1, :] = jnp.sum(acc[v].T, axis=0, keepdims=True)
-
-
-def row_last_kernel(base_ref, cent_ref, *refs):
-    *part_refs, out_ref, code_ref, acc = refs
-    i = pl.program_id(0)
-    rows = base_ref.shape[2]
-    rc = tile_of(rows, 256)
-
-    @pl.when(i == 0)
-    def _():
-        acc[...] = jnp.zeros_like(acc)
-        code_ref[...] = jnp.zeros_like(code_ref)
-
+        load_scales(part_refs, rows_ref, cols_ref, v)
+        for j in range(m // 2):
+            sums = block_sum(base_refs[v * (m // 2) + j], rows_ref, cols_ref, acc)
+            out_ref[v : v + 1, j * rc : (j + 1) * rc] = sums
+
+
+def row_last_kernel(m, *refs):
+    base_refs, cent_ref, part_refs = refs[:m], refs[m], refs[m + 1 : -6]
+    out_ref, code_ref, rows_ref, cols_ref, acc, scaled = refs[-6:]
+    n, rc, kt = base_refs[0].shape
     for v in range(2):
-        c = 1.0 / sum(p[v, pl.ds(i, 1), :] for p in part_refs)
-
-        def step(j, carry):
-            r = pl.ds(pl.multiple_of(j * rc, rc), rc)
-            w = base_ref[0, v, r, :].astype(F32) * c
-            acc[v, r, :] += lane_fold(w)
-            code_ref[v, r, :] += jnp.dot(w.astype(BF16), cent_ref[...], preferred_element_type=F32)
-            return carry
-
-        lax.fori_loop(0, rows // rc, step, 0, unroll=True)
-
-    @pl.when(i == pl.num_programs(0) - 1)
-    def _():
-        for v in range(2):
-            out_ref[v : v + 1, :] = jnp.sum(acc[v].T, axis=0, keepdims=True)
+        load_scales(part_refs, rows_ref, cols_ref, v)
+        for i in range(n):
+            c = spread(rows_ref[i : i + 1, :])
+            c = jnp.concatenate([c] * (scaled.shape[2] // 128), axis=1)
+            scaled[i] = (cent_ref[i * kt : (i + 1) * kt, :].astype(F32) * c).astype(BF16)
+        for j in range(m // 2):
+            base_ref = base_refs[v * (m // 2) + j]
+            r = slice(j * rc, (j + 1) * rc)
+            out_ref[v : v + 1, r] = block_sum(base_ref, rows_ref, cols_ref, acc)
+            total = jnp.dot(base_ref[0], scaled[0], preferred_element_type=F32)
+            for i in range(1, n):
+                total = total + jnp.dot(base_ref[i], scaled[i], preferred_element_type=F32)
+            code_ref[v, r, :] = total
 
 
 def row_pass(base, parts, centers=None):
-    n, _, rows, kt = base.shape
-    whole = lambda *s: pl.BlockSpec(s, lambda i: (0,) * len(s))
-    in_specs = [pl.BlockSpec((1, 2, rows, kt), lambda i: (i, 0, 0, 0))]
-    out_specs = [whole(2, rows)]
+    m = len(base)
+    n, rc, kt = base[0].shape
+    rows = m // 2 * rc
     out_shape = [jax.ShapeDtypeStruct((2, rows), F32)]
-    args = [base]
+    args = list(base)
+    scratch = [
+        pltpu.VMEM((n, kt), F32),
+        pltpu.VMEM((n, kt // 2, 128), BF16),
+        pltpu.VMEM((rc, 128), F32),
+    ]
+    kernel = row_kernel
     if centers is not None:
         width = centers.shape[1]
-        in_specs.append(pl.BlockSpec((kt, width), lambda i: (i, 0)))
-        out_specs.append(whole(2, rows, width))
         out_shape.append(jax.ShapeDtypeStruct((2, rows, width), F32))
         args.append(centers)
+        scratch.append(pltpu.VMEM((n, kt, width), BF16))
+        kernel = row_last_kernel
     return pl.pallas_call(
-        row_kernel if centers is None else row_last_kernel,
-        grid=(n,),
-        in_specs=in_specs + [whole(2, n, kt)] * len(parts),
-        out_specs=out_specs,
+        lambda *refs: kernel(m, *refs),
+        in_specs=[in_vmem()] * (len(args) + len(parts)),
+        out_specs=[in_vmem()] * len(out_shape),
         out_shape=out_shape,
-        scratch_shapes=[pltpu.VMEM((2, rows, 128), F32)],
-        compiler_params=params(48),
-        cost_estimate=cost(0, 8 * n * rows * kt),
+        scratch_shapes=scratch,
+        compiler_params=params(16),
+        cost_estimate=cost(0, 4 * n * rows * kt),
         name="row_pass" if centers is None else "row_last",
     )(*args, *parts)
 
 
-def col_kernel(base_ref, total_ref, out_ref, scale):
-    i = pl.program_id(0)
-    rows, kt = base_ref.shape[2:]
-    rc = 16
-
-    @pl.when(i == 0)
-    def _():
-        for v in range(2):
-            scale[v] = spread(1.0 / total_ref[v : v + 1, :])
-
+def col_kernel(total_ref, *refs):
+    *base_refs, out_ref = refs
+    m = len(base_refs) // 2
+    n, rc, kt = base_refs[0].shape
     for v in range(2):
-
-        def step(j, col):
-            r = pl.ds(pl.multiple_of(j * rc, rc), rc)
-            w = jnp.concatenate([scale[v, r, :]] * (kt // 128), axis=1)
-            return col + sub_fold(base_ref[0, v, r, :].astype(F32) * w)
-
-        col = lax.fori_loop(0, rows // rc, step, jnp.zeros((8, kt), F32), unroll=4)
-        out_ref[v, pl.ds(i, 1), :] = jnp.sum(col, axis=0, keepdims=True)
+        high, low = two_terms(1.0 / total_ref[v : v + 1, :])
+        r = jnp.concatenate([high, low, jnp.zeros((14, m * rc), BF16)], axis=0)
+        for i in range(n):
+            total = jnp.zeros((16, kt), F32)
+            for j in range(m):
+                total = total + jnp.dot(
+                    r[:, j * rc : (j + 1) * rc],
+                    base_refs[v * m + j][i],
+                    preferred_element_type=F32,
+                )
+            out_ref[v, i : i + 1, :] = total[0:1] + total[1:2]
 
 
 def col_pass(base, total):
-    n, _, rows, kt = base.shape
-    whole = lambda *s: pl.BlockSpec(s, lambda i: (0,) * len(s))
+    n, rc, kt = base[0].shape
+    m = len(base)
     return pl.pallas_call(
         col_kernel,
-        grid=(n,),
-        in_specs=[pl.BlockSpec((1, 2, rows, kt), lambda i: (i, 0, 0, 0)), whole(2, rows)],
-        out_specs=whole(2, n, kt),
+        in_specs=[in_vmem()] * (m + 1),
+        out_specs=in_vmem(),
         out_shape=jax.ShapeDtypeStruct((2, n, kt), F32),
-        scratch_shapes=[pltpu.VMEM((2, rows, 128), F32)],
-        compiler_params=params(48),
-        cost_estimate=cost(0, 8 * n * rows * kt),
+        compiler_params=params(16),
+        cost_estimate=cost(0, 4 * n * m // 2 * rc * kt),
         name="col_pass",
-    )(base, total)
+    )(total, *base)
 
 
 def pack_kernel(*refs):
@@ -282,13 +292,13 @@
             o = 1 - v
             c = jnp.concatenate([scale[o]] * (rc // 128), axis=1)
             r = slice(j % 2 * rc, (j % 2 + 1) * rc)
-            codes = es[o] * es[o] * (GRAD / row_refs[m // 2 + j // 2][o : o + 1, r]) * c
-            g = (es[v] * (GRAD / row_refs[j // 2][v : v + 1, r]) - codes).astype(BF16)
+            codes = es[o] * es[o] * (GRAD / row_refs[j // 2][o : o + 1, r]) * c
+            g = (es[v] * (GRAD / row_refs[j // 2][2 + v : 3 + v, r]) - codes).astype(BF16)
             total = total + jnp.dot(g, embed[j, v], preferred_element_type=F32)
     out_ref[...] = total
 
 
-def grad_pass(centers, embeds, tot, row, col):
+def grad_pass(centers, embeds, row, col):
     protos, width = centers.shape
     m, _, rc, _ = embeds.shape
     kt = tile_of(protos, 512)
@@ -302,14 +312,14 @@
             whole(2, n, kt),
             whole(m, 2, rc, width),
         ]
-        + [whole(2, 2 * rc)] * m,
+        + [whole(4, 2 * rc)] * (m // 2),
         out_specs=pl.BlockSpec((kt, width), lambda i: (i, 0)),
         out_shape=jax.ShapeDtypeStruct((protos, width), F32),
         scratch_shapes=[pltpu.VMEM((2, kt, 128), F32)],
         compiler_params=params(48),
         cost_estimate=cost(8 * protos * m * rc * width, 4 * m * rc * width),
         name="grad_pass",
-    )(centers, col.reshape(2, n, kt), embeds, *tot, *row)
+    )(centers, col.reshape(2, n, kt), embeds, *row)
 
 
 def place_kernel(at_ref, *refs):
@@ -441,17 +451,20 @@
     chip, core = me // 2, me % 2
     share = protos // (nb // 2)
 
-    lo, hi, centers, base, col, tot, soft = first(features, prototypes)
+    (lo, hi, centers, col, tot, soft), base = first(features, prototypes)
     parts = col_exchange(col, nb)
-    tot = row_exchange(tot, npr)
-    tots = gather_rows(tot, nb)
     have, plan = [{0: lo}, {0: hi}], gather_plan(nb)
     have, parts = lax.optimization_barrier((have, parts))
     for step in range(ITERS - 1):
         if plan:
             send_pair(have, plan.pop(0), nb)
         (row,) = row_pass(base, parts)
-        col = col_pass(base, row_exchange(row, npr))
+        if step == 0:
+            both = row_exchange(jnp.concatenate([row, tot]), npr)
+            row, tot = both[:2], both[2:]
+        else:
+            row = row_exchange(row, npr)
+        col = col_pass(base, row)
         col, have = lax.optimization_barrier((col, have))
         parts = col_exchange(col, nb)
         have, parts = lax.optimization_barrier((have, parts))
@@ -460,7 +473,7 @@
     row, code = row_pass(base, parts, centers)
     row = row_exchange(row, npr)
     row, have = lax.optimization_barrier((row, have))
-    rows_all = gather_rows(row, nb)
+    rows_all = gather_rows(jnp.concatenate([row, tot]), nb)
     embeds = pack([have[h][k] for k in range(0, nb, 2) for h in range(2)])
     col = (1.0 / sum(parts)).reshape(2, protos)
     half = share // 2
@@ -468,7 +481,7 @@
 
     def grads(at):
         c = lax.dynamic_slice_in_dim(col, at, half, axis=1)
-        return grad_pass(cut(centers, at, half), embeds, tots, rows_all, c)
+        return grad_pass(cut(centers, at, half), embeds, rows_all, c)
 
     gf = [
         soft[v] * (GRAD / tot[v])[:, None] - code[1 - v] * (GRAD / row[1 - v])[:, None]

time: 299 us -> 284 us (0.950); the launches traced: 298 us -> 280 us
  Pallas kernels: 134 us -> 98.6 us
  local copies, waits for them, and re-layouts: 12.2 us -> 29.7 us
  starting transfers between devices: 57.3 us -> 49.9 us
  waiting for transfers between devices: 84.9 us -> 91.9 us
    pallas_call x6, Pallas kernels: 104 us -> 68.5 us  [the longest x3 35.2 us: row_pass(): pl.pallas_call(lambda *refs: kernel(m, *refs), in_specs=[in_vmem()] * (le...]
    unnamed x47 -> x79, local copies, waits for them, and re-layouts: 7.04 us -> 24.6 us
    ppermute x55 -> x50, starting transfers between devices: 57.3 us -> 49.9 us  [swap(): return lax.ppermute(x, axis, [(i, i ^ m) for i in range(n)])]
    ppermute x55 -> x50, waiting for transfers between devices: 84.9 us -> 91.9 us  [swap(): return lax.ppermute(x, axis, [(i, i ^ m) for i in range(n)])]
  transfers between devices with their start and end apart: 55 -> 50, of which waited for: 23 -> 28; matrix products, arithmetic and copies ran while one was open for 5% -> 5% of each run, Pallas kernels for 35% -> 24%
where the time goes in v3:
time: 284 us; the launch traced here: 280 us
  Pallas kernels  98.6 us (35%)
  waiting for transfers between devices  91.9 us (32%)
  starting transfers between devices  49.9 us (18%)
  local copies, waits for them, and re-layouts  29.7 us (10%)
  other arithmetic  8.68 us (3%)
    ppermute x50, waiting for transfers between devices, swap(): return lax.ppermute(x, axis, [(i, i ^ m) for i in range(n)])  91.9 us
    ppermute x50, starting transfers between devices, swap(): return lax.ppermute(x, axis, [(i, i ^ m) for i in range(n)])  49.9 us
    pallas_call x3, Pallas kernels, row_pass(): pl.pallas_call(lambda *refs: kernel(m, *refs), in_specs=[in_vmem()] * (le...  35.2 us
    unnamed x79, local copies, waits for them, and re-layouts  24.6 us
    pallas_call x1, Pallas kernels, first(): pl.pallas_call(first_kernel, grid=(n,), in_specs=[in_vmem(), pl.BlockSpec...  24.4 us
    pallas_call x2, Pallas kernels, grad_pass(): pl.pallas_call(grad_kernel, grid=(n,), in_specs=[pl.BlockSpec((kt, width)...  20.3 us
    pallas_call x2, Pallas kernels, col_pass(): pl.pallas_call(col_kernel, in_specs=[in_vmem()] * (m + 1), out_specs=in_v...  8.89 us
    pallas_call x2, Pallas kernels, place(): pl.pallas_call(place_kernel, in_specs=[pl.BlockSpec(memory_space=pltpu.SM...  7.82 us
  transfers between devices with their start and end apart: 50, of which 28 were waited for; matrix products, arithmetic and copies ran while one was open for 5% of the time, Pallas kernels for 24%

profile of v3, /device:TPU:0, one launch (start us, length us, event | category | flops | bytes accessed | tf_op | source)
XLA Modules:
  0.0 280.3 jit_solution(1087795770281293466)
XLA Ops:
  1.9 24.4 %first.1 = (f32[2,512,256]{2,1,0:T(8,128)S(1)}, f32[2,512,256]{2,1,0:T(8,128)S(1)}, bf16[8192,256]{1,0:T(8,128)(2,1)}, f32[2,8,1024]{2,1,0:T(8,128)S(1)}, f32[2,...) custom-call(bf16[2,1024,256]{2,1,0:T(8,128)(2,1)S(1)} %copy-done.27,, ...), custom_call_target="tpu_custom_call" | custom-call | flops 34359738368 | tf_op jit(solution)/shard_map/first/pallas_call | solution.py:108
  27.8 2.9 %collective-permute-start.1 = (f32[2,8,1024]{2,1,0:T(8,128)S(1)}, f32[2,8,1024]{2,1,0:T(8,128)S(1)}, u32[]{:S(2)}, u32[]{:S(2)}) collective-permute-start(f32[2,8,1024]{2,1,0:T(8,128)S(1)} %add.272.refs_8_), channel_id=1, source_target_pairs={{0,8},{4,12},{8,0},{12,4},{16,24},{20,28},{24,16},{28,20},{1,9},{5... | collective-permute-start | bytes 196616 | tf_op jit(solution)/shard_map/ppermute | solution.py:354
  33.1 1.9 collective-permute-done.2.refs_10_
  35.0 2.4 collective-permute-done.3.refs_11_
  38.3 7.5 %row_pass.2 = f32[2,1024]{1,0:T(2,128)S(1)} custom-call(bf16[8,256,1024]{2,1,0:T(8,128)(2,1)S(1)} %get-tuple-element.92.refs_0_, bf16[8,256,1024]{2,1,0:T(8,128)(2,1)S(1)} %get-tuple-element.93.refs_1_, bf16[8,256,1024]{2,1,0:T(8,128)(2,1)S(1)} %get-tuple-element.94.refs_2_, bf16[8,256,1024]{2,1,0:T(8,128)(2,1)S(1)} %get-tuple-element.95.refs_3_, ...), custom_call_target="tpu_custom_call" | custom-call | bytes 33554432 | tf_op jit(solution)/shard_map/row_pass/pallas_call | solution.py:214
  45.9 1.7 collective-permute-start.4
  47.6 2.1 collective-permute-done.4
  49.7 2.8 %collective-permute-start.5 = (f32[4,1024]{1,0:T(4,128)S(1)}, f32[4,1024]{1,0:T(4,128)S(1)}, u32[]{:S(2)}, u32[]{:S(2)}) collective-permute-start(f32[4,1024]{1,0:T(4,128)S(1)} %fusion.20), channel_id=1, source_target_pairs={{0,2},{1,3},{2,0},{3,1},{4,6},{5,7},{6,4},{7,5},{8,10},{9,11},{10,... | collective-permute-start | bytes 49160 | tf_op jit(solution)/shard_map/ppermute | solution.py:354
  52.5 1.9 collective-permute-done.5
  54.4 4.4 %col_pass.2 = f32[2,8,1024]{2,1,0:T(8,128)S(1)} custom-call(f32[2,1024]{1,0:T(2,128)S(1)} %get-tuple-element.211.total_ref, bf16[8,256,1024]{2,1,0:T(8,128)(2,1)S(1)} %get-tuple-element.92.refs_0_, bf16[8,256,1024]{2,1,0:T(8,128)(2,1)S(1)} %get-tuple-element.93.refs_1_, bf16[8,256,1024]{2,1,0:T(8,128)(2,1)S(1)} %get-tuple-element.94.refs_2_, ...), custom_call_target="tpu_custom_call" | custom-call | bytes 33554432 | tf_op jit(solution)/shard_map/col_pass/pallas_call | solution.py:247
  58.8 2.1 collective-permute-done.6.refs_2_
  63.2 2.3 collective-permute-start.11
  71.7 7.5 %row_pass.3 = f32[2,1024]{1,0:T(2,128)S(1)} custom-call(bf16[8,256,1024]{2,1,0:T(8,128)(2,1)S(1)} %get-tuple-element.92.refs_0_, bf16[8,256,1024]{2,1,0:T(8,128)(2,1)S(1)} %get-tuple-element.93.refs_1_, bf16[8,256,1024]{2,1,0:T(8,128)(2,1)S(1)} %get-tuple-element.94.refs_2_, bf16[8,256,1024]{2,1,0:T(8,128)(2,1)S(1)} %get-tuple-element.95.refs_3_, ...), custom_call_target="tpu_custom_call" | custom-call | bytes 33554432 | tf_op jit(solution)/shard_map/row_pass/pallas_call | solution.py:214
  80.9 2.1 collective-permute-done.12
  83.0 2.6 collective-permute-start.13
  85.5 2.0 collective-permute-done.13
  87.6 4.4 %col_pass.3 = f32[2,8,1024]{2,1,0:T(8,128)S(1)} custom-call(f32[2,1024]{1,0:T(2,128)S(1)} %add.277.total_ref, bf16[8,256,1024]{2,1,0:T(8,128)(2,1)S(1)} %get-tuple-element.92.refs_0_, bf16[8,256,1024]{2,1,0:T(8,128)(2,1)S(1)} %get-tuple-element.93.refs_1_, bf16[8,256,1024]{2,1,0:T(8,128)(2,1)S(1)} %get-tuple-element.94.refs_2_, ...), custom_call_target="tpu_custom_call" | custom-call | bytes 33554432 | tf_op jit(solution)/shard_map/col_pass/pallas_call | solution.py:247
  92.1 2.1 collective-permute-done.14.refs_4_
  99.1 1.9 collective-permute-start.19
  106.8 2.3 constant_dynamic-slice_fusion.9
  111.6 2.2 copy-done.1
  113.8 2.2 copy-done.3
  116.0 2.2 copy-done.5
  118.2 2.2 copy-done.7
  120.3 2.2 copy-done.9
  122.5 2.2 copy-done.11
  124.7 2.2 copy-done.13
  126.9 2.2 copy-done.15
  129.1 20.2 %row_last.1 = (f32[2,1024]{1,0:T(2,128)S(1)}, f32[2,1024,256]{2,1,0:T(8,128)S(1)}) custom-call(bf16[8,256,1024]{2,1,0:T(8,128)(2,1)S(1)} %copy-done.1, bf16[8,256,1024]{2,1,0:T(8,128)(2,1)S(1)} %copy-done.3, bf16[8,256,1024]{2,1,0:T(8,128)(2,1)S(1)} %copy-done.5, bf16[8,256,1024]{2,1,0:T(8,128)(2,1)S(1)} %copy-done.7, bf16[8,256,1024]{2,1,0:T(8,128)(2,1)S(1)} %copy-done.9, ...), custom_call_target="tpu_custom_call" | custom-call | bytes 33554432 | tf_op jit(solution)/shard_map/row_last/pallas_call | solution.py:214
  152.2 2.1 collective-permute-done.20
  154.3 2.5 collective-permute-start.21
  156.8 2.0 collective-permute-done.21
  160.5 1.9 collective-permute-start.26
  162.5 2.2 fusion.6
  166.3 1.9 pack.1.embed
  168.3 10.1 %grad_pass.3 = f32[1024,256]{1,0:T(8,128)S(1)} custom-call(bf16[1024,256]{1,0:T(8,128)(2,1)S(1)} %copy-done.36, f32[2,2,512]{2,1,0:T(2,128)S(1)} %reshape.73.col_ref, bf16[8,2,512,256]{3,2,1,0:T(8,128)(2,1)S(1)} %pack.1.embed, f32[4,1024]{1,0:T(4,128)S(1)} %pad_maximum_fusion.3.refs_0_, f32[4,1024]{1,0:T(4,128)S(1)} %collective-permute-done.24.refs_1_, ...), custom_call_target="tpu_custom_call" | custom-call | flops 8589934592 | bytes 4194304 | tf_op jit(solution)/shard_map/grad_pass/pallas_call | solution.py:307
  178.6 2.7 collective-permute-start.29
  182.2 10.2 %grad_pass.2 = f32[1024,256]{1,0:T(8,128)S(1)} custom-call(bf16[1024,256]{1,0:T(8,128)(2,1)S(1)} %copy-done.35, f32[2,2,512]{2,1,0:T(2,128)S(1)} %reshape.72.col_ref, bf16[8,2,512,256]{3,2,1,0:T(8,128)(2,1)S(1)} %pack.1.embed, f32[4,1024]{1,0:T(4,128)S(1)} %pad_maximum_fusion.3.refs_0_, f32[4,1024]{1,0:T(4,128)S(1)} %collective-permute-done.24.refs_1_, ...), custom_call_target="tpu_custom_call" | custom-call | flops 8589934592 | bytes 4194304 | tf_op jit(solution)/shard_map/grad_pass/pallas_call | solution.py:307
  194.0 6.8 %collective-permute-done.30 = f32[512,256]{1,0:T(8,128)S(1)} collective-permute-done((f32[512,256]{1,0:T(8,128)S(1)}, f32[512,256]{1,0:T(8,128)S(1)}, u32[]{:S(2)}, u32[]{:S(2)}) %collective-permute-start.30) | collective-permute-done | bytes 524320 | tf_op jit(solution)/shard_map/ppermute | solution.py:354
  206.1 2.9 %collective-permute-start.33 = (f32[256,256]{1,0:T(8,128)S(1)}, f32[256,256]{1,0:T(8,128)S(1)}, u32[]{:S(2)}, u32[]{:S(2)}) collective-permute-start(f32[256,256]{1,0:T(8,128)S(1)} %fusion.17.refs_0_), channel_id=1, source_target_pairs={{0,2},{1,3},{2,0},{3,1},{4,6},{5,7},{6,4},{7,5},{8,10},{9,11},{10,... | collective-permute-start | bytes 786440 | tf_op jit(solution)/shard_map/ppermute | solution.py:354
  209.1 11.9 %collective-permute-done.34 = f32[256,256]{1,0:T(8,128)S(1)} collective-permute-done((f32[256,256]{1,0:T(8,128)S(1)}, f32[256,256]{1,0:T(8,128)S(1)}, u32[]{:S(2)}, u32[]{:S(2)}) %collective-permute-start.34) | collective-permute-done | bytes 262176 | tf_op jit(solution)/shard_map/ppermute | solution.py:354
  221.1 5.3 %collective-permute-done.33.refs_2_ = f32[256,256]{1,0:T(8,128)S(1)} collective-permute-done((f32[256,256]{1,0:T(8,128)S(1)}, f32[256,256]{1,0:T(8,128)S(1)}, u32[]{:S(2)}, u32[]{:S(2)}) %collective-permute-start.33) | collective-permute-done | bytes 262176 | tf_op jit(solution)/shard_map/ppermute | solution.py:354
  229.9 15.9 %collective-permute-done.38 = f32[512,256]{1,0:T(8,128)S(1)} collective-permute-done((f32[512,256]{1,0:T(8,128)S(1)}, f32[512,256]{1,0:T(8,128)S(1)}, u32[]{:S(2)}, u32[]{:S(2)}) %collective-permute-start.38) | collective-permute-done | bytes 524320 | tf_op jit(solution)/shard_map/ppermute | solution.py:354
  248.2 10.7 %collective-permute-done.46.refs_12_ = f32[512,256]{1,0:T(8,128)} collective-permute-done((f32[512,256]{1,0:T(8,128)S(1)}, f32[512,256]{1,0:T(8,128)}, u32[]{:S(2)}, u32[]{:S(2)}) %collective-permute-start.46) | collective-permute-done | bytes 524320 | tf_op jit(solution)/shard_map/ppermute | solution.py:354
  258.8 2.7 collective-permute-done.48.refs_14_
  265.0 5.8 %collective-permute-done.39 = f32[512,256]{1,0:T(8,128)} collective-permute-done((f32[512,256]{1,0:T(8,128)S(1)}, f32[512,256]{1,0:T(8,128)}, u32[]{:S(2)}, u32[]{:S(2)}) %collective-permute-start.39) | collective-permute-done | bytes 524320 | tf_op jit(solution)/shard_map/ppermute | solution.py:354
  272.2 1.9 place.2
  274.2 5.9 %place.3 = f32[8192,256]{1,0:T(8,128)} custom-call(s32[16]{0:T(128)S(1)} %stack.103.at_ref, f32[512,256]{1,0:T(8,128)S(1)} %get-tuple-element.174.refs_0_, f32[512,256]{1,0:T(8,128)S(1)} %copy-done.32, f32[512,256]{1,0:T(8,128)S(1)} %get-tuple-element.175.refs_2_, f32[512,256]{1,0:T(8,128)S(1)} %copy-done.34, ...), custom_call_target="tpu_custom_call" | custom-call | tf_op jit(solution)/shard_map/place/pallas_call | solution.py:341
  (188 shorter events, 54.2 us)
Async XLA Ops:
  26.4 1.4 collective-permute-start
  27.8 5.3 %collective-permute-start.1 = (f32[2,8,1024]{2,1,0:T(8,128)S(1)}, f32[2,8,1024]{2,1,0:T(8,128)S(1)}, u32[]{:S(2)}, u32[]{:S(2)}) collective-permute-start(f32[2,8,1024]{2,1,0:T(8,128)S(1)} %add.272.refs_8_), channel_id=1, source_target_pairs={{0,8},{4,12},{8,0},{12,4},{16,24},{20,28},{24,16},{28,20},{1,9},{5... | collective-permute-start | bytes 196616 | tf_op jit(solution)/shard_map/ppermute | solution.py:354
  30.7 4.3 %collective-permute-start.2 = (f32[2,8,1024]{2,1,0:T(8,128)S(1)}, f32[2,8,1024]{2,1,0:T(8,128)S(1)}, u32[]{:S(2)}, u32[]{:S(2)}) collective-permute-start(f32[2,8,1024]{2,1,0:T(8,128)S(1)} %add.272.refs_8_), channel_id=1, source_target_pairs={{0,16},{4,20},{8,24},{12,28},{16,0},{20,4},{24,8},{28,12},{1,17},{... | collective-permute-start | bytes 196616 | tf_op jit(solution)/shard_map/ppermute | solution.py:354
  32.2 5.2 %collective-permute-start.3 = (f32[2,8,1024]{2,1,0:T(8,128)S(1)}, f32[2,8,1024]{2,1,0:T(8,128)S(1)}, u32[]{:S(2)}, u32[]{:S(2)}) collective-permute-start(f32[2,8,1024]{2,1,0:T(8,128)S(1)} %add.272.refs_8_), channel_id=1, source_target_pairs={{0,24},{4,28},{8,16},{12,20},{16,8},{20,12},{24,0},{28,4},{1,25},{... | collective-permute-start | bytes 196616 | tf_op jit(solution)/shard_map/ppermute | solution.py:354
  37.4 23.5 %collective-permute-start.6 = (f32[2,512,256]{2,1,0:T(8,128)S(1)}, f32[2,512,256]{2,1,0:T(8,128)S(1)}, u32[]{:S(2)}, u32[]{:S(2)}) collective-permute-start(f32[2,512,256]{2,1,0:T(8,128)S(1)} %get-tuple-element.141.refs_0_), channel_id=1, source_target_pairs={{0,8},{4,12},{8,0},{12,4},{16,24},{20,28},{24,16},{28,20},{1,9},{5... | collective-permute-start | bytes 3145736 | tf_op jit(solution)/shard_map/ppermute | solution.py:354
  37.9 23.3 %collective-permute-start.7 = (f32[2,512,256]{2,1,0:T(8,128)S(1)}, f32[2,512,256]{2,1,0:T(8,128)S(1)}, u32[]{:S(2)}, u32[]{:S(2)}) collective-permute-start(f32[2,512,256]{2,1,0:T(8,128)S(1)} %get-tuple-element.142.refs_1_), channel_id=1, source_target_pairs={{0,16},{4,20},{8,24},{12,28},{16,0},{20,4},{24,8},{28,12},{1,17},{... | collective-permute-start | bytes 3145736 | tf_op jit(solution)/shard_map/ppermute | solution.py:354
  45.9 3.8 %collective-permute-start.4 = (f32[4,1024]{1,0:T(4,128)S(1)}, f32[4,1024]{1,0:T(4,128)S(1)}, u32[]{:S(2)}, u32[]{:S(2)}) collective-permute-start(f32[4,1024]{1,0:T(4,128)S(1)} %pad_maximum_fusion.2), channel_id=1, source_target_pairs={{0,1},{1,0},{2,3},{3,2},{4,5},{5,4},{6,7},{7,6},{8,9},{9,8},{10,11... | collective-permute-start | bytes 49160 | tf_op jit(solution)/shard_map/ppermute | solution.py:354
  49.7 4.7 %collective-permute-start.5 = (f32[4,1024]{1,0:T(4,128)S(1)}, f32[4,1024]{1,0:T(4,128)S(1)}, u32[]{:S(2)}, u32[]{:S(2)}) collective-permute-start(f32[4,1024]{1,0:T(4,128)S(1)} %fusion.20), channel_id=1, source_target_pairs={{0,2},{1,3},{2,0},{3,1},{4,6},{5,7},{6,4},{7,5},{8,10},{9,11},{10,... | collective-permute-start | bytes 49160 | tf_op jit(solution)/shard_map/ppermute | solution.py:354
  62.5 5.0 %collective-permute-start.10 = (f32[2,8,1024]{2,1,0:T(8,128)S(1)}, f32[2,8,1024]{2,1,0:T(8,128)S(1)}, u32[]{:S(2)}, u32[]{:S(2)}) collective-permute-start(f32[2,8,1024]{2,1,0:T(8,128)S(1)} %add.275.refs_8_), channel_id=1, source_target_pairs={{0,16},{4,20},{8,24},{12,28},{16,0},{20,4},{24,8},{28,12},{1,17},{... | collective-permute-start | bytes 196616 | tf_op jit(solution)/shard_map/ppermute | solution.py:354
  63.2 5.8 %collective-permute-start.11 = (f32[2,8,1024]{2,1,0:T(8,128)S(1)}, f32[2,8,1024]{2,1,0:T(8,128)S(1)}, u32[]{:S(2)}, u32[]{:S(2)}) collective-permute-start(f32[2,8,1024]{2,1,0:T(8,128)S(1)} %add.275.refs_8_), channel_id=1, source_target_pairs={{0,24},{4,28},{8,16},{12,20},{16,8},{20,12},{24,0},{28,4},{1,25},{... | collective-permute-start | bytes 196616 | tf_op jit(solution)/shard_map/ppermute | solution.py:354
  65.4 4.3 %collective-permute-start.9 = (f32[2,8,1024]{2,1,0:T(8,128)S(1)}, f32[2,8,1024]{2,1,0:T(8,128)S(1)}, u32[]{:S(2)}, u32[]{:S(2)}) collective-permute-start(f32[2,8,1024]{2,1,0:T(8,128)S(1)} %add.275.refs_8_), channel_id=1, source_target_pairs={{0,8},{4,12},{8,0},{12,4},{16,24},{20,28},{24,16},{28,20},{1,9},{5... | collective-permute-start | bytes 196616 | tf_op jit(solution)/shard_map/ppermute | solution.py:354
  69.7 24.5 %collective-permute-start.14 = (f32[2,512,256]{2,1,0:T(8,128)S(1)}, f32[2,512,256]{2,1,0:T(8,128)S(1)}, u32[]{:S(2)}, u32[]{:S(2)}) collective-permute-start(f32[2,512,256]{2,1,0:T(8,128)S(1)} %get-tuple-element.141.refs_0_), channel_id=1, source_target_pairs={{0,16},{4,20},{8,24},{12,28},{16,0},{20,4},{24,8},{28,12},{1,17},{... | collective-permute-start | bytes 3145736 | tf_op jit(solution)/shard_map/ppermute | solution.py:354
  70.4 24.8 %collective-permute-start.15 = (f32[2,512,256]{2,1,0:T(8,128)S(1)}, f32[2,512,256]{2,1,0:T(8,128)S(1)}, u32[]{:S(2)}, u32[]{:S(2)}) collective-permute-start(f32[2,512,256]{2,1,0:T(8,128)S(1)} %get-tuple-element.142.refs_1_), channel_id=1, source_target_pairs={{0,8},{4,12},{8,0},{12,4},{16,24},{20,28},{24,16},{28,20},{1,9},{5... | collective-permute-start | bytes 3145736 | tf_op jit(solution)/shard_map/ppermute | solution.py:354
  79.2 3.7 %collective-permute-start.12 = (f32[2,1024]{1,0:T(2,128)S(1)}, f32[2,1024]{1,0:T(2,128)S(1)}, u32[]{:S(2)}, u32[]{:S(2)}) collective-permute-start(f32[2,1024]{1,0:T(2,128)S(1)} %row_pass.3), channel_id=1, source_target_pairs={{0,1},{1,0},{2,3},{3,2},{4,5},{5,4},{6,7},{7,6},{8,9},{9,8},{10,11... | collective-permute-start | bytes 24584 | tf_op jit(solution)/shard_map/ppermute | solution.py:354
  83.0 4.5 %collective-permute-start.13 = (f32[2,1024]{1,0:T(2,128)S(1)}, f32[2,1024]{1,0:T(2,128)S(1)}, u32[]{:S(2)}, u32[]{:S(2)}) collective-permute-start(f32[2,1024]{1,0:T(2,128)S(1)} %add.276), channel_id=1, source_target_pairs={{0,2},{1,3},{2,0},{3,1},{4,6},{5,7},{6,4},{7,5},{8,10},{9,11},{10,... | collective-permute-start | bytes 24584 | tf_op jit(solution)/shard_map/ppermute | solution.py:354
  97.5 4.6 %collective-permute-start.17 = (f32[2,8,1024]{2,1,0:T(8,128)S(1)}, f32[2,8,1024]{2,1,0:T(8,128)S(1)}, u32[]{:S(2)}, u32[]{:S(2)}) collective-permute-start(f32[2,8,1024]{2,1,0:T(8,128)S(1)} %add.278.refs_9_), channel_id=1, source_target_pairs={{0,8},{4,12},{8,0},{12,4},{16,24},{20,28},{24,16},{28,20},{1,9},{5... | collective-permute-start | bytes 196616 | tf_op jit(solution)/shard_map/ppermute | solution.py:354
  98.2 5.0 %collective-permute-start.18 = (f32[2,8,1024]{2,1,0:T(8,128)S(1)}, f32[2,8,1024]{2,1,0:T(8,128)S(1)}, u32[]{:S(2)}, u32[]{:S(2)}) collective-permute-start(f32[2,8,1024]{2,1,0:T(8,128)S(1)} %add.278.refs_9_), channel_id=1, source_target_pairs={{0,16},{4,20},{8,24},{12,28},{16,0},{20,4},{24,8},{28,12},{1,17},{... | collective-permute-start | bytes 196616 | tf_op jit(solution)/shard_map/ppermute | solution.py:354
  99.1 5.2 %collective-permute-start.19 = (f32[2,8,1024]{2,1,0:T(8,128)S(1)}, f32[2,8,1024]{2,1,0:T(8,128)S(1)}, u32[]{:S(2)}, u32[]{:S(2)}) collective-permute-start(f32[2,8,1024]{2,1,0:T(8,128)S(1)} %add.278.refs_9_), channel_id=1, source_target_pairs={{0,24},{4,28},{8,16},{12,20},{16,8},{20,12},{24,0},{28,4},{1,25},{... | collective-permute-start | bytes 196616 | tf_op jit(solution)/shard_map/ppermute | solution.py:354
  104.3 54.6 %collective-permute-start.22 = (f32[2,512,256]{2,1,0:T(8,128)}, f32[2,512,256]{2,1,0:T(8,128)}, u32[]{:S(2)}, u32[]{:S(2)}) collective-permute-start(f32[2,512,256]{2,1,0:T(8,128)} %copy-done.19), channel_id=1, source_target_pairs={{0,16},{4,20},{8,24},{12,28},{16,0},{20,4},{24,8},{28,12},{1,17},{... | collective-permute-start | bytes 3145736 | tf_op jit(solution)/shard_map/ppermute | solution.py:354
  105.4 53.5 %collective-permute-start.23 = (f32[2,512,256]{2,1,0:T(8,128)}, f32[2,512,256]{2,1,0:T(8,128)}, u32[]{:S(2)}, u32[]{:S(2)}) collective-permute-start(f32[2,512,256]{2,1,0:T(8,128)} %copy-done.21), channel_id=1, source_target_pairs={{0,8},{4,12},{8,0},{12,4},{16,24},{20,28},{24,16},{28,20},{1,9},{5... | collective-permute-start | bytes 3145736 | tf_op jit(solution)/shard_map/ppermute | solution.py:354
  150.6 3.7 %collective-permute-start.20 = (f32[2,1024]{1,0:T(2,128)S(1)}, f32[2,1024]{1,0:T(2,128)S(1)}, u32[]{:S(2)}, u32[]{:S(2)}) collective-permute-start(f32[2,1024]{1,0:T(2,128)S(1)} %get-tuple-element.134), channel_id=1, source_target_pairs={{0,1},{1,0},{2,3},{3,2},{4,5},{5,4},{6,7},{7,6},{8,9},{9,8},{10,11... | collective-permute-start | bytes 24584 | tf_op jit(solution)/shard_map/ppermute | solution.py:354
  154.3 4.5 %collective-permute-start.21 = (f32[2,1024]{1,0:T(2,128)S(1)}, f32[2,1024]{1,0:T(2,128)S(1)}, u32[]{:S(2)}, u32[]{:S(2)}) collective-permute-start(f32[2,1024]{1,0:T(2,128)S(1)} %add.282), channel_id=1, source_target_pairs={{0,2},{1,3},{2,0},{3,1},{4,6},{5,7},{6,4},{7,5},{8,10},{9,11},{10,... | collective-permute-start | bytes 24584 | tf_op jit(solution)/shard_map/ppermute | solution.py:354
  158.9 9.4 %collective-permute-start.24 = (f32[4,1024]{1,0:T(4,128)S(1)}, f32[4,1024]{1,0:T(4,128)S(1)}, u32[]{:S(2)}, u32[]{:S(2)}) collective-permute-start(f32[4,1024]{1,0:T(4,128)S(1)} %pad_maximum_fusion.3.refs_0_), channel_id=1, source_target_pairs={{0,8},{4,12},{8,0},{12,4},{16,24},{20,28},{24,16},{28,20},{1,9},{5... | collective-permute-start | bytes 49160 | tf_op jit(solution)/shard_map/ppermute | solution.py:354
  159.6 8.7 %collective-permute-start.25 = (f32[4,1024]{1,0:T(4,128)S(1)}, f32[4,1024]{1,0:T(4,128)S(1)}, u32[]{:S(2)}, u32[]{:S(2)}) collective-permute-start(f32[4,1024]{1,0:T(4,128)S(1)} %pad_maximum_fusion.3.refs_0_), channel_id=1, source_target_pairs={{0,16},{4,20},{8,24},{12,28},{16,0},{20,4},{24,8},{28,12},{1,17},{... | collective-permute-start | bytes 49160 | tf_op jit(solution)/shard_map/ppermute | solution.py:354
  160.5 7.8 %collective-permute-start.26 = (f32[4,1024]{1,0:T(4,128)S(1)}, f32[4,1024]{1,0:T(4,128)S(1)}, u32[]{:S(2)}, u32[]{:S(2)}) collective-permute-start(f32[4,1024]{1,0:T(4,128)S(1)} %pad_maximum_fusion.3.refs_0_), channel_id=1, source_target_pairs={{0,24},{4,28},{8,16},{12,20},{16,8},{20,12},{24,0},{28,4},{1,25},{... | collective-permute-start | bytes 49160 | tf_op jit(solution)/shard_map/ppermute | solution.py:354
  164.8 13.7 %collective-permute-start.27 = (f32[512,256]{1,0:T(8,128)S(1)}, f32[512,256]{1,0:T(8,128)S(1)}, u32[]{:S(2)}, u32[]{:S(2)}) collective-permute-start(f32[512,256]{1,0:T(8,128)S(1)} %get-tuple-element.196), channel_id=1, source_target_pairs={{0,1},{1,0},{2,3},{3,2},{4,5},{5,4},{6,7},{7,6},{8,9},{9,8},{10,11... | collective-permute-start | bytes 1572872 | tf_op jit(solution)/shard_map/ppermute | solution.py:354
  178.4 22.4 %collective-permute-start.28 = (f32[1024,256]{1,0:T(8,128)S(1)}, f32[1024,256]{1,0:T(8,128)S(1)}, u32[]{:S(2)}, u32[]{:S(2)}) collective-permute-start(f32[1024,256]{1,0:T(8,128)S(1)} %grad_pass.3), channel_id=1, source_target_pairs={{0,4},{4,0},{8,12},{12,8},{16,20},{20,16},{24,28},{28,24},{1,5},{5... | collective-permute-start | bytes 3145736 | tf_op jit(solution)/shard_map/ppermute | solution.py:354
  178.6 15.4 %collective-permute-start.29 = (f32[256,256]{1,0:T(8,128)S(1)}, f32[256,256]{1,0:T(8,128)S(1)}, u32[]{:S(2)}, u32[]{:S(2)}) collective-permute-start(f32[256,256]{1,0:T(8,128)S(1)} %get-tuple-element.204), channel_id=1, source_target_pairs={{0,2},{1,3},{2,0},{3,1},{4,6},{5,7},{6,4},{7,5},{8,10},{9,11},{10,... | collective-permute-start | bytes 786440 | tf_op jit(solution)/shard_map/ppermute | solution.py:354
  181.4 19.5 %collective-permute-start.30 = (f32[512,256]{1,0:T(8,128)S(1)}, f32[512,256]{1,0:T(8,128)S(1)}, u32[]{:S(2)}, u32[]{:S(2)}) collective-permute-start(f32[512,256]{1,0:T(8,128)S(1)} %get-tuple-element.194), channel_id=1, source_target_pairs={{0,1},{1,0},{2,3},{3,2},{4,5},{5,4},{6,7},{7,6},{8,9},{9,8},{10,11... | collective-permute-start | bytes 1572872 | tf_op jit(solution)/shard_map/ppermute | solution.py:354
  201.0 20.1 %collective-permute-start.34 = (f32[256,256]{1,0:T(8,128)S(1)}, f32[256,256]{1,0:T(8,128)S(1)}, u32[]{:S(2)}, u32[]{:S(2)}) collective-permute-start(f32[256,256]{1,0:T(8,128)S(1)} %get-tuple-element.202), channel_id=1, source_target_pairs={{0,2},{1,3},{2,0},{3,1},{4,6},{5,7},{6,4},{7,5},{8,10},{9,11},{10,... | collective-permute-start | bytes 786440 | tf_op jit(solution)/shard_map/ppermute | solution.py:354
  204.1 22.4 %collective-permute-start.31 = (f32[512,256]{1,0:T(8,128)S(1)}, f32[512,256]{1,0:T(8,128)S(1)}, u32[]{:S(2)}, u32[]{:S(2)}) collective-permute-start(f32[512,256]{1,0:T(8,128)S(1)} %get-tuple-element.174.refs_0_), channel_id=1, source_target_pairs={{0,8},{4,12},{8,0},{12,4},{16,24},{20,28},{24,16},{28,20},{1,9},{5... | collective-permute-start | bytes 1572872 | tf_op jit(solution)/shard_map/ppermute | solution.py:354
  204.8 21.6 %collective-permute-start.32 = (f32[512,256]{1,0:T(8,128)S(1)}, f32[512,256]{1,0:T(8,128)}, u32[]{:S(2)}, u32[]{:S(2)}) collective-permute-start(f32[512,256]{1,0:T(8,128)S(1)} %get-tuple-element.175.refs_2_), channel_id=1, source_target_pairs={{0,16},{4,20},{8,24},{12,28},{16,0},{20,4},{24,8},{28,12},{1,17},{... | collective-permute-start | bytes 1572872 | tf_op jit(solution)/shard_map/ppermute | solution.py:354
  206.1 20.3 %collective-permute-start.33 = (f32[256,256]{1,0:T(8,128)S(1)}, f32[256,256]{1,0:T(8,128)S(1)}, u32[]{:S(2)}, u32[]{:S(2)}) collective-permute-start(f32[256,256]{1,0:T(8,128)S(1)} %fusion.17.refs_0_), channel_id=1, source_target_pairs={{0,2},{1,3},{2,0},{3,1},{4,6},{5,7},{6,4},{7,5},{8,10},{9,11},{10,... | collective-permute-start | bytes 786440 | tf_op jit(solution)/shard_map/ppermute | solution.py:354
  226.5 19.3 %collective-permute-start.38 = (f32[512,256]{1,0:T(8,128)S(1)}, f32[512,256]{1,0:T(8,128)S(1)}, u32[]{:S(2)}, u32[]{:S(2)}) collective-permute-start(f32[512,256]{1,0:T(8,128)S(1)} %pad_maximum_fusion), channel_id=1, source_target_pairs={{0,1},{1,0},{2,3},{3,2},{4,5},{5,4},{6,7},{7,6},{8,9},{9,8},{10,11... | collective-permute-start | bytes 1572872 | tf_op jit(solution)/shard_map/ppermute | solution.py:354
  226.6 19.3 %collective-permute-start.35 = (f32[512,256]{1,0:T(8,128)S(1)}, f32[512,256]{1,0:T(8,128)}, u32[]{:S(2)}, u32[]{:S(2)}) collective-permute-start(f32[512,256]{1,0:T(8,128)S(1)} %get-tuple-element.174.refs_0_), channel_id=1, source_target_pairs={{0,16},{4,20},{8,24},{12,28},{16,0},{20,4},{24,8},{28,12},{1,17},{... | collective-permute-start | bytes 1572872 | tf_op jit(solution)/shard_map/ppermute | solution.py:354
  227.6 18.3 %collective-permute-start.36 = (f32[512,256]{1,0:T(8,128)S(1)}, f32[512,256]{1,0:T(8,128)}, u32[]{:S(2)}, u32[]{:S(2)}) collective-permute-start(f32[512,256]{1,0:T(8,128)S(1)} %get-tuple-element.175.refs_2_), channel_id=1, source_target_pairs={{0,8},{4,12},{8,0},{12,4},{16,24},{20,28},{24,16},{28,20},{1,9},{5... | collective-permute-start | bytes 1572872 | tf_op jit(solution)/shard_map/ppermute | solution.py:354
  228.6 17.2 %collective-permute-start.37 = (f32[256,256]{1,0:T(8,128)S(1)}, f32[256,256]{1,0:T(8,128)S(1)}, u32[]{:S(2)}, u32[]{:S(2)}) collective-permute-start(f32[256,256]{1,0:T(8,128)S(1)} %fusion.14.refs_4_), channel_id=1, source_target_pairs={{0,2},{1,3},{2,0},{3,1},{4,6},{5,7},{6,4},{7,5},{8,10},{9,11},{10,... | collective-permute-start | bytes 786440 | tf_op jit(solution)/shard_map/ppermute | solution.py:354
  245.9 13.0 %collective-permute-start.46 = (f32[512,256]{1,0:T(8,128)S(1)}, f32[512,256]{1,0:T(8,128)}, u32[]{:S(2)}, u32[]{:S(2)}) collective-permute-start(f32[512,256]{1,0:T(8,128)S(1)} %collective-permute-done.31.refs_4_), channel_id=1, source_target_pairs={{0,16},{4,20},{8,24},{12,28},{16,0},{20,4},{24,8},{28,12},{1,17},{... | collective-permute-start | bytes 1572872 | tf_op jit(solution)/shard_map/ppermute | solution.py:354
  246.9 16.8 %collective-permute-start.42 = (f32[512,256]{1,0:T(8,128)S(1)}, f32[512,256]{1,0:T(8,128)S(1)}, u32[]{:S(2)}, u32[]{:S(2)}) collective-permute-start(f32[512,256]{1,0:T(8,128)S(1)} %collective-permute-done.31.refs_4_), channel_id=1, source_target_pairs={{0,4},{4,0},{8,12},{12,8},{16,20},{20,16},{24,28},{28,24},{1,5},{5... | collective-permute-start | bytes 1572872 | tf_op jit(solution)/shard_map/ppermute | solution.py:354
  246.9 14.7 %collective-permute-start.48 = (f32[512,256]{1,0:T(8,128)}, f32[512,256]{1,0:T(8,128)}, u32[]{:S(2)}, u32[]{:S(2)}) collective-permute-start(f32[512,256]{1,0:T(8,128)} %collective-permute-done.32.refs_10_), channel_id=1, source_target_pairs={{0,8},{4,12},{8,0},{12,4},{16,24},{20,28},{24,16},{28,20},{1,9},{5... | collective-permute-start | bytes 1572872 | tf_op jit(solution)/shard_map/ppermute | solution.py:354
  247.6 14.0 %collective-permute-start.40 = (f32[512,256]{1,0:T(8,128)S(1)}, f32[512,256]{1,0:T(8,128)S(1)}, u32[]{:S(2)}, u32[]{:S(2)}) collective-permute-start(f32[512,256]{1,0:T(8,128)S(1)} %get-tuple-element.174.refs_0_), channel_id=1, source_target_pairs={{0,4},{4,0},{8,12},{12,8},{16,20},{20,16},{24,28},{28,24},{1,5},{5... | collective-permute-start | bytes 1572872 | tf_op jit(solution)/shard_map/ppermute | solution.py:354
  247.8 15.0 %collective-permute-start.41 = (f32[512,256]{1,0:T(8,128)S(1)}, f32[512,256]{1,0:T(8,128)S(1)}, u32[]{:S(2)}, u32[]{:S(2)}) collective-permute-start(f32[512,256]{1,0:T(8,128)S(1)} %get-tuple-element.175.refs_2_), channel_id=1, source_target_pairs={{0,4},{4,0},{8,12},{12,8},{16,20},{20,16},{24,28},{28,24},{1,5},{5... | collective-permute-start | bytes 1572872 | tf_op jit(solution)/shard_map/ppermute | solution.py:354
  258.8 12.0 %collective-permute-start.39 = (f32[512,256]{1,0:T(8,128)S(1)}, f32[512,256]{1,0:T(8,128)}, u32[]{:S(2)}, u32[]{:S(2)}) collective-permute-start(f32[512,256]{1,0:T(8,128)S(1)} %pad_maximum_fusion.1), channel_id=1, source_target_pairs={{0,1},{1,0},{2,3},{3,2},{4,5},{5,4},{6,7},{7,6},{8,9},{9,8},{10,11... | collective-permute-start | bytes 1572872 | tf_op jit(solution)/shard_map/ppermute | solution.py:354
  261.6 12.6 %collective-permute-start.45 = (f32[512,256]{1,0:T(8,128)}, f32[512,256]{1,0:T(8,128)}, u32[]{:S(2)}, u32[]{:S(2)}) collective-permute-start(f32[512,256]{1,0:T(8,128)} %collective-permute-done.32.refs_10_), channel_id=1, source_target_pairs={{0,4},{4,0},{8,12},{12,8},{16,20},{20,16},{24,28},{28,24},{1,5},{5... | collective-permute-start | bytes 1572872 | tf_op jit(solution)/shard_map/ppermute | solution.py:354
  262.4 11.8 %collective-permute-start.43 = (f32[512,256]{1,0:T(8,128)}, f32[512,256]{1,0:T(8,128)}, u32[]{:S(2)}, u32[]{:S(2)}) collective-permute-start(f32[512,256]{1,0:T(8,128)} %collective-permute-done.36.refs_6_), channel_id=1, source_target_pairs={{0,4},{4,0},{8,12},{12,8},{16,20},{20,16},{24,28},{28,24},{1,5},{5... | collective-permute-start | bytes 1572872 | tf_op jit(solution)/shard_map/ppermute | solution.py:354
  263.7 10.5 %collective-permute-start.44 = (f32[512,256]{1,0:T(8,128)}, f32[512,256]{1,0:T(8,128)}, u32[]{:S(2)}, u32[]{:S(2)}) collective-permute-start(f32[512,256]{1,0:T(8,128)} %collective-permute-done.35.refs_8_), channel_id=1, source_target_pairs={{0,4},{4,0},{8,12},{12,8},{16,20},{20,16},{24,28},{28,24},{1,5},{5... | collective-permute-start | bytes 1572872 | tf_op jit(solution)/shard_map/ppermute | solution.py:354
  264.5 9.7 %collective-permute-start.47 = (f32[512,256]{1,0:T(8,128)}, f32[512,256]{1,0:T(8,128)}, u32[]{:S(2)}, u32[]{:S(2)}) collective-permute-start(f32[512,256]{1,0:T(8,128)} %collective-permute-done.46.refs_12_), channel_id=1, source_target_pairs={{0,4},{4,0},{8,12},{12,8},{16,20},{20,16},{24,28},{28,24},{1,5},{5... | collective-permute-start | bytes 1572872 | tf_op jit(solution)/shard_map/ppermute | solution.py:354
  270.8 3.4 %collective-permute-start.49 = (f32[512,256]{1,0:T(8,128)}, f32[512,256]{1,0:T(8,128)}, u32[]{:S(2)}, u32[]{:S(2)}) collective-permute-start(f32[512,256]{1,0:T(8,128)} %collective-permute-done.48.refs_14_), channel_id=1, source_target_pairs={{0,4},{4,0},{8,12},{12,8},{16,20},{20,16},{24,28},{28,24},{1,5},{5... | collective-permute-start | bytes 1572872 | tf_op jit(solution)/shard_map/ppermute | solution.py:354
  (41 other events, 659.9 us)

commit v4 on v3

--- a/solution.py
+++ b/solution.py
@@ -57,12 +57,16 @@
     return high, (x - high.astype(F32)).astype(BF16)
 
 
+def in_hbm(x):
+    return pltpu.with_memory_space_constraint(x, pltpu.HBM)
+
+
 def in_vmem():
     return pl.BlockSpec(memory_space=pltpu.VMEM)
 
 
 def first_kernel(feat_ref, proto_ref, lo_ref, hi_ref, cent_ref, col_ref, tot_ref, soft_ref, *refs):
-    *base_refs, acc, embed_ref = refs
+    kept_ref, *base_refs, acc, embed_ref, sems = refs
     i = pl.program_id(0)
     rows = feat_ref.shape[1]
     kt = proto_ref.shape[0]
@@ -92,8 +96,17 @@
             col = col + sub_fold(b)
         col_ref[v, pl.ds(i, 1), :] = jnp.sum(col, axis=0, keepdims=True)
 
+    def keep(tile, j):
+        return pltpu.make_async_copy(base_refs[j].at[tile], kept_ref.at[j, tile], sems.at[tile, j])
+
+    for j in range(len(base_refs)):
+        keep(i, j).start()
+
     @pl.when(i == pl.num_programs(0) - 1)
     def _():
+        for tile in range(sems.shape[0]):
+            for j in range(len(base_refs)):
+                keep(tile, j).wait()
         for v in range(2):
             tot_ref[v : v + 1, :] = jnp.sum(acc[v].T, axis=0, keepdims=True)
 
@@ -116,6 +129,7 @@
             in_vmem(),
             in_vmem(),
             in_vmem(),
+            pl.BlockSpec(memory_space=pl.ANY),
         ]
         + [in_vmem()] * m,
         out_shape=[
@@ -125,14 +139,19 @@
             jax.ShapeDtypeStruct((2, n, kt), F32),
             jax.ShapeDtypeStruct((2, rows), F32),
             jax.ShapeDtypeStruct((2, rows, width), F32),
+            pltpu.HBM((m, n, rc, kt), BF16),
         ]
         + [pltpu.VMEM((n, rc, kt), BF16)] * m,
-        scratch_shapes=[pltpu.VMEM((2, rows, 128), F32), pltpu.VMEM((2, rows, width), BF16)],
+        scratch_shapes=[
+            pltpu.VMEM((2, rows, 128), F32),
+            pltpu.VMEM((2, rows, width), BF16),
+            pltpu.SemaphoreType.DMA((n, m)),
+        ],
         compiler_params=params(16),
         cost_estimate=cost(16 * rows * protos * width, 0),
         name="first",
     )(features, prototypes)
-    return outs[:6], outs[6:]
+    return outs[:7], outs[7:]
 
 
 def load_scales(part_refs, rows_ref, cols_ref, v):
@@ -173,54 +192,103 @@
             out_ref[v : v + 1, j * rc : (j + 1) * rc] = sums
 
 
-def row_last_kernel(m, *refs):
-    base_refs, cent_ref, part_refs = refs[:m], refs[m], refs[m + 1 : -6]
-    out_ref, code_ref, rows_ref, cols_ref, acc, scaled = refs[-6:]
-    n, rc, kt = base_refs[0].shape
-    for v in range(2):
-        load_scales(part_refs, rows_ref, cols_ref, v)
-        for i in range(n):
-            c = spread(rows_ref[i : i + 1, :])
-            c = jnp.concatenate([c] * (scaled.shape[2] // 128), axis=1)
-            scaled[i] = (cent_ref[i * kt : (i + 1) * kt, :].astype(F32) * c).astype(BF16)
-        for j in range(m // 2):
-            base_ref = base_refs[v * (m // 2) + j]
-            r = slice(j * rc, (j + 1) * rc)
-            out_ref[v : v + 1, r] = block_sum(base_ref, rows_ref, cols_ref, acc)
-            total = jnp.dot(base_ref[0], scaled[0], preferred_element_type=F32)
-            for i in range(1, n):
-                total = total + jnp.dot(base_ref[i], scaled[i], preferred_element_type=F32)
-            code_ref[v, r, :] = total
-
-
-def row_pass(base, parts, centers=None):
+def row_pass(base, parts):
     m = len(base)
     n, rc, kt = base[0].shape
     rows = m // 2 * rc
-    out_shape = [jax.ShapeDtypeStruct((2, rows), F32)]
-    args = list(base)
-    scratch = [
-        pltpu.VMEM((n, kt), F32),
-        pltpu.VMEM((n, kt // 2, 128), BF16),
-        pltpu.VMEM((rc, 128), F32),
-    ]
-    kernel = row_kernel
-    if centers is not None:
-        width = centers.shape[1]
-        out_shape.append(jax.ShapeDtypeStruct((2, rows, width), F32))
-        args.append(centers)
-        scratch.append(pltpu.VMEM((n, kt, width), BF16))
-        kernel = row_last_kernel
     return pl.pallas_call(
-        lambda *refs: kernel(m, *refs),
-        in_specs=[in_vmem()] * (len(args) + len(parts)),
-        out_specs=[in_vmem()] * len(out_shape),
-        out_shape=out_shape,
-        scratch_shapes=scratch,
+        lambda *refs: row_kernel(m, *refs),
+        in_specs=[in_vmem()] * (m + len(parts)),
+        out_specs=in_vmem(),
+        out_shape=jax.ShapeDtypeStruct((2, rows), F32),
+        scratch_shapes=[
+            pltpu.VMEM((n, kt), F32),
+            pltpu.VMEM((n, kt // 2, 128), BF16),
+            pltpu.VMEM((rc, 128), F32),
+        ],
         compiler_params=params(16),
         cost_estimate=cost(0, 4 * n * rows * kt),
-        name="row_pass" if centers is None else "row_last",
-    )(*args, *parts)
+        name="row_pass",
+    )(*base, *parts)
+
+
+def row_last_kernel(base_ref, *refs):
+    *part_refs, out_ref, acc = refs
+    m, _, rc, kt = base_ref.shape
+    half = kt // 2
+    i = pl.program_id(0)
+
+    @pl.when(i == 0)
+    def _():
+        acc[...] = jnp.zeros_like(acc)
+
+    for v in range(2):
+        c = 1.0 / sum(p[v, pl.ds(i, 1), :] for p in part_refs)
+        high, low = two_terms(c[:, half:])
+        cols = jnp.concatenate([high, low, jnp.zeros((126, half), BF16)], axis=0).T
+        for j in range(m // 2):
+            k = v * (m // 2) + j
+            total = jnp.dot(base_ref[k, 0, :, half:], cols, preferred_element_type=F32)
+            total = total + lane_fold(base_ref[k, 0, :, :half].astype(F32) * c[:, :half])
+            acc[v, j * rc : (j + 1) * rc, :] += total
+
+    @pl.when(i == pl.num_programs(0) - 1)
+    def _():
+        for v in range(2):
+            out_ref[v : v + 1, :] = jnp.sum(acc[v].T, axis=0, keepdims=True)
+
+
+def row_last(kept, parts):
+    m, n, rc, kt = kept.shape
+    rows = m // 2 * rc
+    return pl.pallas_call(
+        row_last_kernel,
+        grid=(n,),
+        in_specs=[pl.BlockSpec((m, 1, rc, kt), lambda i: (0, i, 0, 0))] + [in_vmem()] * len(parts),
+        out_specs=in_vmem(),
+        out_shape=jax.ShapeDtypeStruct((2, rows), F32),
+        scratch_shapes=[pltpu.VMEM((2, rows, 128), F32)],
+        compiler_params=params(16),
+        cost_estimate=cost(0, 4 * n * rows * kt),
+        name="row_last",
+    )(in_hbm(kept), *parts)
+
+
+def code_kernel(v, cent_ref, base_ref, *refs):
+    *part_refs, out_ref = refs
+    m, _, rc, _ = base_ref.shape
+    i = pl.program_id(0)
+
+    @pl.when(i == 0)
+    def _():
+        out_ref[...] = jnp.zeros_like(out_ref)
+
+    c = spread(1.0 / sum(p[v, pl.ds(i, 1), :] for p in part_refs))
+    c = jnp.concatenate([c] * (cent_ref.shape[1] // 128), axis=1)
+    scaled = (cent_ref[...].astype(F32) * c).astype(BF16)
+    for j in range(m):
+        r = slice(j * rc, (j + 1) * rc)
+        out_ref[r, :] += jnp.dot(base_ref[j, 0], scaled, preferred_element_type=F32)
+
+
+def code_pass(kept, centers, parts, v):
+    m, n, rc, kt = kept.shape
+    m //= 2
+    width = centers.shape[1]
+    return pl.pallas_call(
+        lambda *refs: code_kernel(v, *refs),
+        grid=(n,),
+        in_specs=[
+            pl.BlockSpec((kt, width), lambda i: (i, 0)),
+            pl.BlockSpec((m, 1, rc, kt), lambda i: (v, i, 0, 0)),
+        ]
+        + [in_vmem()] * len(parts),
+        out_specs=in_vmem(),
+        out_shape=jax.ShapeDtypeStruct((m * rc, width), F32),
+        compiler_params=params(16),
+        cost_estimate=cost(2 * n * m * rc * kt * width, 0),
+        name="code_pass",
+    )(in_hbm(centers), in_hbm(kept), *parts)
 
 
 def col_kernel(total_ref, *refs):
@@ -270,7 +338,7 @@
         in_specs=[pl.BlockSpec((1, rc, width), lambda v: (v, 0, 0))] * m,
         out_specs=pl.BlockSpec((m, 1, rc, width), lambda v: (0, v, 0, 0)),
         out_shape=jax.ShapeDtypeStruct((m, 2, rc, width), BF16),
-        compiler_params=params(32),
+        compiler_params=params(16),
         cost_estimate=cost(0, 12 * m * rc * width),
         name="pack",
     )(*parts)
@@ -309,14 +377,14 @@
         grid=(n,),
         in_specs=[
             pl.BlockSpec((kt, width), lambda i: (i, 0)),
-            whole(2, n, kt),
-            whole(m, 2, rc, width),
+            in_vmem(),
+            in_vmem(),
         ]
-        + [whole(4, 2 * rc)] * (m // 2),
+        + [in_vmem()] * (m // 2),
         out_specs=pl.BlockSpec((kt, width), lambda i: (i, 0)),
         out_shape=jax.ShapeDtypeStruct((protos, width), F32),
         scratch_shapes=[pltpu.VMEM((2, kt, 128), F32)],
-        compiler_params=params(48),
+        compiler_params=params(16),
         cost_estimate=cost(8 * protos * m * rc * width, 4 * m * rc * width),
         name="grad_pass",
     )(centers, col.reshape(2, n, kt), embeds, *row)
@@ -345,7 +413,7 @@
         out_specs=pl.BlockSpec(memory_space=pl.ANY),
         out_shape=jax.ShapeDtypeStruct((size, pieces[0].shape[1]), F32),
         scratch_shapes=[pltpu.SemaphoreType.DMA((m,))],
-        compiler_params=params(24),
+        compiler_params=params(16),
         name="place",
     )(jnp.stack(at).astype(jnp.int32), *pieces)
 
@@ -401,47 +469,8 @@
     return lax.dynamic_slice_in_dim(x, at, size, axis=0)
 
 
-def halve_over_proto(x, n, m=1):
-    size = x.shape[0] // 2
-    side = (lax.axis_index("proto") // m) % 2
-    return cut(x, side * size, size), swap(cut(x, (1 - side) * size, size), "proto", n, m)
-
-
-def home(i, n, size):
-    at = 0 * i
-    for m in bits_of(n):
-        size //= 2
-        at = at + (i // m) % 2 * size
-    return at
-
-
-def spread_out(pieces, n):
-    bits = bits_of(n)[::-1]
-    keys = [0, bits[0]]
-    size = pieces[0].shape[0]
-    x = jnp.concatenate(pieces, axis=0)
-    for m in bits[1:-1]:
-        x = jnp.concatenate([x, swap(x, "proto", n, m)], axis=0)
-        keys = keys + [k ^ m for k in keys]
-    y = swap(x, "proto", n, bits[-1])
-    found = {}
-    for j, k in enumerate(keys):
-        found[k] = x[j * size : (j + 1) * size]
-        found[k ^ bits[-1]] = y[j * size : (j + 1) * size]
-    return found
-
-
-def bits_of(n):
-    return [2**j for j in range(n.bit_length()) if 2**j < n]
-
-
-def shard_back(pair, given, n):
-    x = pair[0] + pair[1]
-    for m in bits_of(n)[2:]:
-        a, b = halve_over_proto(x, n, m)
-        x = a + b
-    at = home(lax.axis_index("proto"), n, given.shape[0])
-    return norm_back(x, cut(given, at, x.shape[0]))
+def tie(*xs):
+    return lax.optimization_barrier(xs)
 
 
 def per_device(nb, npr, features, prototypes):
@@ -451,14 +480,14 @@
     chip, core = me // 2, me % 2
     share = protos // (nb // 2)
 
-    (lo, hi, centers, col, tot, soft), base = first(features, prototypes)
+    (lo, hi, centers, col, tot, soft, kept), base = first(features, prototypes)
     parts = col_exchange(col, nb)
     have, plan = [{0: lo}, {0: hi}], gather_plan(nb)
     have, parts = lax.optimization_barrier((have, parts))
     for step in range(ITERS - 1):
         if plan:
             send_pair(have, plan.pop(0), nb)
-        (row,) = row_pass(base, parts)
+        row = row_pass(base, parts)
         if step == 0:
             both = row_exchange(jnp.concatenate([row, tot]), npr)
             row, tot = both[:2], both[2:]
@@ -470,9 +499,9 @@
         have, parts = lax.optimization_barrier((have, parts))
     for pair in plan:
         send_pair(have, pair, nb)
-    row, code = row_pass(base, parts, centers)
-    row = row_exchange(row, npr)
-    row, have = lax.optimization_barrier((row, have))
+    row = row_exchange(row_last(kept, parts), npr)
+    code = [code_pass(kept, centers, parts, v) for v in range(2)]
+    row, have, centers, code, parts = tie(row, have, centers, code, parts)
     rows_all = gather_rows(jnp.concatenate([row, tot]), nb)
     embeds = pack([have[h][k] for k in range(0, nb, 2) for h in range(2)])
     col = (1.0 / sum(parts)).reshape(2, protos)
@@ -480,52 +509,87 @@
     quarter = half // 2
 
     def grads(at):
-        c = lax.dynamic_slice_in_dim(col, at, half, axis=1)
-        return grad_pass(cut(centers, at, half), embeds, rows_all, c)
-
-    gf = [
-        soft[v] * (GRAD / tot[v])[:, None] - code[1 - v] * (GRAD / row[1 - v])[:, None]
-        for v in range(2)
-    ]
-    pair = halve_over_proto(gf[0], npr, 1)
-    theirs = grads(chip * share + (1 - core) * half)
-    theirs, pair, late = lax.optimization_barrier((theirs, pair, gf[1]))
-    theirs = swap(theirs, "batch", nb, 1)
-    pair = halve_over_proto(pair[0] + pair[1], npr, 2)
-    pair_late = halve_over_proto(late, npr, 1)
-    mine = grads(chip * share + core * half)
-    mine, theirs, pair, pair_late = lax.optimization_barrier((mine, theirs, pair, pair_late))
-    grad = norm_back(mine + theirs, cut(prototypes, chip * share + core * half, half))
-
-    have, plan = [{0: grad[:quarter]}, {0: grad[quarter:]}], gather_plan(nb)
-    last = bits_of(npr)[-1]
-    send_pair(have, plan.pop(0), nb)
-    shard = shard_back(pair, features[0], npr)
-    near = swap(shard, "proto", npr, last)
-    late = halve_over_proto(pair_late[0] + pair_late[1], npr, 2)
-    have, near, late = lax.optimization_barrier((have, near, late))
-    send_pair(have, plan.pop(0), nb)
-    shards = [spread_out([shard, near], npr), shard_back(late, features[1], npr)]
-    near = swap(shards[1], "proto", npr, last)
-    have, near, first_view = lax.optimization_barrier((have, near, shards[0]))
-    for p in plan:
-        send_pair(have, p, nb)
-    shards = [first_view, spread_out([shards[1], near], npr)]
-    idx = lax.axis_index("proto")
+        c = lax.dynamic_slice_in_dim(col, at, quarter, axis=1)
+        return grad_pass(cut(centers, at, quarter), embeds, rows_all, c)
+
+    h = rows // 2
+    d = []
+    for v in range(2):
+        part = soft[v] * (GRAD / tot[v])[:, None] - code[1 - v] * (GRAD / row[1 - v])[:, None]
+        d += [part[:h], part[h:]]
+    line = npr == 4
+    if not line:
+        d = [row_exchange(x, npr) for x in d]
+
+    def hop(x, pairs):
+        return lax.ppermute(x, "proto", pairs) if line else jnp.zeros_like(x)
+
+    def inwards(x):
+        return hop(x, [(0, 1), (3, 2)])
+
+    def across(x):
+        return hop(x, [(1, 2), (2, 1)])
+
+    def outwards(x):
+        return hop(x, [(1, 0), (2, 3)])
+
+    mine_at = chip * share + core * half
+    their_at = chip * share + (1 - core) * half
+    plan = gather_plan(nb)
+
+    def send(hs, k, m):
+        got[hs][k ^ m] = swap(got[hs][k], "batch", nb, m)
+
+    a0 = inwards(d[0])
+    theirs = swap(grads(their_at), "batch", nb, 1)
+    mine = grads(mine_at)
+    mine, theirs, a0, d, features, prototypes = tie(mine, theirs, a0, d, features, prototypes)
+
+    got = [{0: norm_back(mine + theirs, cut(prototypes, mine_at, quarter))}, {}]
+    send(0, *plan[0][0])
+    s0 = d[0] + a0
+    a1, b0 = inwards(d[1]), across(s0)
+    theirs = swap(grads(their_at + quarter), "batch", nb, 1)
+    mine = grads(mine_at + quarter)
+    mine, theirs, a1, b0, got, d = tie(mine, theirs, a1, b0, got, d)
+
+    got[1][0] = norm_back(mine + theirs, cut(prototypes, mine_at + quarter, quarter))
+    send(1, *plan[0][1])
+    send(1, *plan[1][1])
+    t0, s1 = s0 + b0, d[1] + a1
+    a2, b1, c0 = inwards(d[2]), across(s1), outwards(t0)
+    a2, b1, c0, got, d = tie(a2, b1, c0, got, d)
+
+    send(0, *plan[1][0])
+    for pair in plan[2:]:
+        for hs in range(2):
+            send(hs, *pair[hs])
+    early = [(0, 0), (1, 0), (0, plan[0][0][1]), (1, plan[0][1][1])]
+    near = {(hs, k): swap(got[hs][k], "batch", nb, 1) for hs, k in early}
+    t1, s2 = s1 + b1, d[2] + a2
+    a3, b2, c1 = inwards(d[3]), across(s2), outwards(t1)
+    a3, b2, c1, got, near = tie(a3, b2, c1, got, near)
+
+    t2, s3 = s2 + b2, d[3] + a3
+    b3, c2 = across(s3), outwards(t2)
     out, where = [], []
-    for v in range(2):
-        for k, x in shards[v].items():
-            out.append(x)
-            where.append(home(idx ^ k, npr, rows) + v * rows)
-    grad_features = place(out, where, 2 * rows).reshape(2, rows, width)
-
-    out, where = [], []
-    for k in have[0]:
-        for h in range(2):
-            at = (chip ^ (k // 2)) * share + h * quarter
-            out += [have[h][k], swap(have[h][k], "batch", nb, 1)]
+    for k in got[0]:
+        for hs in range(2):
+            at = (chip ^ (k // 2)) * share + hs * quarter
+            other = near[hs, k] if (hs, k) in near else swap(got[hs][k], "batch", nb, 1)
+            out += [got[hs][k], other]
             where += [at + core * half, at + (1 - core) * half]
-    return grad_features, place(out, where, protos)
+    out, b3, c2 = tie(out, b3, c2)
+    t3 = s3 + b3
+    c3 = outwards(t3)
+    grad_prototypes = place(out, where, protos)
+    grad_prototypes, c3 = tie(grad_prototypes, c3)
+
+    z = lax.axis_index("proto")
+    ends = jnp.logical_and(line, jnp.logical_or(z == 0, z == 3))
+    chunks = [jnp.where(ends, c, t) for t, c in ((t0, c0), (t1, c1), (t2, c2), (t3, c3))]
+    grad_embed = jnp.concatenate(chunks).reshape(2, rows, width)
+    return norm_back(grad_embed, features), grad_prototypes
 
 
 def solution(mesh):

time: 284 us -> 308 us (1.085)
  starting transfers between devices: 49.9 us -> 71.6 us
  local copies, waits for them, and re-layouts: 29.7 us -> 10.1 us
  Pallas kernels: 98.6 us -> 117 us
  other arithmetic: 8.68 us -> 23 us
  waiting for transfers between devices: 91.9 us -> 80.3 us
    ppermute x50 -> x43, waiting for transfers between devices: 91.9 us -> 45.3 us  [swap(): return lax.ppermute(x, axis, [(i, i ^ m) for i in range(n)])]
    ppermute x0 -> x12, waiting for transfers between devices: none -> 35 us  [hop(): return lax.ppermute(x, 'proto', pairs) if line else jnp.zeros_like(x)]
    ppermute x0 -> x12, starting transfers between devices: none -> 28.1 us  [hop(): return lax.ppermute(x, 'proto', pairs) if line else jnp.zeros_like(x)]
    pallas_call x3 -> x5, Pallas kernels: 35.2 us -> 52.6 us  [the longest x2 23.5 us: code_pass(): pl.pallas_call(lambda *refs: code_kernel(v, *refs), grid=(n,), in_specs=[...]
    unnamed x79 -> x69, local copies, waits for them, and re-layouts: 24.6 us -> 8.41 us
    mul x0 -> x1, other arithmetic: none -> 11.5 us  [norm_back(): unit * jnp.sum(unit * grad, axis=-1, keepdims=True)]
    ppermute x50 -> x43, starting transfers between devices: 49.9 us -> 43.5 us  [swap(): return lax.ppermute(x, axis, [(i, i ^ m) for i in range(n)])]
    add x2 -> x8, other arithmetic: 0.14 us -> 3.83 us  [the longest x2 2.22 us: per_device(): t2, s3 = (s2 + b2, d[3] + a3)]
  transfers between devices with their start and end apart: 50 -> 55, of which waited for: 28 -> 29; matrix products, arithmetic and copies ran while one was open for 5% -> 3% of each run, Pallas kernels for 24% -> 30%
where the time goes in v4:
time: 308 us; the launch traced here: 304 us
  Pallas kernels  117 us (38%)
  waiting for transfers between devices  80.3 us (26%)
  starting transfers between devices  71.6 us (23%)
  other arithmetic  23 us (7%)
  local copies, waits for them, and re-layouts  10.1 us (3%)
    ppermute x43, waiting for transfers between devices, swap(): return lax.ppermute(x, axis, [(i, i ^ m) for i in range(n)])  45.3 us
    ppermute x43, starting transfers between devices, swap(): return lax.ppermute(x, axis, [(i, i ^ m) for i in range(n)])  43.5 us
    ppermute x12, waiting for transfers between devices, hop(): return lax.ppermute(x, 'proto', pairs) if line else jnp.zeros_like(x)  35 us
    ppermute x12, starting transfers between devices, hop(): return lax.ppermute(x, 'proto', pairs) if line else jnp.zeros_like(x)  28.1 us
    pallas_call x1, Pallas kernels, first(): pl.pallas_call(first_kernel, grid=(n,), in_specs=[in_vmem(), pl.BlockSpec...  26.4 us
    pallas_call x2, Pallas kernels, code_pass(): pl.pallas_call(lambda *refs: code_kernel(v, *refs), grid=(n,), in_specs=[...  23.5 us
    pallas_call x4, Pallas kernels, grad_pass(): pl.pallas_call(grad_kernel, grid=(n,), in_specs=[pl.BlockSpec((kt, width)...  22.1 us
    pallas_call x2, Pallas kernels, row_pass(): pl.pallas_call(lambda *refs: row_kernel(m, *refs), in_specs=[in_vmem()] *...  15 us
  transfers between devices with their start and end apart: 55, of which 29 were waited for; matrix products, arithmetic and copies ran while one was open for 3% of the time, Pallas kernels for 30%

profile of v4, /device:TPU:0, one launch (start us, length us, event | category | flops | bytes accessed | tf_op | source)
XLA Modules:
  0.0 304.1 jit_solution(15620955366555008159)
XLA Ops:
  1.9 26.4 %first.1 = (f32[2,512,256]{2,1,0:T(8,128)S(1)}, f32[2,512,256]{2,1,0:T(8,128)S(1)}, bf16[8192,256]{1,0:T(8,128)(2,1)}, f32[2,8,1024]{2,1,0:T(8,128)S(1)}, f32[2,...) custom-call(bf16[2,1024,256]{2,1,0:T(8,128)(2,1)S(1)} %copy-done, ...), custom_call_target="tpu_custom_call" | custom-call | flops 34359738368 | tf_op jit(solution)/shard_map/first/pallas_call | solution.py:121
  29.7 3.9 %collective-permute-start.3 = (f32[2,8,1024]{2,1,0:T(8,128)S(1)}, f32[2,8,1024]{2,1,0:T(8,128)S(1)}, u32[]{:S(2)}, u32[]{:S(2)}) collective-permute-start(f32[2,8,1024]{2,1,0:T(8,128)S(1)} %add.189.refs_8_), channel_id=1, source_target_pairs={{0,24},{4,28},{8,16},{12,20},{16,8},{20,12},{24,0},{28,4},{1,25},{... | collective-permute-start | bytes 196616 | tf_op jit(solution)/shard_map/ppermute | solution.py:422
  34.2 1.8 collective-permute-done.3.refs_11_
  36.0 1.9 collective-permute-done.2.refs_10_
  40.4 7.5 %row_pass.2 = f32[2,1024]{1,0:T(2,128)S(1)} custom-call(bf16[8,256,1024]{2,1,0:T(8,128)(2,1)S(1)} %get-tuple-element.133.refs_0_, bf16[8,256,1024]{2,1,0:T(8,128)(2,1)S(1)} %get-tuple-element.134.refs_1_, bf16[8,256,1024]{2,1,0:T(8,128)(2,1)S(1)} %get-tuple-element.135.refs_2_, bf16[8,256,1024]{2,1,0:T(8,128)(2,1)S(1)} %get-tuple-element.136.refs_3_, ...), custom_call_target="tpu_custom_call" | custom-call | bytes 33554432 | tf_op jit(solution)/shard_map/row_pass/pallas_call | solution.py:199
  48.0 1.6 collective-permute-start.4
  49.6 2.2 collective-permute-done.4
  51.8 2.7 collective-permute-start.5
  54.4 2.0 collective-permute-done.5
  56.5 4.4 %col_pass.2 = f32[2,8,1024]{2,1,0:T(8,128)S(1)} custom-call(f32[2,1024]{1,0:T(2,128)S(1)} %get-tuple-element.284.total_ref, bf16[8,256,1024]{2,1,0:T(8,128)(2,1)S(1)} %get-tuple-element.133.refs_0_, bf16[8,256,1024]{2,1,0:T(8,128)(2,1)S(1)} %get-tuple-element.134.refs_1_, bf16[8,256,1024]{2,1,0:T(8,128)(2,1)S(1)} %get-tuple-element.135.refs_2_, ...), custom_call_target="tpu_custom_call" | custom-call | bytes 33554432 | tf_op jit(solution)/shard_map/col_pass/pallas_call | solution.py:315
  60.9 1.5 collective-permute-done.6.refs_2_
  65.2 1.6 collective-permute-start.11
  67.0 2.1 collective-permute-start.9
  73.8 7.5 %row_pass.3 = f32[2,1024]{1,0:T(2,128)S(1)} custom-call(bf16[8,256,1024]{2,1,0:T(8,128)(2,1)S(1)} %get-tuple-element.133.refs_0_, bf16[8,256,1024]{2,1,0:T(8,128)(2,1)S(1)} %get-tuple-element.134.refs_1_, bf16[8,256,1024]{2,1,0:T(8,128)(2,1)S(1)} %get-tuple-element.135.refs_2_, bf16[8,256,1024]{2,1,0:T(8,128)(2,1)S(1)} %get-tuple-element.136.refs_3_, ...), custom_call_target="tpu_custom_call" | custom-call | bytes 33554432 | tf_op jit(solution)/shard_map/row_pass/pallas_call | solution.py:199
  81.3 1.6 collective-permute-start.12
  82.9 2.1 collective-permute-done.12
  85.0 2.6 collective-permute-start.13
  87.6 2.0 collective-permute-done.13
  89.6 4.4 %col_pass.3 = f32[2,8,1024]{2,1,0:T(8,128)S(1)} custom-call(f32[2,1024]{1,0:T(2,128)S(1)} %add.194.total_ref, bf16[8,256,1024]{2,1,0:T(8,128)(2,1)S(1)} %get-tuple-element.133.refs_0_, bf16[8,256,1024]{2,1,0:T(8,128)(2,1)S(1)} %get-tuple-element.134.refs_1_, bf16[8,256,1024]{2,1,0:T(8,128)(2,1)S(1)} %get-tuple-element.135.refs_2_, ...), custom_call_target="tpu_custom_call" | custom-call | bytes 33554432 | tf_op jit(solution)/shard_map/col_pass/pallas_call | solution.py:315
  94.0 2.7 collective-permute-done.14.refs_4_
  100.0 1.6 collective-permute-start.19
  103.6 1.7 collective-permute-done.19.refs_3_.refs_5_
  108.6 14.0 %row_last.1 = f32[2,1024]{1,0:T(2,128)S(1)} custom-call(bf16[8,8,256,1024]{3,2,1,0:T(8,128)(2,1)} %get-tuple-element.132.base_ref.refs_1_, f32[2,8,1024]{2,1,0:T(8,128)S(1)} %add.195.refs_0_.refs_2_, f32[2,8,1024]{2,1,0:T(8,128)S(1)} %collective-permute-done.17.refs_1_.refs_3_, f32[2,8,1024]{2,1,0:T(8,128)S(1)} %collective-permute-done.18.refs_2_.refs_4_, ...), custom_call_target="tpu_custom_call" | custom-call | bytes 33554432 | tf_op jit(solution)/shard_map/row_last/pallas_call | solution.py:244
  122.7 1.6 collective-permute-start.20
  124.3 11.8 %code_pass.3 = f32[1024,256]{1,0:T(8,128)S(1)} custom-call(bf16[8192,256]{1,0:T(8,128)(2,1)} %get-tuple-element.182.refs_0_, bf16[8,8,256,1024]{3,2,1,0:T(8,128)(2,1)} %get-tuple-element.132.base_ref.refs_1_, f32[2,8,1024]{2,1,0:T(8,128)S(1)} %add.195.refs_0_.refs_2_, f32[2,8,1024]{2,1,0:T(8,128)S(1)} %collective-permute-done.17.refs_1_.refs_3_, ...), custom_call_target="tpu_custom_call" | custom-call | flops 4294967296 | tf_op jit(solution)/shard_map/code_pass/pallas_call | solution.py:278
  136.1 2.6 collective-permute-start.21
  138.8 11.8 %code_pass.2 = f32[1024,256]{1,0:T(8,128)S(1)} custom-call(bf16[8192,256]{1,0:T(8,128)(2,1)} %get-tuple-element.182.refs_0_, bf16[8,8,256,1024]{3,2,1,0:T(8,128)(2,1)} %get-tuple-element.132.base_ref.refs_1_, f32[2,8,1024]{2,1,0:T(8,128)S(1)} %add.195.refs_0_.refs_2_, f32[2,8,1024]{2,1,0:T(8,128)S(1)} %collective-permute-done.17.refs_1_.refs_3_, ...), custom_call_target="tpu_custom_call" | custom-call | flops 4294967296 | tf_op jit(solution)/shard_map/code_pass/pallas_call | solution.py:278
  156.8 2.4 collective-permute-start.28
  159.3 2.7 pack.1.embed
  162.0 5.5 %grad_pass.5 = f32[512,256]{1,0:T(8,128)S(1)} custom-call(bf16[512,256]{1,0:T(8,128)(2,1)S(1)} %get-tuple-element.267.cent_ref, f32[2,1,512]{2,1,0:T(1,128)S(1)} %reshape.73.col_ref, bf16[8,2,512,256]{3,2,1,0:T(8,128)(2,1)S(1)} %pack.1.embed, f32[4,1024]{1,0:T(4,128)S(1)} %pad_maximum_fusion.2.refs_0_, f32[4,1024]{1,0:T(4,128)S(1)} %collective-permute-done.24.refs_1_, ...), custom_call_target="tpu_custom_call" | custom-call | flops 4294967296 | bytes 4194304 | tf_op jit(solution)/shard_map/grad_pass/pallas_call | solution.py:375
  167.6 5.5 %grad_pass.7 = f32[512,256]{1,0:T(8,128)S(1)} custom-call(bf16[512,256]{1,0:T(8,128)(2,1)S(1)} %get-tuple-element.268.cent_ref, f32[2,1,512]{2,1,0:T(1,128)S(1)} %reshape.75.col_ref, bf16[8,2,512,256]{3,2,1,0:T(8,128)(2,1)S(1)} %pack.1.embed, f32[4,1024]{1,0:T(4,128)S(1)} %pad_maximum_fusion.2.refs_0_, f32[4,1024]{1,0:T(4,128)S(1)} %collective-permute-done.24.refs_1_, ...), custom_call_target="tpu_custom_call" | custom-call | flops 4294967296 | bytes 4194304 | tf_op jit(solution)/shard_map/grad_pass/pallas_call | solution.py:375
  173.7 5.8 %grad_pass.4 = f32[512,256]{1,0:T(8,128)S(1)} custom-call(bf16[512,256]{1,0:T(8,128)(2,1)S(1)} %get-tuple-element.270.cent_ref, f32[2,1,512]{2,1,0:T(1,128)S(1)} %reshape.72.col_ref, bf16[8,2,512,256]{3,2,1,0:T(8,128)(2,1)S(1)} %pack.1.embed, f32[4,1024]{1,0:T(4,128)S(1)} %pad_maximum_fusion.2.refs_0_, f32[4,1024]{1,0:T(4,128)S(1)} %collective-permute-done.24.refs_1_, ...), custom_call_target="tpu_custom_call" | custom-call | flops 4294967296 | bytes 4194304 | tf_op jit(solution)/shard_map/grad_pass/pallas_call | solution.py:375
  185.2 2.9 collective-permute-start.30
  188.2 5.3 %grad_pass.6 = f32[512,256]{1,0:T(8,128)S(1)} custom-call(bf16[512,256]{1,0:T(8,128)(2,1)S(1)} %get-tuple-element.269.cent_ref, f32[2,1,512]{2,1,0:T(1,128)S(1)} %reshape.74.col_ref, bf16[8,2,512,256]{3,2,1,0:T(8,128)(2,1)S(1)} %pack.1.embed, f32[4,1024]{1,0:T(4,128)S(1)} %pad_maximum_fusion.2.refs_0_, f32[4,1024]{1,0:T(4,128)S(1)} %collective-permute-done.24.refs_1_, ...), custom_call_target="tpu_custom_call" | custom-call | flops 4294967296 | bytes 4194304 | tf_op jit(solution)/shard_map/grad_pass/pallas_call | solution.py:375
  193.5 3.5 %collective-permute-done.32.refs_4_ = f32[512,256]{1,0:T(8,128)S(1)} collective-permute-done((f32[512,256]{1,0:T(8,128)S(1)}, f32[512,256]{1,0:T(8,128)S(1)}, u32[]{:S(2)}, u32[]{:S(2)}) %collective-permute-start.32) | collective-permute-done | bytes 524320 | tf_op jit(solution)/shard_map/ppermute | solution.py:422
  197.0 1.9 collective-permute-done.30
  205.5 7.4 %collective-permute-start.33 = (f32[512,256]{1,0:T(8,128)S(1)}, f32[512,256]{1,0:T(8,128)S(1)}, u32[]{:S(2)}, u32[]{:S(2)}) collective-permute-start(f32[512,256]{1,0:T(8,128)S(1)} %get-tuple-element.219), channel_id=1, source_target_pairs={{0,1},{3,2},{4,5},{7,6},{8,9},{11,10},{12,13},{15,14},{16,17},{19,... | collective-permute-start | bytes 1572872 | tf_op jit(solution)/shard_map/ppermute | solution.py:525
  214.2 3.1 %collective-permute-done.35 = f32[512,256]{1,0:T(8,128)S(1)} collective-permute-done((f32[512,256]{1,0:T(8,128)S(1)}, f32[512,256]{1,0:T(8,128)S(1)}, u32[]{:S(2)}, u32[]{:S(2)}) %collective-permute-start.35) | collective-permute-done | bytes 524320 | tf_op jit(solution)/shard_map/ppermute | solution.py:525
  217.3 4.5 %collective-permute-done.33 = f32[512,256]{1,0:T(8,128)S(1)} collective-permute-done((f32[512,256]{1,0:T(8,128)S(1)}, f32[512,256]{1,0:T(8,128)S(1)}, u32[]{:S(2)}, u32[]{:S(2)}) %collective-permute-start.33) | collective-permute-done | bytes 524320 | tf_op jit(solution)/shard_map/ppermute | solution.py:525
  224.1 6.1 %collective-permute-start.38 = (f32[512,256]{1,0:T(8,128)S(1)}, f32[512,256]{1,0:T(8,128)S(1)}, u32[]{:S(2)}, u32[]{:S(2)}) collective-permute-start(f32[512,256]{1,0:T(8,128)S(1)} %get-tuple-element.218), channel_id=1, source_target_pairs={{0,1},{3,2},{4,5},{7,6},{8,9},{11,10},{12,13},{15,14},{16,17},{19,... | collective-permute-start | bytes 1572872 | tf_op jit(solution)/shard_map/ppermute | solution.py:525
  231.6 5.1 %collective-permute-done.40 = f32[512,256]{1,0:T(8,128)S(1)} collective-permute-done((f32[512,256]{1,0:T(8,128)S(1)}, f32[512,256]{1,0:T(8,128)S(1)}, u32[]{:S(2)}, u32[]{:S(2)}) %collective-permute-start.40) | collective-permute-done | bytes 524320 | tf_op jit(solution)/shard_map/ppermute | solution.py:525
  241.5 4.1 %collective-permute-done.41.refs_8_ = f32[512,256]{1,0:T(8,128)S(1)} collective-permute-done((f32[512,256]{1,0:T(8,128)S(1)}, f32[512,256]{1,0:T(8,128)S(1)}, u32[]{:S(2)}, u32[]{:S(2)}) %collective-permute-start.41) | collective-permute-done | bytes 524320 | tf_op jit(solution)/shard_map/ppermute | solution.py:422
  246.6 9.3 %collective-permute-done.42.refs_12_ = f32[512,256]{1,0:T(8,128)S(1)} collective-permute-done((f32[512,256]{1,0:T(8,128)S(1)}, f32[512,256]{1,0:T(8,128)S(1)}, u32[]{:S(2)}, u32[]{:S(2)}) %collective-permute-start.42) | collective-permute-done | bytes 524320 | tf_op jit(solution)/shard_map/ppermute | solution.py:422
  258.4 1.7 collective-permute-start.52
  264.7 12.0 %collective-permute-done.53 = f32[512,256]{1,0:T(8,128)S(1)} collective-permute-done((f32[512,256]{1,0:T(8,128)S(1)}, f32[512,256]{1,0:T(8,128)S(1)}, u32[]{:S(2)}, u32[]{:S(2)}) %collective-permute-start.53) | collective-permute-done | bytes 524320 | tf_op jit(solution)/shard_map/ppermute | solution.py:525
  279.5 4.5 %place.1 = f32[8192,256]{1,0:T(8,128)} custom-call(s32[16]{0:T(128)S(1)} %stack.67.at_ref, f32[512,256]{1,0:T(8,128)S(1)} %fusion.20.refs_0_, f32[512,256]{1,0:T(8,128)S(1)} %copy-done.15, f32[512,256]{1,0:T(8,128)S(1)} %fusion.17.refs_2_, f32[512,256]{1,0:T(8,128)S(1)} %copy-done.13, f32[512,256]{1,0:T(8,128)S(1)} %collective-permute-done.32.refs_4_, ...), custom_call_target="tpu_custom_call" | custom-call | tf_op jit(solution)/shard_map/place/pallas_call | solution.py:409
  284.1 8.0 %collective-permute-done.54 = f32[512,256]{1,0:T(8,128)S(1)} collective-permute-done((f32[512,256]{1,0:T(8,128)S(1)}, f32[512,256]{1,0:T(8,128)S(1)}, u32[]{:S(2)}, u32[]{:S(2)}) %collective-permute-start.54) | collective-permute-done | bytes 524320 | tf_op jit(solution)/shard_map/ppermute | solution.py:525
  292.3 11.5 %fusion.4 = f32[2,1024,256]{2,1,0:T(8,128)} fusion(f32[2,1024,256]{2,1,0:T(8,128)S(1)} %bitcast.32, bf16[2,1024,256]{2,1,0:T(8,128)(2,1)S(1)} %copy-done.1, f32[2,1024]{1,0:T(2,128)S(1)} %add_rsqrt_fusion), kind=kOutput, calls=%fused_computation.6 | output fusion | flops 4196607 | bytes 5251072 | tf_op jit(solution)/shard_map/mul | solution.py:465
  (193 shorter events, 61.8 us)
Async XLA Ops:
  29.7 6.3 %collective-permute-start.3 = (f32[2,8,1024]{2,1,0:T(8,128)S(1)}, f32[2,8,1024]{2,1,0:T(8,128)S(1)}, u32[]{:S(2)}, u32[]{:S(2)}) collective-permute-start(f32[2,8,1024]{2,1,0:T(8,128)S(1)} %add.189.refs_8_), channel_id=1, source_target_pairs={{0,24},{4,28},{8,16},{12,20},{16,8},{20,12},{24,0},{28,4},{1,25},{... | collective-permute-start | bytes 196616 | tf_op jit(solution)/shard_map/ppermute | solution.py:422
  33.6 4.3 %collective-permute-start.2 = (f32[2,8,1024]{2,1,0:T(8,128)S(1)}, f32[2,8,1024]{2,1,0:T(8,128)S(1)}, u32[]{:S(2)}, u32[]{:S(2)}) collective-permute-start(f32[2,8,1024]{2,1,0:T(8,128)S(1)} %add.189.refs_8_), channel_id=1, source_target_pairs={{0,16},{4,20},{8,24},{12,28},{16,0},{20,4},{24,8},{28,12},{1,17},{... | collective-permute-start | bytes 196616 | tf_op jit(solution)/shard_map/ppermute | solution.py:422
  38.4 24.1 %collective-permute-start.6 = (f32[2,512,256]{2,1,0:T(8,128)S(1)}, f32[2,512,256]{2,1,0:T(8,128)}, u32[]{:S(2)}, u32[]{:S(2)}) collective-permute-start(f32[2,512,256]{2,1,0:T(8,128)S(1)} %get-tuple-element.187.refs_0_), channel_id=1, source_target_pairs={{0,8},{4,12},{8,0},{12,4},{16,24},{20,28},{24,16},{28,20},{1,9},{5... | collective-permute-start | bytes 3145736 | tf_op jit(solution)/shard_map/ppermute | solution.py:422
  39.1 24.8 %collective-permute-start.7 = (f32[2,512,256]{2,1,0:T(8,128)S(1)}, f32[2,512,256]{2,1,0:T(8,128)}, u32[]{:S(2)}, u32[]{:S(2)}) collective-permute-start(f32[2,512,256]{2,1,0:T(8,128)S(1)} %get-tuple-element.188.refs_1_), channel_id=1, source_target_pairs={{0,16},{4,20},{8,24},{12,28},{16,0},{20,4},{24,8},{28,12},{1,17},{... | collective-permute-start | bytes 3145736 | tf_op jit(solution)/shard_map/ppermute | solution.py:422
  51.8 4.7 %collective-permute-start.5 = (f32[4,1024]{1,0:T(4,128)S(1)}, f32[4,1024]{1,0:T(4,128)S(1)}, u32[]{:S(2)}, u32[]{:S(2)}) collective-permute-start(f32[4,1024]{1,0:T(4,128)S(1)} %fusion.23), channel_id=1, source_target_pairs={{0,2},{1,3},{2,0},{3,1},{4,6},{5,7},{6,4},{7,5},{8,10},{9,11},{10,... | collective-permute-start | bytes 49160 | tf_op jit(solution)/shard_map/ppermute | solution.py:422
  65.2 5.3 %collective-permute-start.11 = (f32[2,8,1024]{2,1,0:T(8,128)S(1)}, f32[2,8,1024]{2,1,0:T(8,128)S(1)}, u32[]{:S(2)}, u32[]{:S(2)}) collective-permute-start(f32[2,8,1024]{2,1,0:T(8,128)S(1)} %add.192.refs_8_), channel_id=1, source_target_pairs={{0,24},{4,28},{8,16},{12,20},{16,8},{20,12},{24,0},{28,4},{1,25},{... | collective-permute-start | bytes 196616 | tf_op jit(solution)/shard_map/ppermute | solution.py:422
  66.8 5.0 %collective-permute-start.10 = (f32[2,8,1024]{2,1,0:T(8,128)S(1)}, f32[2,8,1024]{2,1,0:T(8,128)S(1)}, u32[]{:S(2)}, u32[]{:S(2)}) collective-permute-start(f32[2,8,1024]{2,1,0:T(8,128)S(1)} %add.192.refs_8_), channel_id=1, source_target_pairs={{0,16},{4,20},{8,24},{12,28},{16,0},{20,4},{24,8},{28,12},{1,17},{... | collective-permute-start | bytes 196616 | tf_op jit(solution)/shard_map/ppermute | solution.py:422
  67.0 4.7 %collective-permute-start.9 = (f32[2,8,1024]{2,1,0:T(8,128)S(1)}, f32[2,8,1024]{2,1,0:T(8,128)S(1)}, u32[]{:S(2)}, u32[]{:S(2)}) collective-permute-start(f32[2,8,1024]{2,1,0:T(8,128)S(1)} %add.192.refs_8_), channel_id=1, source_target_pairs={{0,8},{4,12},{8,0},{12,4},{16,24},{20,28},{24,16},{28,20},{1,9},{5... | collective-permute-start | bytes 196616 | tf_op jit(solution)/shard_map/ppermute | solution.py:422
  71.7 25.0 %collective-permute-start.14 = (f32[2,512,256]{2,1,0:T(8,128)S(1)}, f32[2,512,256]{2,1,0:T(8,128)S(1)}, u32[]{:S(2)}, u32[]{:S(2)}) collective-permute-start(f32[2,512,256]{2,1,0:T(8,128)S(1)} %get-tuple-element.187.refs_0_), channel_id=1, source_target_pairs={{0,16},{4,20},{8,24},{12,28},{16,0},{20,4},{24,8},{28,12},{1,17},{... | collective-permute-start | bytes 3145736 | tf_op jit(solution)/shard_map/ppermute | solution.py:422
  73.1 24.7 %collective-permute-start.15 = (f32[2,512,256]{2,1,0:T(8,128)S(1)}, f32[2,512,256]{2,1,0:T(8,128)S(1)}, u32[]{:S(2)}, u32[]{:S(2)}) collective-permute-start(f32[2,512,256]{2,1,0:T(8,128)S(1)} %get-tuple-element.188.refs_1_), channel_id=1, source_target_pairs={{0,8},{4,12},{8,0},{12,4},{16,24},{20,28},{24,16},{28,20},{1,9},{5... | collective-permute-start | bytes 3145736 | tf_op jit(solution)/shard_map/ppermute | solution.py:422
  85.0 4.5 %collective-permute-start.13 = (f32[2,1024]{1,0:T(2,128)S(1)}, f32[2,1024]{1,0:T(2,128)S(1)}, u32[]{:S(2)}, u32[]{:S(2)}) collective-permute-start(f32[2,1024]{1,0:T(2,128)S(1)} %add.193), channel_id=1, source_target_pairs={{0,2},{1,3},{2,0},{3,1},{4,6},{5,7},{6,4},{7,5},{8,10},{9,11},{10,... | collective-permute-start | bytes 24584 | tf_op jit(solution)/shard_map/ppermute | solution.py:422
  100.0 5.3 %collective-permute-start.19 = (f32[2,8,1024]{2,1,0:T(8,128)S(1)}, f32[2,8,1024]{2,1,0:T(8,128)S(1)}, u32[]{:S(2)}, u32[]{:S(2)}) collective-permute-start(f32[2,8,1024]{2,1,0:T(8,128)S(1)} %add.195.refs_0_.refs_2_), channel_id=1, source_target_pairs={{0,24},{4,28},{8,16},{12,20},{16,8},{20,12},{24,0},{28,4},{1,25},{... | collective-permute-start | bytes 196616 | tf_op jit(solution)/shard_map/ppermute | solution.py:422
  101.6 5.0 %collective-permute-start.18 = (f32[2,8,1024]{2,1,0:T(8,128)S(1)}, f32[2,8,1024]{2,1,0:T(8,128)S(1)}, u32[]{:S(2)}, u32[]{:S(2)}) collective-permute-start(f32[2,8,1024]{2,1,0:T(8,128)S(1)} %add.195.refs_0_.refs_2_), channel_id=1, source_target_pairs={{0,16},{4,20},{8,24},{12,28},{16,0},{20,4},{24,8},{28,12},{1,17},{... | collective-permute-start | bytes 196616 | tf_op jit(solution)/shard_map/ppermute | solution.py:422
  106.6 44.0 %collective-permute-start.22 = (f32[2,512,256]{2,1,0:T(8,128)}, f32[2,512,256]{2,1,0:T(8,128)}, u32[]{:S(2)}, u32[]{:S(2)}) collective-permute-start(f32[2,512,256]{2,1,0:T(8,128)} %collective-permute-done.6.refs_2_), channel_id=1, source_target_pairs={{0,16},{4,20},{8,24},{12,28},{16,0},{20,4},{24,8},{28,12},{1,17},{... | collective-permute-start | bytes 3145736 | tf_op jit(solution)/shard_map/ppermute | solution.py:422
  107.9 42.7 %collective-permute-start.23 = (f32[2,512,256]{2,1,0:T(8,128)}, f32[2,512,256]{2,1,0:T(8,128)}, u32[]{:S(2)}, u32[]{:S(2)}) collective-permute-start(f32[2,512,256]{2,1,0:T(8,128)} %collective-permute-done.7.refs_5_), channel_id=1, source_target_pairs={{0,8},{4,12},{8,0},{12,4},{16,24},{20,28},{24,16},{28,20},{1,9},{5... | collective-permute-start | bytes 3145736 | tf_op jit(solution)/shard_map/ppermute | solution.py:422
  122.7 13.4 %collective-permute-start.20 = (f32[2,1024]{1,0:T(2,128)S(1)}, f32[2,1024]{1,0:T(2,128)S(1)}, u32[]{:S(2)}, u32[]{:S(2)}) collective-permute-start(f32[2,1024]{1,0:T(2,128)S(1)} %row_last.1), channel_id=1, source_target_pairs={{0,1},{1,0},{2,3},{3,2},{4,5},{5,4},{6,7},{7,6},{8,9},{9,8},{10,11... | collective-permute-start | bytes 24584 | tf_op jit(solution)/shard_map/ppermute | solution.py:422
  136.1 14.4 %collective-permute-start.21 = (f32[2,1024]{1,0:T(2,128)S(1)}, f32[2,1024]{1,0:T(2,128)S(1)}, u32[]{:S(2)}, u32[]{:S(2)}) collective-permute-start(f32[2,1024]{1,0:T(2,128)S(1)} %add.196), channel_id=1, source_target_pairs={{0,2},{1,3},{2,0},{3,1},{4,6},{5,7},{6,4},{7,5},{8,10},{9,11},{10,... | collective-permute-start | bytes 24584 | tf_op jit(solution)/shard_map/ppermute | solution.py:422
  150.6 11.4 %collective-permute-start.26 = (f32[4,1024]{1,0:T(4,128)S(1)}, f32[4,1024]{1,0:T(4,128)S(1)}, u32[]{:S(2)}, u32[]{:S(2)}) collective-permute-start(f32[4,1024]{1,0:T(4,128)S(1)} %pad_maximum_fusion.2.refs_0_), channel_id=1, source_target_pairs={{0,24},{4,28},{8,16},{12,20},{16,8},{20,12},{24,0},{28,4},{1,25},{... | collective-permute-start | bytes 49160 | tf_op jit(solution)/shard_map/ppermute | solution.py:422
  152.1 9.9 %collective-permute-start.25 = (f32[4,1024]{1,0:T(4,128)S(1)}, f32[4,1024]{1,0:T(4,128)S(1)}, u32[]{:S(2)}, u32[]{:S(2)}) collective-permute-start(f32[4,1024]{1,0:T(4,128)S(1)} %pad_maximum_fusion.2.refs_0_), channel_id=1, source_target_pairs={{0,16},{4,20},{8,24},{12,28},{16,0},{20,4},{24,8},{28,12},{1,17},{... | collective-permute-start | bytes 49160 | tf_op jit(solution)/shard_map/ppermute | solution.py:422
  153.5 8.6 %collective-permute-start.24 = (f32[4,1024]{1,0:T(4,128)S(1)}, f32[4,1024]{1,0:T(4,128)S(1)}, u32[]{:S(2)}, u32[]{:S(2)}) collective-permute-start(f32[4,1024]{1,0:T(4,128)S(1)} %pad_maximum_fusion.2.refs_0_), channel_id=1, source_target_pairs={{0,8},{4,12},{8,0},{12,4},{16,24},{20,28},{24,16},{28,20},{1,9},{5... | collective-permute-start | bytes 49160 | tf_op jit(solution)/shard_map/ppermute | solution.py:422
  156.8 22.6 %collective-permute-start.28 = (f32[512,256]{1,0:T(8,128)S(1)}, f32[512,256]{1,0:T(8,128)S(1)}, u32[]{:S(2)}, u32[]{:S(2)}) collective-permute-start(f32[512,256]{1,0:T(8,128)S(1)} %get-tuple-element.201), channel_id=1, source_target_pairs={{0,1},{3,2},{4,5},{7,6},{8,9},{11,10},{12,13},{15,14},{16,17},{19,... | collective-permute-start | bytes 1572872 | tf_op jit(solution)/shard_map/ppermute | solution.py:525
  167.5 11.9 %collective-permute-start.27 = (f32[512,256]{1,0:T(8,128)S(1)}, f32[512,256]{1,0:T(8,128)S(1)}, u32[]{:S(2)}, u32[]{:S(2)}) collective-permute-start(f32[512,256]{1,0:T(8,128)S(1)} %grad_pass.5), channel_id=1, source_target_pairs={{0,4},{4,0},{8,12},{12,8},{16,20},{20,16},{24,28},{28,24},{1,5},{5... | collective-permute-start | bytes 1572872 | tf_op jit(solution)/shard_map/ppermute | solution.py:422
  173.1 20.4 %collective-permute-start.29 = (f32[512,256]{1,0:T(8,128)S(1)}, f32[512,256]{1,0:T(8,128)S(1)}, u32[]{:S(2)}, u32[]{:S(2)}) collective-permute-start(f32[512,256]{1,0:T(8,128)S(1)} %grad_pass.7), channel_id=1, source_target_pairs={{0,4},{4,0},{8,12},{12,8},{16,20},{20,16},{24,28},{28,24},{1,5},{5... | collective-permute-start | bytes 1572872 | tf_op jit(solution)/shard_map/ppermute | solution.py:422
  183.1 13.9 %collective-permute-start.32 = (f32[512,256]{1,0:T(8,128)S(1)}, f32[512,256]{1,0:T(8,128)S(1)}, u32[]{:S(2)}, u32[]{:S(2)}) collective-permute-start(f32[512,256]{1,0:T(8,128)S(1)} %fusion.20.refs_0_), channel_id=1, source_target_pairs={{0,8},{4,12},{8,0},{12,4},{16,24},{20,28},{24,16},{28,20},{1,9},{5... | collective-permute-start | bytes 1572872 | tf_op jit(solution)/shard_map/ppermute | solution.py:422
  184.5 12.5 %collective-permute-start.31 = (f32[512,256]{1,0:T(8,128)S(1)}, f32[512,256]{1,0:T(8,128)S(1)}, u32[]{:S(2)}, u32[]{:S(2)}) collective-permute-start(f32[512,256]{1,0:T(8,128)S(1)} %add.212), channel_id=1, source_target_pairs={{1,2},{2,1},{5,6},{6,5},{9,10},{10,9},{13,14},{14,13},{17,18},{18,... | collective-permute-start | bytes 1572872 | tf_op jit(solution)/shard_map/ppermute | solution.py:525
  185.2 13.7 %collective-permute-start.30 = (f32[512,256]{1,0:T(8,128)S(1)}, f32[512,256]{1,0:T(8,128)S(1)}, u32[]{:S(2)}, u32[]{:S(2)}) collective-permute-start(f32[512,256]{1,0:T(8,128)S(1)} %get-tuple-element.209), channel_id=1, source_target_pairs={{0,1},{3,2},{4,5},{7,6},{8,9},{11,10},{12,13},{15,14},{16,17},{19,... | collective-permute-start | bytes 1572872 | tf_op jit(solution)/shard_map/ppermute | solution.py:525
  201.3 12.4 %collective-permute-start.37 = (f32[512,256]{1,0:T(8,128)S(1)}, f32[512,256]{1,0:T(8,128)S(1)}, u32[]{:S(2)}, u32[]{:S(2)}) collective-permute-start(f32[512,256]{1,0:T(8,128)S(1)} %fusion.17.refs_2_), channel_id=1, source_target_pairs={{0,16},{4,20},{8,24},{12,28},{16,0},{20,4},{24,8},{28,12},{1,17},{... | collective-permute-start | bytes 1572872 | tf_op jit(solution)/shard_map/ppermute | solution.py:422
  202.1 12.1 %collective-permute-start.36 = (f32[512,256]{1,0:T(8,128)S(1)}, f32[512,256]{1,0:T(8,128)S(1)}, u32[]{:S(2)}, u32[]{:S(2)}) collective-permute-start(f32[512,256]{1,0:T(8,128)S(1)} %fusion.17.refs_2_), channel_id=1, source_target_pairs={{0,8},{4,12},{8,0},{12,4},{16,24},{20,28},{24,16},{28,20},{1,9},{5... | collective-permute-start | bytes 1572872 | tf_op jit(solution)/shard_map/ppermute | solution.py:422
  203.5 13.8 %collective-permute-start.35 = (f32[512,256]{1,0:T(8,128)S(1)}, f32[512,256]{1,0:T(8,128)S(1)}, u32[]{:S(2)}, u32[]{:S(2)}) collective-permute-start(f32[512,256]{1,0:T(8,128)S(1)} %add.216), channel_id=1, source_target_pairs={{1,0},{2,3},{5,4},{6,7},{9,8},{10,11},{13,12},{14,15},{17,16},{18,... | collective-permute-start | bytes 1572872 | tf_op jit(solution)/shard_map/ppermute | solution.py:525
  204.8 12.5 %collective-permute-start.34 = (f32[512,256]{1,0:T(8,128)S(1)}, f32[512,256]{1,0:T(8,128)S(1)}, u32[]{:S(2)}, u32[]{:S(2)}) collective-permute-start(f32[512,256]{1,0:T(8,128)S(1)} %add.215), channel_id=1, source_target_pairs={{1,2},{2,1},{5,6},{6,5},{9,10},{10,9},{13,14},{14,13},{17,18},{18,... | collective-permute-start | bytes 1572872 | tf_op jit(solution)/shard_map/ppermute | solution.py:525
  205.5 16.2 %collective-permute-start.33 = (f32[512,256]{1,0:T(8,128)S(1)}, f32[512,256]{1,0:T(8,128)S(1)}, u32[]{:S(2)}, u32[]{:S(2)}) collective-permute-start(f32[512,256]{1,0:T(8,128)S(1)} %get-tuple-element.219), channel_id=1, source_target_pairs={{0,1},{3,2},{4,5},{7,6},{8,9},{11,10},{12,13},{15,14},{16,17},{19,... | collective-permute-start | bytes 1572872 | tf_op jit(solution)/shard_map/ppermute | solution.py:525
  221.9 8.9 %collective-permute-start.39 = (f32[512,256]{1,0:T(8,128)S(1)}, f32[512,256]{1,0:T(8,128)S(1)}, u32[]{:S(2)}, u32[]{:S(2)}) collective-permute-start(f32[512,256]{1,0:T(8,128)S(1)} %add.219), channel_id=1, source_target_pairs={{1,2},{2,1},{5,6},{6,5},{9,10},{10,9},{13,14},{14,13},{17,18},{18,... | collective-permute-start | bytes 1572872 | tf_op jit(solution)/shard_map/ppermute | solution.py:525
  222.8 13.9 %collective-permute-start.40 = (f32[512,256]{1,0:T(8,128)S(1)}, f32[512,256]{1,0:T(8,128)S(1)}, u32[]{:S(2)}, u32[]{:S(2)}) collective-permute-start(f32[512,256]{1,0:T(8,128)S(1)} %add.220), channel_id=1, source_target_pairs={{1,0},{2,3},{5,4},{6,7},{9,8},{10,11},{13,12},{14,15},{17,16},{18,... | collective-permute-start | bytes 1572872 | tf_op jit(solution)/shard_map/ppermute | solution.py:525
  224.1 13.8 %collective-permute-start.38 = (f32[512,256]{1,0:T(8,128)S(1)}, f32[512,256]{1,0:T(8,128)S(1)}, u32[]{:S(2)}, u32[]{:S(2)}) collective-permute-start(f32[512,256]{1,0:T(8,128)S(1)} %get-tuple-element.218), channel_id=1, source_target_pairs={{0,1},{3,2},{4,5},{7,6},{8,9},{11,10},{12,13},{15,14},{16,17},{19,... | collective-permute-start | bytes 1572872 | tf_op jit(solution)/shard_map/ppermute | solution.py:525
  230.2 8.4 %collective-permute-start.46 = (f32[512,256]{1,0:T(8,128)S(1)}, f32[512,256]{1,0:T(8,128)S(1)}, u32[]{:S(2)}, u32[]{:S(2)}) collective-permute-start(f32[512,256]{1,0:T(8,128)S(1)} %fusion.17.refs_2_), channel_id=1, source_target_pairs={{0,4},{4,0},{8,12},{12,8},{16,20},{20,16},{24,28},{28,24},{1,5},{5... | collective-permute-start | bytes 1572872 | tf_op jit(solution)/shard_map/ppermute | solution.py:422
  230.3 9.1 %collective-permute-start.44 = (f32[512,256]{1,0:T(8,128)S(1)}, f32[512,256]{1,0:T(8,128)S(1)}, u32[]{:S(2)}, u32[]{:S(2)}) collective-permute-start(f32[512,256]{1,0:T(8,128)S(1)} %fusion.20.refs_0_), channel_id=1, source_target_pairs={{0,4},{4,0},{8,12},{12,8},{16,20},{20,16},{24,28},{28,24},{1,5},{5... | collective-permute-start | bytes 1572872 | tf_op jit(solution)/shard_map/ppermute | solution.py:422
  230.8 14.8 %collective-permute-start.41 = (f32[512,256]{1,0:T(8,128)S(1)}, f32[512,256]{1,0:T(8,128)S(1)}, u32[]{:S(2)}, u32[]{:S(2)}) collective-permute-start(f32[512,256]{1,0:T(8,128)S(1)} %fusion.20.refs_0_), channel_id=1, source_target_pairs={{0,16},{4,20},{8,24},{12,28},{16,0},{20,4},{24,8},{28,12},{1,17},{... | collective-permute-start | bytes 1572872 | tf_op jit(solution)/shard_map/ppermute | solution.py:422
  236.6 8.9 %collective-permute-start.45 = (f32[512,256]{1,0:T(8,128)S(1)}, f32[512,256]{1,0:T(8,128)S(1)}, u32[]{:S(2)}, u32[]{:S(2)}) collective-permute-start(f32[512,256]{1,0:T(8,128)S(1)} %collective-permute-done.32.refs_4_), channel_id=1, source_target_pairs={{0,4},{4,0},{8,12},{12,8},{16,20},{20,16},{24,28},{28,24},{1,5},{5... | collective-permute-start | bytes 1572872 | tf_op jit(solution)/shard_map/ppermute | solution.py:422
  237.9 18.1 %collective-permute-start.42 = (f32[512,256]{1,0:T(8,128)S(1)}, f32[512,256]{1,0:T(8,128)S(1)}, u32[]{:S(2)}, u32[]{:S(2)}) collective-permute-start(f32[512,256]{1,0:T(8,128)S(1)} %collective-permute-done.32.refs_4_), channel_id=1, source_target_pairs={{0,16},{4,20},{8,24},{12,28},{16,0},{20,4},{24,8},{28,12},{1,17},{... | collective-permute-start | bytes 1572872 | tf_op jit(solution)/shard_map/ppermute | solution.py:422
  239.4 16.5 %collective-permute-start.47 = (f32[512,256]{1,0:T(8,128)S(1)}, f32[512,256]{1,0:T(8,128)S(1)}, u32[]{:S(2)}, u32[]{:S(2)}) collective-permute-start(f32[512,256]{1,0:T(8,128)S(1)} %collective-permute-done.37.refs_10_), channel_id=1, source_target_pairs={{0,4},{4,0},{8,12},{12,8},{16,20},{20,16},{24,28},{28,24},{1,5},{5... | collective-permute-start | bytes 1572872 | tf_op jit(solution)/shard_map/ppermute | solution.py:422
  240.2 17.3 %collective-permute-start.43 = (f32[512,256]{1,0:T(8,128)S(1)}, f32[512,256]{1,0:T(8,128)}, u32[]{:S(2)}, u32[]{:S(2)}) collective-permute-start(f32[512,256]{1,0:T(8,128)S(1)} %collective-permute-done.37.refs_10_), channel_id=1, source_target_pairs={{0,8},{4,12},{8,0},{12,4},{16,24},{20,28},{24,16},{28,20},{1,9},{5... | collective-permute-start | bytes 1572872 | tf_op jit(solution)/shard_map/ppermute | solution.py:422
  258.4 5.4 %collective-permute-start.52 = (f32[512,256]{1,0:T(8,128)}, f32[512,256]{1,0:T(8,128)}, u32[]{:S(2)}, u32[]{:S(2)}) collective-permute-start(f32[512,256]{1,0:T(8,128)} %add.221), channel_id=1, source_target_pairs={{1,2},{2,1},{5,6},{6,5},{9,10},{10,9},{13,14},{14,13},{17,18},{18,... | collective-permute-start | bytes 1572872 | tf_op jit(solution)/shard_map/ppermute | solution.py:525
  261.7 15.1 %collective-permute-start.53 = (f32[512,256]{1,0:T(8,128)S(1)}, f32[512,256]{1,0:T(8,128)S(1)}, u32[]{:S(2)}, u32[]{:S(2)}) collective-permute-start(f32[512,256]{1,0:T(8,128)S(1)} %add.222), channel_id=1, source_target_pairs={{1,0},{2,3},{5,4},{6,7},{9,8},{10,11},{13,12},{14,15},{17,16},{18,... | collective-permute-start | bytes 1572872 | tf_op jit(solution)/shard_map/ppermute | solution.py:525
  263.1 13.7 %collective-permute-start.48 = (f32[512,256]{1,0:T(8,128)}, f32[512,256]{1,0:T(8,128)S(1)}, u32[]{:S(2)}, u32[]{:S(2)}) collective-permute-start(f32[512,256]{1,0:T(8,128)} %copy-done.10), channel_id=1, source_target_pairs={{0,4},{4,0},{8,12},{12,8},{16,20},{20,16},{24,28},{28,24},{1,5},{5... | collective-permute-start | bytes 1572872 | tf_op jit(solution)/shard_map/ppermute | solution.py:422
  263.2 13.6 %collective-permute-start.49 = (f32[512,256]{1,0:T(8,128)}, f32[512,256]{1,0:T(8,128)S(1)}, u32[]{:S(2)}, u32[]{:S(2)}) collective-permute-start(f32[512,256]{1,0:T(8,128)} %copy-done.16), channel_id=1, source_target_pairs={{0,4},{4,0},{8,12},{12,8},{16,20},{20,16},{24,28},{28,24},{1,5},{5... | collective-permute-start | bytes 1572872 | tf_op jit(solution)/shard_map/ppermute | solution.py:422
  263.7 13.1 %collective-permute-start.50 = (f32[512,256]{1,0:T(8,128)}, f32[512,256]{1,0:T(8,128)S(1)}, u32[]{:S(2)}, u32[]{:S(2)}) collective-permute-start(f32[512,256]{1,0:T(8,128)} %copy-done.20), channel_id=1, source_target_pairs={{0,4},{4,0},{8,12},{12,8},{16,20},{20,16},{24,28},{28,24},{1,5},{5... | collective-permute-start | bytes 1572872 | tf_op jit(solution)/shard_map/ppermute | solution.py:422
  263.8 13.0 %collective-permute-start.51 = (f32[512,256]{1,0:T(8,128)}, f32[512,256]{1,0:T(8,128)S(1)}, u32[]{:S(2)}, u32[]{:S(2)}) collective-permute-start(f32[512,256]{1,0:T(8,128)} %collective-permute-done.43.refs_14_), channel_id=1, source_target_pairs={{0,4},{4,0},{8,12},{12,8},{16,20},{20,16},{24,28},{28,24},{1,5},{5... | collective-permute-start | bytes 1572872 | tf_op jit(solution)/shard_map/ppermute | solution.py:422
  278.1 14.0 %collective-permute-start.54 = (f32[512,256]{1,0:T(8,128)S(1)}, f32[512,256]{1,0:T(8,128)S(1)}, u32[]{:S(2)}, u32[]{:S(2)}) collective-permute-start(f32[512,256]{1,0:T(8,128)S(1)} %add.241), channel_id=1, source_target_pairs={{1,0},{2,3},{5,4},{6,7},{9,8},{10,11},{13,12},{14,15},{17,16},{18,... | collective-permute-start | bytes 1572872 | tf_op jit(solution)/shard_map/ppermute | solution.py:525
  (41 other events, 494.8 us)

commit v5 on v3

--- a/solution.py
+++ b/solution.py
@@ -57,12 +57,16 @@
     return high, (x - high.astype(F32)).astype(BF16)
 
 
+def in_hbm(x):
+    return pltpu.with_memory_space_constraint(x, pltpu.HBM)
+
+
 def in_vmem():
     return pl.BlockSpec(memory_space=pltpu.VMEM)
 
 
 def first_kernel(feat_ref, proto_ref, lo_ref, hi_ref, cent_ref, col_ref, tot_ref, soft_ref, *refs):
-    *base_refs, acc, embed_ref = refs
+    kept_ref, *base_refs, acc, embed_ref, sems = refs
     i = pl.program_id(0)
     rows = feat_ref.shape[1]
     kt = proto_ref.shape[0]
@@ -92,8 +96,17 @@
             col = col + sub_fold(b)
         col_ref[v, pl.ds(i, 1), :] = jnp.sum(col, axis=0, keepdims=True)
 
+    def keep(tile, j):
+        return pltpu.make_async_copy(base_refs[j].at[tile], kept_ref.at[j, tile], sems.at[tile, j])
+
+    for j in range(len(base_refs)):
+        keep(i, j).start()
+
     @pl.when(i == pl.num_programs(0) - 1)
     def _():
+        for tile in range(sems.shape[0]):
+            for j in range(len(base_refs)):
+                keep(tile, j).wait()
         for v in range(2):
             tot_ref[v : v + 1, :] = jnp.sum(acc[v].T, axis=0, keepdims=True)
 
@@ -116,6 +129,7 @@
             in_vmem(),
             in_vmem(),
             in_vmem(),
+            pl.BlockSpec(memory_space=pl.ANY),
         ]
         + [in_vmem()] * m,
         out_shape=[
@@ -125,14 +139,19 @@
             jax.ShapeDtypeStruct((2, n, kt), F32),
             jax.ShapeDtypeStruct((2, rows), F32),
             jax.ShapeDtypeStruct((2, rows, width), F32),
+            pltpu.HBM((m, n, rc, kt), BF16),
         ]
         + [pltpu.VMEM((n, rc, kt), BF16)] * m,
-        scratch_shapes=[pltpu.VMEM((2, rows, 128), F32), pltpu.VMEM((2, rows, width), BF16)],
+        scratch_shapes=[
+            pltpu.VMEM((2, rows, 128), F32),
+            pltpu.VMEM((2, rows, width), BF16),
+            pltpu.SemaphoreType.DMA((n, m)),
+        ],
         compiler_params=params(16),
         cost_estimate=cost(16 * rows * protos * width, 0),
         name="first",
     )(features, prototypes)
-    return outs[:6], outs[6:]
+    return outs[:7], outs[7:]
 
 
 def load_scales(part_refs, rows_ref, cols_ref, v):
@@ -173,54 +192,72 @@
             out_ref[v : v + 1, j * rc : (j + 1) * rc] = sums
 
 
-def row_last_kernel(m, *refs):
-    base_refs, cent_ref, part_refs = refs[:m], refs[m], refs[m + 1 : -6]
-    out_ref, code_ref, rows_ref, cols_ref, acc, scaled = refs[-6:]
-    n, rc, kt = base_refs[0].shape
-    for v in range(2):
-        load_scales(part_refs, rows_ref, cols_ref, v)
-        for i in range(n):
-            c = spread(rows_ref[i : i + 1, :])
-            c = jnp.concatenate([c] * (scaled.shape[2] // 128), axis=1)
-            scaled[i] = (cent_ref[i * kt : (i + 1) * kt, :].astype(F32) * c).astype(BF16)
-        for j in range(m // 2):
-            base_ref = base_refs[v * (m // 2) + j]
-            r = slice(j * rc, (j + 1) * rc)
-            out_ref[v : v + 1, r] = block_sum(base_ref, rows_ref, cols_ref, acc)
-            total = jnp.dot(base_ref[0], scaled[0], preferred_element_type=F32)
-            for i in range(1, n):
-                total = total + jnp.dot(base_ref[i], scaled[i], preferred_element_type=F32)
-            code_ref[v, r, :] = total
-
-
-def row_pass(base, parts, centers=None):
+def row_pass(base, parts):
     m = len(base)
     n, rc, kt = base[0].shape
     rows = m // 2 * rc
-    out_shape = [jax.ShapeDtypeStruct((2, rows), F32)]
-    args = list(base)
-    scratch = [
-        pltpu.VMEM((n, kt), F32),
-        pltpu.VMEM((n, kt // 2, 128), BF16),
-        pltpu.VMEM((rc, 128), F32),
-    ]
-    kernel = row_kernel
-    if centers is not None:
-        width = centers.shape[1]
-        out_shape.append(jax.ShapeDtypeStruct((2, rows, width), F32))
-        args.append(centers)
-        scratch.append(pltpu.VMEM((n, kt, width), BF16))
-        kernel = row_last_kernel
     return pl.pallas_call(
-        lambda *refs: kernel(m, *refs),
-        in_specs=[in_vmem()] * (len(args) + len(parts)),
-        out_specs=[in_vmem()] * len(out_shape),
-        out_shape=out_shape,
-        scratch_shapes=scratch,
+        lambda *refs: row_kernel(m, *refs),
+        in_specs=[in_vmem()] * (m + len(parts)),
+        out_specs=in_vmem(),
+        out_shape=jax.ShapeDtypeStruct((2, rows), F32),
+        scratch_shapes=[
+            pltpu.VMEM((n, kt), F32),
+            pltpu.VMEM((n, kt // 2, 128), BF16),
+            pltpu.VMEM((rc, 128), F32),
+        ],
         compiler_params=params(16),
         cost_estimate=cost(0, 4 * n * rows * kt),
-        name="row_pass" if centers is None else "row_last",
-    )(*args, *parts)
+        name="row_pass",
+    )(*base, *parts)
+
+
+def row_last_kernel(base_ref, cent_ref, *refs):
+    *part_refs, out_ref, code_ref, acc = refs
+    m, _, rc, _ = base_ref.shape
+    i = pl.program_id(0)
+
+    @pl.when(i == 0)
+    def _():
+        acc[...] = jnp.zeros_like(acc)
+        code_ref[...] = jnp.zeros_like(code_ref)
+
+    for v in range(2):
+        c = 1.0 / sum(p[v, pl.ds(i, 1), :] for p in part_refs)
+        for j in range(m // 2):
+            r = slice(j * rc, (j + 1) * rc)
+            w = base_ref[v * (m // 2) + j, 0].astype(F32) * c
+            acc[v, r, :] += lane_fold(w)
+            code_ref[v, r, :] += jnp.dot(w.astype(BF16), cent_ref[...], preferred_element_type=F32)
+
+    @pl.when(i == pl.num_programs(0) - 1)
+    def _():
+        for v in range(2):
+            out_ref[v : v + 1, :] = jnp.sum(acc[v].T, axis=0, keepdims=True)
+
+
+def row_last(kept, centers, parts):
+    m, n, rc, kt = kept.shape
+    rows = m // 2 * rc
+    width = centers.shape[1]
+    return pl.pallas_call(
+        row_last_kernel,
+        grid=(n,),
+        in_specs=[
+            pl.BlockSpec((m, 1, rc, kt), lambda i: (0, i, 0, 0)),
+            pl.BlockSpec((kt, width), lambda i: (i, 0)),
+        ]
+        + [in_vmem()] * len(parts),
+        out_specs=[in_vmem()] * 2,
+        out_shape=[
+            jax.ShapeDtypeStruct((2, rows), F32),
+            jax.ShapeDtypeStruct((2, rows, width), F32),
+        ],
+        scratch_shapes=[pltpu.VMEM((2, rows, 128), F32)],
+        compiler_params=params(16),
+        cost_estimate=cost(0, 8 * n * rows * kt),
+        name="row_last",
+    )(in_hbm(kept), in_hbm(centers), *parts)
 
 
 def col_kernel(total_ref, *refs):
@@ -346,6 +383,7 @@
         out_shape=jax.ShapeDtypeStruct((size, pieces[0].shape[1]), F32),
         scratch_shapes=[pltpu.SemaphoreType.DMA((m,))],
         compiler_params=params(24),
+        cost_estimate=cost(0, 12 * size * pieces[0].shape[1]),
         name="place",
     )(jnp.stack(at).astype(jnp.int32), *pieces)
 
@@ -451,14 +489,14 @@
     chip, core = me // 2, me % 2
     share = protos // (nb // 2)
 
-    (lo, hi, centers, col, tot, soft), base = first(features, prototypes)
+    (lo, hi, centers, col, tot, soft, kept), base = first(features, prototypes)
     parts = col_exchange(col, nb)
     have, plan = [{0: lo}, {0: hi}], gather_plan(nb)
     have, parts = lax.optimization_barrier((have, parts))
     for step in range(ITERS - 1):
         if plan:
             send_pair(have, plan.pop(0), nb)
-        (row,) = row_pass(base, parts)
+        row = row_pass(base, parts)
         if step == 0:
             both = row_exchange(jnp.concatenate([row, tot]), npr)
             row, tot = both[:2], both[2:]
@@ -470,9 +508,9 @@
         have, parts = lax.optimization_barrier((have, parts))
     for pair in plan:
         send_pair(have, pair, nb)
-    row, code = row_pass(base, parts, centers)
+    row, code = row_last(kept, centers, parts)
     row = row_exchange(row, npr)
-    row, have = lax.optimization_barrier((row, have))
+    row, have, centers = lax.optimization_barrier((row, have, centers))
     rows_all = gather_rows(jnp.concatenate([row, tot]), nb)
     embeds = pack([have[h][k] for k in range(0, nb, 2) for h in range(2)])
     col = (1.0 / sum(parts)).reshape(2, protos)
@@ -489,7 +527,9 @@
     ]
     pair = halve_over_proto(gf[0], npr, 1)
     theirs = grads(chip * share + (1 - core) * half)
-    theirs, pair, late = lax.optimization_barrier((theirs, pair, gf[1]))
+    theirs, pair, late, features, prototypes = lax.optimization_barrier(
+        (theirs, pair, gf[1], features, prototypes)
+    )
     theirs = swap(theirs, "batch", nb, 1)
     pair = halve_over_proto(pair[0] + pair[1], npr, 2)
     pair_late = halve_over_proto(late, npr, 1)
@@ -508,24 +548,27 @@
     shards = [spread_out([shard, near], npr), shard_back(late, features[1], npr)]
     near = swap(shards[1], "proto", npr, last)
     have, near, first_view = lax.optimization_barrier((have, near, shards[0]))
+    twin = {(h, 0): swap(have[h][0], "batch", nb, 1) for h in range(2)}
     for p in plan:
         send_pair(have, p, nb)
     shards = [first_view, spread_out([shards[1], near], npr)]
+    have, twin, shards = lax.optimization_barrier((have, twin, shards))
+    out, where = [], []
+    for k in have[0]:
+        for h in range(2):
+            at = (chip ^ (k // 2)) * share + h * quarter
+            other = twin[h, k] if (h, k) in twin else swap(have[h][k], "batch", nb, 1)
+            out += [have[h][k], other]
+            where += [at + core * half, at + (1 - core) * half]
+    grad_prototypes = place(out, where, protos)
+
     idx = lax.axis_index("proto")
     out, where = [], []
     for v in range(2):
         for k, x in shards[v].items():
             out.append(x)
             where.append(home(idx ^ k, npr, rows) + v * rows)
-    grad_features = place(out, where, 2 * rows).reshape(2, rows, width)
-
-    out, where = [], []
-    for k in have[0]:
-        for h in range(2):
-            at = (chip ^ (k // 2)) * share + h * quarter
-            out += [have[h][k], swap(have[h][k], "batch", nb, 1)]
-            where += [at + core * half, at + (1 - core) * half]
-    return grad_features, place(out, where, protos)
+    return place(out, where, 2 * rows).reshape(2, rows, width), grad_prototypes
 
 
 def solution(mesh):

time: 284 us -> 272 us (0.958)
  local copies, waits for them, and re-layouts: 29.7 us -> 10.5 us
  waiting for transfers between devices: 91.9 us -> 98.5 us
    unnamed x79 -> x39, local copies, waits for them, and re-layouts: 24.6 us -> 7.73 us
    ppermute x50, waiting for transfers between devices: 91.9 us -> 98.5 us  [swap(): return lax.ppermute(x, axis, [(i, i ^ m) for i in range(n)])]
  transfers between devices with their start and end apart: 50 -> 50, of which waited for: 28 -> 29; matrix products, arithmetic and copies ran while one was open for 5% -> 3% of each run, Pallas kernels for 24% -> 25%
where the time goes in v5:
time: 272 us; the launch traced here: 269 us
  Pallas kernels  99.1 us (36%)
  waiting for transfers between devices  98.5 us (36%)
  starting transfers between devices  51.7 us (19%)
  local copies, waits for them, and re-layouts  10.5 us (4%)
  other arithmetic  7.51 us (3%)
    ppermute x50, waiting for transfers between devices, swap(): return lax.ppermute(x, axis, [(i, i ^ m) for i in range(n)])  98.5 us
    ppermute x50, starting transfers between devices, swap(): return lax.ppermute(x, axis, [(i, i ^ m) for i in range(n)])  51.7 us
    pallas_call x1, Pallas kernels, first(): pl.pallas_call(first_kernel, grid=(n,), in_specs=[in_vmem(), pl.BlockSpec...  26.4 us
    pallas_call x2, Pallas kernels, grad_pass(): pl.pallas_call(grad_kernel, grid=(n,), in_specs=[pl.BlockSpec((kt, width)...  20.3 us
    pallas_call x1, Pallas kernels, row_last(): pl.pallas_call(row_last_kernel, grid=(n,), in_specs=[pl.BlockSpec((m, 1,...  18.1 us
    pallas_call x2, Pallas kernels, row_pass(): pl.pallas_call(lambda *refs: row_kernel(m, *refs), in_specs=[in_vmem()] *...  15 us
    pallas_call x2, Pallas kernels, col_pass(): pl.pallas_call(col_kernel, in_specs=[in_vmem()] * (m + 1), out_specs=in_v...  8.89 us
    pallas_call x2, Pallas kernels, place(): pl.pallas_call(place_kernel, in_specs=[pl.BlockSpec(memory_space=pltpu.SM...  7.82 us
  transfers between devices with their start and end apart: 50, of which 29 were waited for; matrix products, arithmetic and copies ran while one was open for 3% of the time, Pallas kernels for 25%

profile of v5, /device:TPU:0, one launch (start us, length us, event | category | flops | bytes accessed | tf_op | source)
XLA Modules:
  0.0 268.7 jit_solution(248458600479642276)
XLA Ops:
  1.9 26.4 %first.1 = (f32[2,512,256]{2,1,0:T(8,128)S(1)}, f32[2,512,256]{2,1,0:T(8,128)S(1)}, bf16[8192,256]{1,0:T(8,128)(2,1)}, f32[2,8,1024]{2,1,0:T(8,128)S(1)}, f32[2,...) custom-call(bf16[2,1024,256]{2,1,0:T(8,128)(2,1)S(1)} %copy-done.7, ...), custom_call_target="tpu_custom_call" | custom-call | flops 34359738368 | tf_op jit(solution)/shard_map/first/pallas_call | solution.py:121
  29.7 3.9 %collective-permute-start.3 = (f32[2,8,1024]{2,1,0:T(8,128)S(1)}, f32[2,8,1024]{2,1,0:T(8,128)S(1)}, u32[]{:S(2)}, u32[]{:S(2)}) collective-permute-start(f32[2,8,1024]{2,1,0:T(8,128)S(1)} %add.267.refs_8_), channel_id=1, source_target_pairs={{0,24},{4,28},{8,16},{12,20},{16,8},{20,12},{24,0},{28,4},{1,25},{... | collective-permute-start | bytes 196616 | tf_op jit(solution)/shard_map/ppermute | solution.py:392
  34.2 1.8 collective-permute-done.3.refs_11_
  35.9 1.9 collective-permute-done.2.refs_10_
  40.4 7.5 %row_pass.2 = f32[2,1024]{1,0:T(2,128)S(1)} custom-call(bf16[8,256,1024]{2,1,0:T(8,128)(2,1)S(1)} %get-tuple-element.115.refs_0_, bf16[8,256,1024]{2,1,0:T(8,128)(2,1)S(1)} %get-tuple-element.116.refs_1_, bf16[8,256,1024]{2,1,0:T(8,128)(2,1)S(1)} %get-tuple-element.117.refs_2_, bf16[8,256,1024]{2,1,0:T(8,128)(2,1)S(1)} %get-tuple-element.118.refs_3_, ...), custom_call_target="tpu_custom_call" | custom-call | bytes 33554432 | tf_op jit(solution)/shard_map/row_pass/pallas_call | solution.py:199
  47.9 1.6 collective-permute-start.4
  49.5 2.2 collective-permute-done.4
  51.7 2.7 collective-permute-start.5
  54.4 2.0 collective-permute-done.5
  56.4 4.4 %col_pass.2 = f32[2,8,1024]{2,1,0:T(8,128)S(1)} custom-call(f32[2,1024]{1,0:T(2,128)S(1)} %get-tuple-element.255.total_ref, bf16[8,256,1024]{2,1,0:T(8,128)(2,1)S(1)} %get-tuple-element.115.refs_0_, bf16[8,256,1024]{2,1,0:T(8,128)(2,1)S(1)} %get-tuple-element.116.refs_1_, bf16[8,256,1024]{2,1,0:T(8,128)(2,1)S(1)} %get-tuple-element.117.refs_2_, ...), custom_call_target="tpu_custom_call" | custom-call | bytes 33554432 | tf_op jit(solution)/shard_map/col_pass/pallas_call | solution.py:284
  60.9 1.5 collective-permute-done.6.refs_2_
  62.4 1.5 collective-permute-done.7.refs_5_
  65.2 1.6 collective-permute-start.11
  67.0 1.7 collective-permute-start.9
  68.7 1.9 collective-permute-done.11.refs_11_
  73.7 7.5 %row_pass.3 = f32[2,1024]{1,0:T(2,128)S(1)} custom-call(bf16[8,256,1024]{2,1,0:T(8,128)(2,1)S(1)} %get-tuple-element.115.refs_0_, bf16[8,256,1024]{2,1,0:T(8,128)(2,1)S(1)} %get-tuple-element.116.refs_1_, bf16[8,256,1024]{2,1,0:T(8,128)(2,1)S(1)} %get-tuple-element.117.refs_2_, bf16[8,256,1024]{2,1,0:T(8,128)(2,1)S(1)} %get-tuple-element.118.refs_3_, ...), custom_call_target="tpu_custom_call" | custom-call | bytes 33554432 | tf_op jit(solution)/shard_map/row_pass/pallas_call | solution.py:199
  81.3 1.6 collective-permute-start.12
  82.9 2.1 collective-permute-done.12
  85.0 2.6 collective-permute-start.13
  87.6 2.0 collective-permute-done.13
  89.5 4.4 %col_pass.3 = f32[2,8,1024]{2,1,0:T(8,128)S(1)} custom-call(f32[2,1024]{1,0:T(2,128)S(1)} %add.272.total_ref, bf16[8,256,1024]{2,1,0:T(8,128)(2,1)S(1)} %get-tuple-element.115.refs_0_, bf16[8,256,1024]{2,1,0:T(8,128)(2,1)S(1)} %get-tuple-element.116.refs_1_, bf16[8,256,1024]{2,1,0:T(8,128)(2,1)S(1)} %get-tuple-element.117.refs_2_, ...), custom_call_target="tpu_custom_call" | custom-call | bytes 33554432 | tf_op jit(solution)/shard_map/col_pass/pallas_call | solution.py:284
  94.0 2.7 %collective-permute-done.14.refs_4_ = f32[2,512,256]{2,1,0:T(8,128)S(1)} collective-permute-done((f32[2,512,256]{2,1,0:T(8,128)S(1)}, f32[2,512,256]{2,1,0:T(8,128)S(1)}, u32[]{:S(2)}, u32[]{:S(2)}) %collective-permute-start.14) | collective-permute-done | bytes 1048608 | tf_op jit(solution)/shard_map/ppermute | solution.py:392
  100.0 1.6 collective-permute-start.19
  103.5 1.7 collective-permute-done.19.refs_3_
  108.6 18.1 %row_last.1 = (f32[2,1024]{1,0:T(2,128)S(1)}, f32[2,1024,256]{2,1,0:T(8,128)S(1)}) custom-call(bf16[8,8,256,1024]{3,2,1,0:T(8,128)(2,1)} %get-tuple-element.113.base_ref, bf16[8192,256]{1,0:T(8,128)(2,1)} %get-tuple-element.164.cent_ref, f32[2,8,1024]{2,1,0:T(8,128)S(1)} %add.273.refs_0_, f32[2,8,1024]{2,1,0:T(8,128)S(1)} %collective-permute-done.17.refs_1_, ...), custom_call_target="tpu_custom_call" | custom-call | bytes 67108864 | tf_op jit(solution)/shard_map/row_last/pallas_call | solution.py:243
  128.0 1.6 collective-permute-start.20
  129.7 2.0 collective-permute-done.20
  131.7 2.6 collective-permute-start.21
  134.3 1.9 collective-permute-done.21
  136.3 1.5 collective-permute-start.26
  141.2 2.2 fusion.6
  144.2 1.6 collective-permute-start.27
  145.8 2.5 pack.1.embed
  148.4 10.1 %grad_pass.2 = f32[1024,256]{1,0:T(8,128)S(1)} custom-call(bf16[1024,256]{1,0:T(8,128)(2,1)S(1)} %get-tuple-element.231.cent_ref, f32[2,2,512]{2,1,0:T(2,128)S(1)} %reshape.72.col_ref, bf16[8,2,512,256]{3,2,1,0:T(8,128)(2,1)S(1)} %pack.1.embed, f32[4,1024]{1,0:T(4,128)S(1)} %pad_maximum_fusion.3.refs_0_, f32[4,1024]{1,0:T(4,128)S(1)} %collective-permute-done.24.refs_1_, ...), custom_call_target="tpu_custom_call" | custom-call | flops 8589934592 | bytes 4194304 | tf_op jit(solution)/shard_map/grad_pass/pallas_call | solution.py:344
  159.3 10.2 %grad_pass.3 = f32[1024,256]{1,0:T(8,128)S(1)} custom-call(bf16[1024,256]{1,0:T(8,128)(2,1)S(1)} %get-tuple-element.230.cent_ref, f32[2,2,512]{2,1,0:T(2,128)S(1)} %reshape.73.col_ref, bf16[8,2,512,256]{3,2,1,0:T(8,128)(2,1)S(1)} %pack.1.embed, f32[4,1024]{1,0:T(4,128)S(1)} %pad_maximum_fusion.3.refs_0_, f32[4,1024]{1,0:T(4,128)S(1)} %collective-permute-done.24.refs_1_, ...), custom_call_target="tpu_custom_call" | custom-call | flops 8589934592 | bytes 4194304 | tf_op jit(solution)/shard_map/grad_pass/pallas_call | solution.py:344
  169.7 2.7 collective-permute-start.29
  174.4 9.8 %collective-permute-done.29 = f32[256,256]{1,0:T(8,128)S(1)} collective-permute-done((f32[256,256]{1,0:T(8,128)S(1)}, f32[256,256]{1,0:T(8,128)S(1)}, u32[]{:S(2)}, u32[]{:S(2)}) %collective-permute-start.29) | collective-permute-done | bytes 262176 | tf_op jit(solution)/shard_map/ppermute | solution.py:392
  184.2 7.1 %collective-permute-done.30 = f32[512,256]{1,0:T(8,128)S(1)} collective-permute-done((f32[512,256]{1,0:T(8,128)S(1)}, f32[512,256]{1,0:T(8,128)S(1)}, u32[]{:S(2)}, u32[]{:S(2)}) %collective-permute-start.30) | collective-permute-done | bytes 524320 | tf_op jit(solution)/shard_map/ppermute | solution.py:392
  191.3 1.4 fusion.2
  196.9 3.0 %collective-permute-start.34 = (f32[256,256]{1,0:T(8,128)S(1)}, f32[256,256]{1,0:T(8,128)S(1)}, u32[]{:S(2)}, u32[]{:S(2)}) collective-permute-start(f32[256,256]{1,0:T(8,128)S(1)} %get-tuple-element.246), channel_id=1, source_target_pairs={{0,2},{1,3},{2,0},{3,1},{4,6},{5,7},{6,4},{7,5},{8,10},{9,11},{10,... | collective-permute-start | bytes 786440 | tf_op jit(solution)/shard_map/ppermute | solution.py:392
  200.0 15.3 %collective-permute-done.33.refs_2_ = f32[256,256]{1,0:T(8,128)S(1)} collective-permute-done((f32[256,256]{1,0:T(8,128)S(1)}, f32[256,256]{1,0:T(8,128)S(1)}, u32[]{:S(2)}, u32[]{:S(2)}) %collective-permute-start.33) | collective-permute-done | bytes 262176 | tf_op jit(solution)/shard_map/ppermute | solution.py:392
  215.3 5.5 %collective-permute-done.34 = f32[256,256]{1,0:T(8,128)S(1)} collective-permute-done((f32[256,256]{1,0:T(8,128)S(1)}, f32[256,256]{1,0:T(8,128)S(1)}, u32[]{:S(2)}, u32[]{:S(2)}) %collective-permute-start.34) | collective-permute-done | bytes 262176 | tf_op jit(solution)/shard_map/ppermute | solution.py:392
  223.3 1.5 collective-permute-start.37
  224.8 15.4 %collective-permute-done.38 = f32[512,256]{1,0:T(8,128)S(1)} collective-permute-done((f32[512,256]{1,0:T(8,128)S(1)}, f32[512,256]{1,0:T(8,128)S(1)}, u32[]{:S(2)}, u32[]{:S(2)}) %collective-permute-start.38) | collective-permute-done | bytes 524320 | tf_op jit(solution)/shard_map/ppermute | solution.py:392
  242.8 10.6 %collective-permute-done.43 = f32[512,256]{1,0:T(8,128)S(1)} collective-permute-done((f32[512,256]{1,0:T(8,128)S(1)}, f32[512,256]{1,0:T(8,128)S(1)}, u32[]{:S(2)}, u32[]{:S(2)}) %collective-permute-start.43) | collective-permute-done | bytes 524320 | tf_op jit(solution)/shard_map/ppermute | solution.py:392
  257.6 1.6 collective-permute-done.44.refs_5_
  260.3 1.9 place.2
  262.6 5.9 %place.3 = f32[8192,256]{1,0:T(8,128)} custom-call(s32[16]{0:T(128)S(1)} %stack.103.at_ref, f32[512,256]{1,0:T(8,128)S(1)} %get-tuple-element.214.refs_0_, f32[512,256]{1,0:T(8,128)S(1)} %copy-done.12, f32[512,256]{1,0:T(8,128)S(1)} %get-tuple-element.216.refs_2_, f32[512,256]{1,0:T(8,128)S(1)} %copy-done.14, f32[512,256]{1,0:T(8,128)S(1)} %copy-done.10, ...), custom_call_target="tpu_custom_call" | custom-call | bytes 25165824 | tf_op jit(solution)/shard_map/place/pallas_call | solution.py:378
  (148 shorter events, 42.5 us)
Async XLA Ops:
  28.2 1.4 collective-permute-start
  29.7 6.3 %collective-permute-start.3 = (f32[2,8,1024]{2,1,0:T(8,128)S(1)}, f32[2,8,1024]{2,1,0:T(8,128)S(1)}, u32[]{:S(2)}, u32[]{:S(2)}) collective-permute-start(f32[2,8,1024]{2,1,0:T(8,128)S(1)} %add.267.refs_8_), channel_id=1, source_target_pairs={{0,24},{4,28},{8,16},{12,20},{16,8},{20,12},{24,0},{28,4},{1,25},{... | collective-permute-start | bytes 196616 | tf_op jit(solution)/shard_map/ppermute | solution.py:392
  33.5 4.3 %collective-permute-start.2 = (f32[2,8,1024]{2,1,0:T(8,128)S(1)}, f32[2,8,1024]{2,1,0:T(8,128)S(1)}, u32[]{:S(2)}, u32[]{:S(2)}) collective-permute-start(f32[2,8,1024]{2,1,0:T(8,128)S(1)} %add.267.refs_8_), channel_id=1, source_target_pairs={{0,16},{4,20},{8,24},{12,28},{16,0},{20,4},{24,8},{28,12},{1,17},{... | collective-permute-start | bytes 196616 | tf_op jit(solution)/shard_map/ppermute | solution.py:392
  34.0 4.3 %collective-permute-start.1 = (f32[2,8,1024]{2,1,0:T(8,128)S(1)}, f32[2,8,1024]{2,1,0:T(8,128)S(1)}, u32[]{:S(2)}, u32[]{:S(2)}) collective-permute-start(f32[2,8,1024]{2,1,0:T(8,128)S(1)} %add.267.refs_8_), channel_id=1, source_target_pairs={{0,8},{4,12},{8,0},{12,4},{16,24},{20,28},{24,16},{28,20},{1,9},{5... | collective-permute-start | bytes 196616 | tf_op jit(solution)/shard_map/ppermute | solution.py:392
  38.3 24.1 %collective-permute-start.6 = (f32[2,512,256]{2,1,0:T(8,128)S(1)}, f32[2,512,256]{2,1,0:T(8,128)}, u32[]{:S(2)}, u32[]{:S(2)}) collective-permute-start(f32[2,512,256]{2,1,0:T(8,128)S(1)} %get-tuple-element.165.refs_0_), channel_id=1, source_target_pairs={{0,8},{4,12},{8,0},{12,4},{16,24},{20,28},{24,16},{28,20},{1,9},{5... | collective-permute-start | bytes 3145736 | tf_op jit(solution)/shard_map/ppermute | solution.py:392
  39.1 24.8 %collective-permute-start.7 = (f32[2,512,256]{2,1,0:T(8,128)S(1)}, f32[2,512,256]{2,1,0:T(8,128)}, u32[]{:S(2)}, u32[]{:S(2)}) collective-permute-start(f32[2,512,256]{2,1,0:T(8,128)S(1)} %get-tuple-element.166.refs_1_), channel_id=1, source_target_pairs={{0,16},{4,20},{8,24},{12,28},{16,0},{20,4},{24,8},{28,12},{1,17},{... | collective-permute-start | bytes 3145736 | tf_op jit(solution)/shard_map/ppermute | solution.py:392
  47.9 3.8 %collective-permute-start.4 = (f32[4,1024]{1,0:T(4,128)S(1)}, f32[4,1024]{1,0:T(4,128)S(1)}, u32[]{:S(2)}, u32[]{:S(2)}) collective-permute-start(f32[4,1024]{1,0:T(4,128)S(1)} %pad_maximum_fusion.2), channel_id=1, source_target_pairs={{0,1},{1,0},{2,3},{3,2},{4,5},{5,4},{6,7},{7,6},{8,9},{9,8},{10,11... | collective-permute-start | bytes 49160 | tf_op jit(solution)/shard_map/ppermute | solution.py:392
  51.7 4.7 %collective-permute-start.5 = (f32[4,1024]{1,0:T(4,128)S(1)}, f32[4,1024]{1,0:T(4,128)S(1)}, u32[]{:S(2)}, u32[]{:S(2)}) collective-permute-start(f32[4,1024]{1,0:T(4,128)S(1)} %fusion.20), channel_id=1, source_target_pairs={{0,2},{1,3},{2,0},{3,1},{4,6},{5,7},{6,4},{7,5},{8,10},{9,11},{10,... | collective-permute-start | bytes 49160 | tf_op jit(solution)/shard_map/ppermute | solution.py:392
  65.2 5.5 %collective-permute-start.11 = (f32[2,8,1024]{2,1,0:T(8,128)S(1)}, f32[2,8,1024]{2,1,0:T(8,128)S(1)}, u32[]{:S(2)}, u32[]{:S(2)}) collective-permute-start(f32[2,8,1024]{2,1,0:T(8,128)S(1)} %add.270.refs_8_), channel_id=1, source_target_pairs={{0,24},{4,28},{8,16},{12,20},{16,8},{20,12},{24,0},{28,4},{1,25},{... | collective-permute-start | bytes 196616 | tf_op jit(solution)/shard_map/ppermute | solution.py:392
  66.7 5.0 %collective-permute-start.10 = (f32[2,8,1024]{2,1,0:T(8,128)S(1)}, f32[2,8,1024]{2,1,0:T(8,128)S(1)}, u32[]{:S(2)}, u32[]{:S(2)}) collective-permute-start(f32[2,8,1024]{2,1,0:T(8,128)S(1)} %add.270.refs_8_), channel_id=1, source_target_pairs={{0,16},{4,20},{8,24},{12,28},{16,0},{20,4},{24,8},{28,12},{1,17},{... | collective-permute-start | bytes 196616 | tf_op jit(solution)/shard_map/ppermute | solution.py:392
  67.0 4.7 %collective-permute-start.9 = (f32[2,8,1024]{2,1,0:T(8,128)S(1)}, f32[2,8,1024]{2,1,0:T(8,128)S(1)}, u32[]{:S(2)}, u32[]{:S(2)}) collective-permute-start(f32[2,8,1024]{2,1,0:T(8,128)S(1)} %add.270.refs_8_), channel_id=1, source_target_pairs={{0,8},{4,12},{8,0},{12,4},{16,24},{20,28},{24,16},{28,20},{1,9},{5... | collective-permute-start | bytes 196616 | tf_op jit(solution)/shard_map/ppermute | solution.py:392
  71.7 25.0 %collective-permute-start.14 = (f32[2,512,256]{2,1,0:T(8,128)S(1)}, f32[2,512,256]{2,1,0:T(8,128)S(1)}, u32[]{:S(2)}, u32[]{:S(2)}) collective-permute-start(f32[2,512,256]{2,1,0:T(8,128)S(1)} %get-tuple-element.165.refs_0_), channel_id=1, source_target_pairs={{0,16},{4,20},{8,24},{12,28},{16,0},{20,4},{24,8},{28,12},{1,17},{... | collective-permute-start | bytes 3145736 | tf_op jit(solution)/shard_map/ppermute | solution.py:392
  73.0 24.7 %collective-permute-start.15 = (f32[2,512,256]{2,1,0:T(8,128)S(1)}, f32[2,512,256]{2,1,0:T(8,128)S(1)}, u32[]{:S(2)}, u32[]{:S(2)}) collective-permute-start(f32[2,512,256]{2,1,0:T(8,128)S(1)} %get-tuple-element.166.refs_1_), channel_id=1, source_target_pairs={{0,8},{4,12},{8,0},{12,4},{16,24},{20,28},{24,16},{28,20},{1,9},{5... | collective-permute-start | bytes 3145736 | tf_op jit(solution)/shard_map/ppermute | solution.py:392
  81.3 3.7 %collective-permute-start.12 = (f32[2,1024]{1,0:T(2,128)S(1)}, f32[2,1024]{1,0:T(2,128)S(1)}, u32[]{:S(2)}, u32[]{:S(2)}) collective-permute-start(f32[2,1024]{1,0:T(2,128)S(1)} %row_pass.3), channel_id=1, source_target_pairs={{0,1},{1,0},{2,3},{3,2},{4,5},{5,4},{6,7},{7,6},{8,9},{9,8},{10,11... | collective-permute-start | bytes 24584 | tf_op jit(solution)/shard_map/ppermute | solution.py:392
  85.0 4.5 %collective-permute-start.13 = (f32[2,1024]{1,0:T(2,128)S(1)}, f32[2,1024]{1,0:T(2,128)S(1)}, u32[]{:S(2)}, u32[]{:S(2)}) collective-permute-start(f32[2,1024]{1,0:T(2,128)S(1)} %add.271), channel_id=1, source_target_pairs={{0,2},{1,3},{2,0},{3,1},{4,6},{5,7},{6,4},{7,5},{8,10},{9,11},{10,... | collective-permute-start | bytes 24584 | tf_op jit(solution)/shard_map/ppermute | solution.py:392
  100.0 5.3 %collective-permute-start.19 = (f32[2,8,1024]{2,1,0:T(8,128)S(1)}, f32[2,8,1024]{2,1,0:T(8,128)S(1)}, u32[]{:S(2)}, u32[]{:S(2)}) collective-permute-start(f32[2,8,1024]{2,1,0:T(8,128)S(1)} %add.273.refs_0_), channel_id=1, source_target_pairs={{0,24},{4,28},{8,16},{12,20},{16,8},{20,12},{24,0},{28,4},{1,25},{... | collective-permute-start | bytes 196616 | tf_op jit(solution)/shard_map/ppermute | solution.py:392
  101.5 5.0 %collective-permute-start.18 = (f32[2,8,1024]{2,1,0:T(8,128)S(1)}, f32[2,8,1024]{2,1,0:T(8,128)S(1)}, u32[]{:S(2)}, u32[]{:S(2)}) collective-permute-start(f32[2,8,1024]{2,1,0:T(8,128)S(1)} %add.273.refs_0_), channel_id=1, source_target_pairs={{0,16},{4,20},{8,24},{12,28},{16,0},{20,4},{24,8},{28,12},{1,17},{... | collective-permute-start | bytes 196616 | tf_op jit(solution)/shard_map/ppermute | solution.py:392
  102.3 4.3 %collective-permute-start.17 = (f32[2,8,1024]{2,1,0:T(8,128)S(1)}, f32[2,8,1024]{2,1,0:T(8,128)S(1)}, u32[]{:S(2)}, u32[]{:S(2)}) collective-permute-start(f32[2,8,1024]{2,1,0:T(8,128)S(1)} %add.273.refs_0_), channel_id=1, source_target_pairs={{0,8},{4,12},{8,0},{12,4},{16,24},{20,28},{24,16},{28,20},{1,9},{5... | collective-permute-start | bytes 196616 | tf_op jit(solution)/shard_map/ppermute | solution.py:392
  106.5 29.7 %collective-permute-start.22 = (f32[2,512,256]{2,1,0:T(8,128)}, f32[2,512,256]{2,1,0:T(8,128)}, u32[]{:S(2)}, u32[]{:S(2)}) collective-permute-start(f32[2,512,256]{2,1,0:T(8,128)} %collective-permute-done.6.refs_2_), channel_id=1, source_target_pairs={{0,16},{4,20},{8,24},{12,28},{16,0},{20,4},{24,8},{28,12},{1,17},{... | collective-permute-start | bytes 3145736 | tf_op jit(solution)/shard_map/ppermute | solution.py:392
  107.8 28.4 %collective-permute-start.23 = (f32[2,512,256]{2,1,0:T(8,128)}, f32[2,512,256]{2,1,0:T(8,128)}, u32[]{:S(2)}, u32[]{:S(2)}) collective-permute-start(f32[2,512,256]{2,1,0:T(8,128)} %collective-permute-done.7.refs_5_), channel_id=1, source_target_pairs={{0,8},{4,12},{8,0},{12,4},{16,24},{20,28},{24,16},{28,20},{1,9},{5... | collective-permute-start | bytes 3145736 | tf_op jit(solution)/shard_map/ppermute | solution.py:392
  128.0 3.7 %collective-permute-start.20 = (f32[2,1024]{1,0:T(2,128)S(1)}, f32[2,1024]{1,0:T(2,128)S(1)}, u32[]{:S(2)}, u32[]{:S(2)}) collective-permute-start(f32[2,1024]{1,0:T(2,128)S(1)} %get-tuple-element.157), channel_id=1, source_target_pairs={{0,1},{1,0},{2,3},{3,2},{4,5},{5,4},{6,7},{7,6},{8,9},{9,8},{10,11... | collective-permute-start | bytes 24584 | tf_op jit(solution)/shard_map/ppermute | solution.py:392
  131.7 4.5 %collective-permute-start.21 = (f32[2,1024]{1,0:T(2,128)S(1)}, f32[2,1024]{1,0:T(2,128)S(1)}, u32[]{:S(2)}, u32[]{:S(2)}) collective-permute-start(f32[2,1024]{1,0:T(2,128)S(1)} %add.274), channel_id=1, source_target_pairs={{0,2},{1,3},{2,0},{3,1},{4,6},{5,7},{6,4},{7,5},{8,10},{9,11},{10,... | collective-permute-start | bytes 24584 | tf_op jit(solution)/shard_map/ppermute | solution.py:392
  136.3 12.1 %collective-permute-start.26 = (f32[4,1024]{1,0:T(4,128)S(1)}, f32[4,1024]{1,0:T(4,128)S(1)}, u32[]{:S(2)}, u32[]{:S(2)}) collective-permute-start(f32[4,1024]{1,0:T(4,128)S(1)} %pad_maximum_fusion.3.refs_0_), channel_id=1, source_target_pairs={{0,24},{4,28},{8,16},{12,20},{16,8},{20,12},{24,0},{28,4},{1,25},{... | collective-permute-start | bytes 49160 | tf_op jit(solution)/shard_map/ppermute | solution.py:392
  137.8 10.5 %collective-permute-start.25 = (f32[4,1024]{1,0:T(4,128)S(1)}, f32[4,1024]{1,0:T(4,128)S(1)}, u32[]{:S(2)}, u32[]{:S(2)}) collective-permute-start(f32[4,1024]{1,0:T(4,128)S(1)} %pad_maximum_fusion.3.refs_0_), channel_id=1, source_target_pairs={{0,16},{4,20},{8,24},{12,28},{16,0},{20,4},{24,8},{28,12},{1,17},{... | collective-permute-start | bytes 49160 | tf_op jit(solution)/shard_map/ppermute | solution.py:392
  139.1 9.3 %collective-permute-start.24 = (f32[4,1024]{1,0:T(4,128)S(1)}, f32[4,1024]{1,0:T(4,128)S(1)}, u32[]{:S(2)}, u32[]{:S(2)}) collective-permute-start(f32[4,1024]{1,0:T(4,128)S(1)} %pad_maximum_fusion.3.refs_0_), channel_id=1, source_target_pairs={{0,8},{4,12},{8,0},{12,4},{16,24},{20,28},{24,16},{28,20},{1,9},{5... | collective-permute-start | bytes 49160 | tf_op jit(solution)/shard_map/ppermute | solution.py:392
  144.2 14.2 %collective-permute-start.27 = (f32[512,256]{1,0:T(8,128)}, f32[512,256]{1,0:T(8,128)S(1)}, u32[]{:S(2)}, u32[]{:S(2)}) collective-permute-start(f32[512,256]{1,0:T(8,128)} %get-tuple-element.240), channel_id=1, source_target_pairs={{0,1},{1,0},{2,3},{3,2},{4,5},{5,4},{6,7},{7,6},{8,9},{9,8},{10,11... | collective-permute-start | bytes 1572872 | tf_op jit(solution)/shard_map/ppermute | solution.py:392
  158.5 32.8 %collective-permute-start.28 = (f32[1024,256]{1,0:T(8,128)S(1)}, f32[1024,256]{1,0:T(8,128)S(1)}, u32[]{:S(2)}, u32[]{:S(2)}) collective-permute-start(f32[1024,256]{1,0:T(8,128)S(1)} %grad_pass.2), channel_id=1, source_target_pairs={{0,4},{4,0},{8,12},{12,8},{16,20},{20,16},{24,28},{28,24},{1,5},{5... | collective-permute-start | bytes 3145736 | tf_op jit(solution)/shard_map/ppermute | solution.py:392
  169.7 14.6 %collective-permute-start.29 = (f32[256,256]{1,0:T(8,128)S(1)}, f32[256,256]{1,0:T(8,128)S(1)}, u32[]{:S(2)}, u32[]{:S(2)}) collective-permute-start(f32[256,256]{1,0:T(8,128)S(1)} %get-tuple-element.248), channel_id=1, source_target_pairs={{0,2},{1,3},{2,0},{3,1},{4,6},{5,7},{6,4},{7,5},{8,10},{9,11},{10,... | collective-permute-start | bytes 786440 | tf_op jit(solution)/shard_map/ppermute | solution.py:392
  172.4 18.9 %collective-permute-start.30 = (f32[512,256]{1,0:T(8,128)S(1)}, f32[512,256]{1,0:T(8,128)S(1)}, u32[]{:S(2)}, u32[]{:S(2)}) collective-permute-start(f32[512,256]{1,0:T(8,128)S(1)} %get-tuple-element.238), channel_id=1, source_target_pairs={{0,1},{1,0},{2,3},{3,2},{4,5},{5,4},{6,7},{7,6},{8,9},{9,8},{10,11... | collective-permute-start | bytes 1572872 | tf_op jit(solution)/shard_map/ppermute | solution.py:392
  194.3 26.5 %collective-permute-start.32 = (f32[512,256]{1,0:T(8,128)S(1)}, f32[512,256]{1,0:T(8,128)}, u32[]{:S(2)}, u32[]{:S(2)}) collective-permute-start(f32[512,256]{1,0:T(8,128)S(1)} %get-tuple-element.216.refs_2_), channel_id=1, source_target_pairs={{0,16},{4,20},{8,24},{12,28},{16,0},{20,4},{24,8},{28,12},{1,17},{... | collective-permute-start | bytes 1572872 | tf_op jit(solution)/shard_map/ppermute | solution.py:392
  195.6 25.2 %collective-permute-start.31 = (f32[512,256]{1,0:T(8,128)S(1)}, f32[512,256]{1,0:T(8,128)S(1)}, u32[]{:S(2)}, u32[]{:S(2)}) collective-permute-start(f32[512,256]{1,0:T(8,128)S(1)} %get-tuple-element.214.refs_0_), channel_id=1, source_target_pairs={{0,8},{4,12},{8,0},{12,4},{16,24},{20,28},{24,16},{28,20},{1,9},{5... | collective-permute-start | bytes 1572872 | tf_op jit(solution)/shard_map/ppermute | solution.py:392
  196.7 18.6 %collective-permute-start.33 = (f32[256,256]{1,0:T(8,128)S(1)}, f32[256,256]{1,0:T(8,128)S(1)}, u32[]{:S(2)}, u32[]{:S(2)}) collective-permute-start(f32[256,256]{1,0:T(8,128)S(1)} %fusion.17.refs_0_), channel_id=1, source_target_pairs={{0,2},{1,3},{2,0},{3,1},{4,6},{5,7},{6,4},{7,5},{8,10},{9,11},{10,... | collective-permute-start | bytes 786440 | tf_op jit(solution)/shard_map/ppermute | solution.py:392
  196.9 23.9 %collective-permute-start.34 = (f32[256,256]{1,0:T(8,128)S(1)}, f32[256,256]{1,0:T(8,128)S(1)}, u32[]{:S(2)}, u32[]{:S(2)}) collective-permute-start(f32[256,256]{1,0:T(8,128)S(1)} %get-tuple-element.246), channel_id=1, source_target_pairs={{0,2},{1,3},{2,0},{3,1},{4,6},{5,7},{6,4},{7,5},{8,10},{9,11},{10,... | collective-permute-start | bytes 786440 | tf_op jit(solution)/shard_map/ppermute | solution.py:392
  220.8 19.5 %collective-permute-start.38 = (f32[512,256]{1,0:T(8,128)S(1)}, f32[512,256]{1,0:T(8,128)S(1)}, u32[]{:S(2)}, u32[]{:S(2)}) collective-permute-start(f32[512,256]{1,0:T(8,128)S(1)} %pad_maximum_fusion), channel_id=1, source_target_pairs={{0,1},{1,0},{2,3},{3,2},{4,5},{5,4},{6,7},{7,6},{8,9},{9,8},{10,11... | collective-permute-start | bytes 1572872 | tf_op jit(solution)/shard_map/ppermute | solution.py:392
  220.9 19.4 %collective-permute-start.35 = (f32[512,256]{1,0:T(8,128)S(1)}, f32[512,256]{1,0:T(8,128)}, u32[]{:S(2)}, u32[]{:S(2)}) collective-permute-start(f32[512,256]{1,0:T(8,128)S(1)} %get-tuple-element.214.refs_0_), channel_id=1, source_target_pairs={{0,16},{4,20},{8,24},{12,28},{16,0},{20,4},{24,8},{28,12},{1,17},{... | collective-permute-start | bytes 1572872 | tf_op jit(solution)/shard_map/ppermute | solution.py:392
  222.2 18.1 %collective-permute-start.36 = (f32[512,256]{1,0:T(8,128)S(1)}, f32[512,256]{1,0:T(8,128)}, u32[]{:S(2)}, u32[]{:S(2)}) collective-permute-start(f32[512,256]{1,0:T(8,128)S(1)} %get-tuple-element.216.refs_2_), channel_id=1, source_target_pairs={{0,8},{4,12},{8,0},{12,4},{16,24},{20,28},{24,16},{28,20},{1,9},{5... | collective-permute-start | bytes 1572872 | tf_op jit(solution)/shard_map/ppermute | solution.py:392
  223.3 17.0 %collective-permute-start.37 = (f32[256,256]{1,0:T(8,128)S(1)}, f32[256,256]{1,0:T(8,128)S(1)}, u32[]{:S(2)}, u32[]{:S(2)}) collective-permute-start(f32[256,256]{1,0:T(8,128)S(1)} %fusion.14.refs_4_), channel_id=1, source_target_pairs={{0,2},{1,3},{2,0},{3,1},{4,6},{5,7},{6,4},{7,5},{8,10},{9,11},{10,... | collective-permute-start | bytes 786440 | tf_op jit(solution)/shard_map/ppermute | solution.py:392
  240.4 13.0 %collective-permute-start.43 = (f32[512,256]{1,0:T(8,128)S(1)}, f32[512,256]{1,0:T(8,128)S(1)}, u32[]{:S(2)}, u32[]{:S(2)}) collective-permute-start(f32[512,256]{1,0:T(8,128)S(1)} %pad_maximum_fusion.1), channel_id=1, source_target_pairs={{0,1},{1,0},{2,3},{3,2},{4,5},{5,4},{6,7},{7,6},{8,9},{9,8},{10,11... | collective-permute-start | bytes 1572872 | tf_op jit(solution)/shard_map/ppermute | solution.py:392
  240.4 12.9 %collective-permute-start.41 = (f32[512,256]{1,0:T(8,128)S(1)}, f32[512,256]{1,0:T(8,128)S(1)}, u32[]{:S(2)}, u32[]{:S(2)}) collective-permute-start(f32[512,256]{1,0:T(8,128)S(1)} %get-tuple-element.214.refs_0_), channel_id=1, source_target_pairs={{0,4},{4,0},{8,12},{12,8},{16,20},{20,16},{24,28},{28,24},{1,5},{5... | collective-permute-start | bytes 1572872 | tf_op jit(solution)/shard_map/ppermute | solution.py:392
  240.5 14.4 %collective-permute-start.39 = (f32[512,256]{1,0:T(8,128)S(1)}, f32[512,256]{1,0:T(8,128)}, u32[]{:S(2)}, u32[]{:S(2)}) collective-permute-start(f32[512,256]{1,0:T(8,128)S(1)} %collective-permute-done.31.refs_4_), channel_id=1, source_target_pairs={{0,16},{4,20},{8,24},{12,28},{16,0},{20,4},{24,8},{28,12},{1,17},{... | collective-permute-start | bytes 1572872 | tf_op jit(solution)/shard_map/ppermute | solution.py:392
  241.9 13.1 %collective-permute-start.42 = (f32[512,256]{1,0:T(8,128)S(1)}, f32[512,256]{1,0:T(8,128)S(1)}, u32[]{:S(2)}, u32[]{:S(2)}) collective-permute-start(f32[512,256]{1,0:T(8,128)S(1)} %get-tuple-element.216.refs_2_), channel_id=1, source_target_pairs={{0,4},{4,0},{8,12},{12,8},{16,20},{20,16},{24,28},{28,24},{1,5},{5... | collective-permute-start | bytes 1572872 | tf_op jit(solution)/shard_map/ppermute | solution.py:392
  242.0 14.5 %collective-permute-start.40 = (f32[512,256]{1,0:T(8,128)}, f32[512,256]{1,0:T(8,128)}, u32[]{:S(2)}, u32[]{:S(2)}) collective-permute-start(f32[512,256]{1,0:T(8,128)} %collective-permute-done.32.refs_10_), channel_id=1, source_target_pairs={{0,8},{4,12},{8,0},{12,4},{16,24},{20,28},{24,16},{28,20},{1,9},{5... | collective-permute-start | bytes 1572872 | tf_op jit(solution)/shard_map/ppermute | solution.py:392
  256.5 2.6 collective-permute-start.44
  256.5 5.7 %collective-permute-start.45 = (f32[512,256]{1,0:T(8,128)}, f32[512,256]{1,0:T(8,128)}, u32[]{:S(2)}, u32[]{:S(2)}) collective-permute-start(f32[512,256]{1,0:T(8,128)} %collective-permute-done.36.refs_6_), channel_id=1, source_target_pairs={{0,4},{4,0},{8,12},{12,8},{16,20},{20,16},{24,28},{28,24},{1,5},{5... | collective-permute-start | bytes 1572872 | tf_op jit(solution)/shard_map/ppermute | solution.py:392
  257.0 5.2 %collective-permute-start.46 = (f32[512,256]{1,0:T(8,128)}, f32[512,256]{1,0:T(8,128)}, u32[]{:S(2)}, u32[]{:S(2)}) collective-permute-start(f32[512,256]{1,0:T(8,128)} %collective-permute-done.35.refs_8_), channel_id=1, source_target_pairs={{0,4},{4,0},{8,12},{12,8},{16,20},{20,16},{24,28},{28,24},{1,5},{5... | collective-permute-start | bytes 1572872 | tf_op jit(solution)/shard_map/ppermute | solution.py:392
  257.0 5.2 %collective-permute-start.47 = (f32[512,256]{1,0:T(8,128)}, f32[512,256]{1,0:T(8,128)}, u32[]{:S(2)}, u32[]{:S(2)}) collective-permute-start(f32[512,256]{1,0:T(8,128)} %collective-permute-done.32.refs_10_), channel_id=1, source_target_pairs={{0,4},{4,0},{8,12},{12,8},{16,20},{20,16},{24,28},{28,24},{1,5},{5... | collective-permute-start | bytes 1572872 | tf_op jit(solution)/shard_map/ppermute | solution.py:392
  257.6 4.7 %collective-permute-start.48 = (f32[512,256]{1,0:T(8,128)}, f32[512,256]{1,0:T(8,128)}, u32[]{:S(2)}, u32[]{:S(2)}) collective-permute-start(f32[512,256]{1,0:T(8,128)} %collective-permute-done.39.refs_12_), channel_id=1, source_target_pairs={{0,4},{4,0},{8,12},{12,8},{16,20},{20,16},{24,28},{28,24},{1,5},{5... | collective-permute-start | bytes 1572872 | tf_op jit(solution)/shard_map/ppermute | solution.py:392
  259.9 2.6 collective-permute-start.49
  (21 other events, 127.5 us)

commit v6 on v5

--- a/solution.py
+++ b/solution.py
@@ -440,9 +440,14 @@
 
 
 def halve_over_proto(x, n, m=1):
+    keep, give = halves_over_proto(x, m)
+    return keep, swap(give, "proto", n, m)
+
+
+def halves_over_proto(x, m):
     size = x.shape[0] // 2
     side = (lax.axis_index("proto") // m) % 2
-    return cut(x, side * size, size), swap(cut(x, (1 - side) * size, size), "proto", n, m)
+    return cut(x, side * size, size), cut(x, (1 - side) * size, size)
 
 
 def home(i, n, size):
@@ -531,8 +536,11 @@
         (theirs, pair, gf[1], features, prototypes)
     )
     theirs = swap(theirs, "batch", nb, 1)
-    pair = halve_over_proto(pair[0] + pair[1], npr, 2)
-    pair_late = halve_over_proto(late, npr, 1)
+    keep, give = halves_over_proto(pair[0] + pair[1], 2)
+    keep_late, give_late = halves_over_proto(late, 1)
+    give, give_late, embeds = lax.optimization_barrier((give, give_late, embeds))
+    pair = keep, swap(give, "proto", npr, 2)
+    pair_late = keep_late, swap(give_late, "proto", npr, 1)
     mine = grads(chip * share + core * half)
     mine, theirs, pair, pair_late = lax.optimization_barrier((mine, theirs, pair, pair_late))
     grad = norm_back(mine + theirs, cut(prototypes, chip * share + core * half, half))

time: 272 us -> 256 us (0.941)
  waiting for transfers between devices: 98.5 us -> 83.4 us
    ppermute x50, waiting for transfers between devices: 98.5 us -> 83.4 us  [swap(): return lax.ppermute(x, axis, [(i, i ^ m) for i in range(n)])]
    unnamed x39 -> x37, local copies, waits for them, and re-layouts: 7.73 us -> 6.97 us
  transfers between devices with their start and end apart: 50 -> 50, of which waited for: 29 -> 29; matrix products, arithmetic and copies ran while one was open for 3% -> 3% of each run, Pallas kernels for 25% -> 26%
where the time goes in v6:
time: 256 us; the launch traced here: 253 us
  Pallas kernels  99.1 us (39%)
  waiting for transfers between devices  83.4 us (33%)
  starting transfers between devices  51.5 us (20%)
  local copies, waits for them, and re-layouts  9.73 us (4%)
  other arithmetic  7.49 us (3%)
    ppermute x50, waiting for transfers between devices, swap(): return lax.ppermute(x, axis, [(i, i ^ m) for i in range(n)])  83.4 us
    ppermute x50, starting transfers between devices, swap(): return lax.ppermute(x, axis, [(i, i ^ m) for i in range(n)])  51.5 us
    pallas_call x1, Pallas kernels, first(): pl.pallas_call(first_kernel, grid=(n,), in_specs=[in_vmem(), pl.BlockSpec...  26.4 us
    pallas_call x2, Pallas kernels, grad_pass(): pl.pallas_call(grad_kernel, grid=(n,), in_specs=[pl.BlockSpec((kt, width)...  20.3 us
    pallas_call x1, Pallas kernels, row_last(): pl.pallas_call(row_last_kernel, grid=(n,), in_specs=[pl.BlockSpec((m, 1,...  18.1 us
    pallas_call x2, Pallas kernels, row_pass(): pl.pallas_call(lambda *refs: row_kernel(m, *refs), in_specs=[in_vmem()] *...  15 us
    pallas_call x2, Pallas kernels, col_pass(): pl.pallas_call(col_kernel, in_specs=[in_vmem()] * (m + 1), out_specs=in_v...  8.89 us
    pallas_call x2, Pallas kernels, place(): pl.pallas_call(place_kernel, in_specs=[pl.BlockSpec(memory_space=pltpu.SM...  7.82 us
  transfers between devices with their start and end apart: 50, of which 29 were waited for; matrix products, arithmetic and copies ran while one was open for 3% of the time, Pallas kernels for 26%

profile of v6, /device:TPU:0, one launch (start us, length us, event | category | flops | bytes accessed | tf_op | source)
XLA Modules:
  0.0 252.7 jit_solution(15986433002916606810)
XLA Ops:
  1.9 26.4 %first.1 = (f32[2,512,256]{2,1,0:T(8,128)S(1)}, f32[2,512,256]{2,1,0:T(8,128)S(1)}, bf16[8192,256]{1,0:T(8,128)(2,1)}, f32[2,8,1024]{2,1,0:T(8,128)S(1)}, f32[2,...) custom-call(bf16[2,1024,256]{2,1,0:T(8,128)(2,1)S(1)} %copy-done.7, ...), custom_call_target="tpu_custom_call" | custom-call | flops 34359738368 | tf_op jit(solution)/shard_map/first/pallas_call | solution.py:121
  29.7 3.9 %collective-permute-start.3 = (f32[2,8,1024]{2,1,0:T(8,128)S(1)}, f32[2,8,1024]{2,1,0:T(8,128)S(1)}, u32[]{:S(2)}, u32[]{:S(2)}) collective-permute-start(f32[2,8,1024]{2,1,0:T(8,128)S(1)} %add.267.refs_8_), channel_id=1, source_target_pairs={{0,24},{4,28},{8,16},{12,20},{16,8},{20,12},{24,0},{28,4},{1,25},{... | collective-permute-start | bytes 196616 | tf_op jit(solution)/shard_map/ppermute | solution.py:392
  34.2 1.8 collective-permute-done.3.refs_11_
  35.9 1.9 collective-permute-done.2.refs_10_
  40.4 7.5 %row_pass.2 = f32[2,1024]{1,0:T(2,128)S(1)} custom-call(bf16[8,256,1024]{2,1,0:T(8,128)(2,1)S(1)} %get-tuple-element.118.refs_0_, bf16[8,256,1024]{2,1,0:T(8,128)(2,1)S(1)} %get-tuple-element.119.refs_1_, bf16[8,256,1024]{2,1,0:T(8,128)(2,1)S(1)} %get-tuple-element.120.refs_2_, bf16[8,256,1024]{2,1,0:T(8,128)(2,1)S(1)} %get-tuple-element.121.refs_3_, ...), custom_call_target="tpu_custom_call" | custom-call | bytes 33554432 | tf_op jit(solution)/shard_map/row_pass/pallas_call | solution.py:199
  47.9 1.6 collective-permute-start.4
  49.5 2.2 collective-permute-done.4
  51.7 2.6 %collective-permute-start.5 = (f32[4,1024]{1,0:T(4,128)S(1)}, f32[4,1024]{1,0:T(4,128)S(1)}, u32[]{:S(2)}, u32[]{:S(2)}) collective-permute-start(f32[4,1024]{1,0:T(4,128)S(1)} %fusion.20), channel_id=1, source_target_pairs={{0,2},{1,3},{2,0},{3,1},{4,6},{5,7},{6,4},{7,5},{8,10},{9,11},{10,... | collective-permute-start | bytes 49160 | tf_op jit(solution)/shard_map/ppermute | solution.py:392
  54.4 2.1 collective-permute-done.5
  56.4 4.4 %col_pass.2 = f32[2,8,1024]{2,1,0:T(8,128)S(1)} custom-call(f32[2,1024]{1,0:T(2,128)S(1)} %get-tuple-element.261.total_ref, bf16[8,256,1024]{2,1,0:T(8,128)(2,1)S(1)} %get-tuple-element.118.refs_0_, bf16[8,256,1024]{2,1,0:T(8,128)(2,1)S(1)} %get-tuple-element.119.refs_1_, bf16[8,256,1024]{2,1,0:T(8,128)(2,1)S(1)} %get-tuple-element.120.refs_2_, ...), custom_call_target="tpu_custom_call" | custom-call | bytes 33554432 | tf_op jit(solution)/shard_map/col_pass/pallas_call | solution.py:284
  60.9 1.5 collective-permute-done.6.refs_2_
  62.4 1.5 collective-permute-done.7.refs_5_
  65.1 1.6 collective-permute-start.11
  67.0 1.7 collective-permute-start.9
  68.7 1.9 collective-permute-done.11.refs_11_
  73.7 7.5 %row_pass.3 = f32[2,1024]{1,0:T(2,128)S(1)} custom-call(bf16[8,256,1024]{2,1,0:T(8,128)(2,1)S(1)} %get-tuple-element.118.refs_0_, bf16[8,256,1024]{2,1,0:T(8,128)(2,1)S(1)} %get-tuple-element.119.refs_1_, bf16[8,256,1024]{2,1,0:T(8,128)(2,1)S(1)} %get-tuple-element.120.refs_2_, bf16[8,256,1024]{2,1,0:T(8,128)(2,1)S(1)} %get-tuple-element.121.refs_3_, ...), custom_call_target="tpu_custom_call" | custom-call | bytes 33554432 | tf_op jit(solution)/shard_map/row_pass/pallas_call | solution.py:199
  81.2 1.6 collective-permute-start.12
  82.9 2.1 collective-permute-done.12
  85.0 2.6 %collective-permute-start.13 = (f32[2,1024]{1,0:T(2,128)S(1)}, f32[2,1024]{1,0:T(2,128)S(1)}, u32[]{:S(2)}, u32[]{:S(2)}) collective-permute-start(f32[2,1024]{1,0:T(2,128)S(1)} %add.271), channel_id=1, source_target_pairs={{0,2},{1,3},{2,0},{3,1},{4,6},{5,7},{6,4},{7,5},{8,10},{9,11},{10,... | collective-permute-start | bytes 24584 | tf_op jit(solution)/shard_map/ppermute | solution.py:392
  87.5 2.0 collective-permute-done.13
  89.5 4.4 %col_pass.3 = f32[2,8,1024]{2,1,0:T(8,128)S(1)} custom-call(f32[2,1024]{1,0:T(2,128)S(1)} %add.272.total_ref, bf16[8,256,1024]{2,1,0:T(8,128)(2,1)S(1)} %get-tuple-element.118.refs_0_, bf16[8,256,1024]{2,1,0:T(8,128)(2,1)S(1)} %get-tuple-element.119.refs_1_, bf16[8,256,1024]{2,1,0:T(8,128)(2,1)S(1)} %get-tuple-element.120.refs_2_, ...), custom_call_target="tpu_custom_call" | custom-call | bytes 33554432 | tf_op jit(solution)/shard_map/col_pass/pallas_call | solution.py:284
  94.0 2.7 %collective-permute-done.14.refs_4_ = f32[2,512,256]{2,1,0:T(8,128)S(1)} collective-permute-done((f32[2,512,256]{2,1,0:T(8,128)S(1)}, f32[2,512,256]{2,1,0:T(8,128)S(1)}, u32[]{:S(2)}, u32[]{:S(2)}) %collective-permute-start.14) | collective-permute-done | bytes 1048608 | tf_op jit(solution)/shard_map/ppermute | solution.py:392
  99.9 1.6 collective-permute-start.19
  103.5 1.7 collective-permute-done.19.refs_3_
  108.5 18.1 %row_last.1 = (f32[2,1024]{1,0:T(2,128)S(1)}, f32[2,1024,256]{2,1,0:T(8,128)S(1)}) custom-call(bf16[8,8,256,1024]{3,2,1,0:T(8,128)(2,1)} %get-tuple-element.116.base_ref, bf16[8192,256]{1,0:T(8,128)(2,1)} %get-tuple-element.167.cent_ref, f32[2,8,1024]{2,1,0:T(8,128)S(1)} %add.273.refs_0_, f32[2,8,1024]{2,1,0:T(8,128)S(1)} %collective-permute-done.17.refs_1_, ...), custom_call_target="tpu_custom_call" | custom-call | bytes 67108864 | tf_op jit(solution)/shard_map/row_last/pallas_call | solution.py:243
  128.0 1.6 collective-permute-start.20
  129.7 2.0 collective-permute-done.20
  131.7 2.6 %collective-permute-start.21 = (f32[2,1024]{1,0:T(2,128)S(1)}, f32[2,1024]{1,0:T(2,128)S(1)}, u32[]{:S(2)}, u32[]{:S(2)}) collective-permute-start(f32[2,1024]{1,0:T(2,128)S(1)} %add.274), channel_id=1, source_target_pairs={{0,2},{1,3},{2,0},{3,1},{4,6},{5,7},{6,4},{7,5},{8,10},{9,11},{10,... | collective-permute-start | bytes 24584 | tf_op jit(solution)/shard_map/ppermute | solution.py:392
  134.3 1.9 collective-permute-done.21
  136.3 1.5 collective-permute-start.26
  141.2 2.2 fusion.6
  144.2 1.6 collective-permute-start.27
  145.8 2.5 %pack.1.embed = bf16[8,2,512,256]{3,2,1,0:T(8,128)(2,1)S(1)} custom-call(f32[2,512,256]{2,1,0:T(8,128)S(1)} %get-tuple-element.168.refs_0_, f32[2,512,256]{2,1,0:T(8,128)S(1)} %copy-done.2, f32[2,512,256]{2,1,0:T(8,128)} %collective-permute-done.6.refs_2_, f32[2,512,256]{2,1,0:T(8,128)S(1)} %copy-done.6, f32[2,512,256]{2,1,0:T(8,128)S(1)} %copy-done.4, ...), custom_call_target="tpu_custom_call" | custom-call | bytes 12582912 | tf_op jit(solution)/shard_map/pack/pallas_call | solution.py:304
  148.4 10.1 %grad_pass.2 = f32[1024,256]{1,0:T(8,128)S(1)} custom-call(bf16[1024,256]{1,0:T(8,128)(2,1)S(1)} %get-tuple-element.237.cent_ref, f32[2,2,512]{2,1,0:T(2,128)S(1)} %reshape.72.col_ref, bf16[8,2,512,256]{3,2,1,0:T(8,128)(2,1)S(1)} %pack.1.embed, f32[4,1024]{1,0:T(4,128)S(1)} %pad_maximum_fusion.3.refs_0_, f32[4,1024]{1,0:T(4,128)S(1)} %collective-permute-done.24.refs_1_, ...), custom_call_target="tpu_custom_call" | custom-call | flops 8589934592 | bytes 4194304 | tf_op jit(solution)/shard_map/grad_pass/pallas_call | solution.py:344
  158.7 2.6 %collective-permute-start.29 = (f32[256,256]{1,0:T(8,128)S(1)}, f32[256,256]{1,0:T(8,128)S(1)}, u32[]{:S(2)}, u32[]{:S(2)}) collective-permute-start(f32[256,256]{1,0:T(8,128)S(1)} %get-tuple-element.185), channel_id=1, source_target_pairs={{0,2},{1,3},{2,0},{3,1},{4,6},{5,7},{6,4},{7,5},{8,10},{9,11},{10,... | collective-permute-start | bytes 786440 | tf_op jit(solution)/shard_map/ppermute | solution.py:392
  161.8 10.2 %grad_pass.3 = f32[1024,256]{1,0:T(8,128)S(1)} custom-call(bf16[1024,256]{1,0:T(8,128)(2,1)S(1)} %get-tuple-element.236.cent_ref, f32[2,2,512]{2,1,0:T(2,128)S(1)} %reshape.73.col_ref, bf16[8,2,512,256]{3,2,1,0:T(8,128)(2,1)S(1)} %pack.1.embed, f32[4,1024]{1,0:T(4,128)S(1)} %pad_maximum_fusion.3.refs_0_, f32[4,1024]{1,0:T(4,128)S(1)} %collective-permute-done.24.refs_1_, ...), custom_call_target="tpu_custom_call" | custom-call | flops 8589934592 | bytes 4194304 | tf_op jit(solution)/shard_map/grad_pass/pallas_call | solution.py:344
  173.6 3.2 %collective-permute-done.30 = f32[512,256]{1,0:T(8,128)S(1)} collective-permute-done((f32[512,256]{1,0:T(8,128)S(1)}, f32[512,256]{1,0:T(8,128)S(1)}, u32[]{:S(2)}, u32[]{:S(2)}) %collective-permute-start.30) | collective-permute-done | bytes 524320 | tf_op jit(solution)/shard_map/ppermute | solution.py:392
  176.8 1.4 fusion.2
  182.3 3.0 %collective-permute-start.34 = (f32[256,256]{1,0:T(8,128)S(1)}, f32[256,256]{1,0:T(8,128)S(1)}, u32[]{:S(2)}, u32[]{:S(2)}) collective-permute-start(f32[256,256]{1,0:T(8,128)S(1)} %get-tuple-element.252), channel_id=1, source_target_pairs={{0,2},{1,3},{2,0},{3,1},{4,6},{5,7},{6,4},{7,5},{8,10},{9,11},{10,... | collective-permute-start | bytes 786440 | tf_op jit(solution)/shard_map/ppermute | solution.py:392
  185.4 15.1 %collective-permute-done.33.refs_2_ = f32[256,256]{1,0:T(8,128)S(1)} collective-permute-done((f32[256,256]{1,0:T(8,128)S(1)}, f32[256,256]{1,0:T(8,128)S(1)}, u32[]{:S(2)}, u32[]{:S(2)}) %collective-permute-start.33) | collective-permute-done | bytes 262176 | tf_op jit(solution)/shard_map/ppermute | solution.py:392
  200.5 4.8 %collective-permute-done.34 = f32[256,256]{1,0:T(8,128)S(1)} collective-permute-done((f32[256,256]{1,0:T(8,128)S(1)}, f32[256,256]{1,0:T(8,128)S(1)}, u32[]{:S(2)}, u32[]{:S(2)}) %collective-permute-start.34) | collective-permute-done | bytes 262176 | tf_op jit(solution)/shard_map/ppermute | solution.py:392
  207.9 1.5 collective-permute-start.37
  209.3 14.8 %collective-permute-done.38 = f32[512,256]{1,0:T(8,128)S(1)} collective-permute-done((f32[512,256]{1,0:T(8,128)S(1)}, f32[512,256]{1,0:T(8,128)S(1)}, u32[]{:S(2)}, u32[]{:S(2)}) %collective-permute-start.38) | collective-permute-done | bytes 524320 | tf_op jit(solution)/shard_map/ppermute | solution.py:392
  226.8 9.8 %collective-permute-done.43 = f32[512,256]{1,0:T(8,128)S(1)} collective-permute-done((f32[512,256]{1,0:T(8,128)S(1)}, f32[512,256]{1,0:T(8,128)S(1)}, u32[]{:S(2)}, u32[]{:S(2)}) %collective-permute-start.43) | collective-permute-done | bytes 524320 | tf_op jit(solution)/shard_map/ppermute | solution.py:392
  237.4 1.5 collective-permute-done.39.refs_12_
  241.6 1.6 collective-permute-done.44.refs_5_
  244.3 1.9 place.2
  246.6 5.9 %place.3 = f32[8192,256]{1,0:T(8,128)} custom-call(s32[16]{0:T(128)S(1)} %stack.103.at_ref, f32[512,256]{1,0:T(8,128)S(1)} %get-tuple-element.220.refs_0_, f32[512,256]{1,0:T(8,128)S(1)} %copy-done.12, f32[512,256]{1,0:T(8,128)S(1)} %get-tuple-element.222.refs_2_, f32[512,256]{1,0:T(8,128)S(1)} %copy-done.14, f32[512,256]{1,0:T(8,128)S(1)} %copy-done.10, ...), custom_call_target="tpu_custom_call" | custom-call | bytes 25165824 | tf_op jit(solution)/shard_map/place/pallas_call | solution.py:378
  (146 shorter events, 40.9 us)
Async XLA Ops:
  28.2 1.4 collective-permute-start
  29.7 6.3 %collective-permute-start.3 = (f32[2,8,1024]{2,1,0:T(8,128)S(1)}, f32[2,8,1024]{2,1,0:T(8,128)S(1)}, u32[]{:S(2)}, u32[]{:S(2)}) collective-permute-start(f32[2,8,1024]{2,1,0:T(8,128)S(1)} %add.267.refs_8_), channel_id=1, source_target_pairs={{0,24},{4,28},{8,16},{12,20},{16,8},{20,12},{24,0},{28,4},{1,25},{... | collective-permute-start | bytes 196616 | tf_op jit(solution)/shard_map/ppermute | solution.py:392
  33.5 4.3 %collective-permute-start.2 = (f32[2,8,1024]{2,1,0:T(8,128)S(1)}, f32[2,8,1024]{2,1,0:T(8,128)S(1)}, u32[]{:S(2)}, u32[]{:S(2)}) collective-permute-start(f32[2,8,1024]{2,1,0:T(8,128)S(1)} %add.267.refs_8_), channel_id=1, source_target_pairs={{0,16},{4,20},{8,24},{12,28},{16,0},{20,4},{24,8},{28,12},{1,17},{... | collective-permute-start | bytes 196616 | tf_op jit(solution)/shard_map/ppermute | solution.py:392
  34.0 4.3 %collective-permute-start.1 = (f32[2,8,1024]{2,1,0:T(8,128)S(1)}, f32[2,8,1024]{2,1,0:T(8,128)S(1)}, u32[]{:S(2)}, u32[]{:S(2)}) collective-permute-start(f32[2,8,1024]{2,1,0:T(8,128)S(1)} %add.267.refs_8_), channel_id=1, source_target_pairs={{0,8},{4,12},{8,0},{12,4},{16,24},{20,28},{24,16},{28,20},{1,9},{5... | collective-permute-start | bytes 196616 | tf_op jit(solution)/shard_map/ppermute | solution.py:392
  38.3 24.1 %collective-permute-start.6 = (f32[2,512,256]{2,1,0:T(8,128)S(1)}, f32[2,512,256]{2,1,0:T(8,128)}, u32[]{:S(2)}, u32[]{:S(2)}) collective-permute-start(f32[2,512,256]{2,1,0:T(8,128)S(1)} %get-tuple-element.168.refs_0_), channel_id=1, source_target_pairs={{0,8},{4,12},{8,0},{12,4},{16,24},{20,28},{24,16},{28,20},{1,9},{5... | collective-permute-start | bytes 3145736 | tf_op jit(solution)/shard_map/ppermute | solution.py:392
  39.1 24.8 %collective-permute-start.7 = (f32[2,512,256]{2,1,0:T(8,128)S(1)}, f32[2,512,256]{2,1,0:T(8,128)}, u32[]{:S(2)}, u32[]{:S(2)}) collective-permute-start(f32[2,512,256]{2,1,0:T(8,128)S(1)} %get-tuple-element.169.refs_1_), channel_id=1, source_target_pairs={{0,16},{4,20},{8,24},{12,28},{16,0},{20,4},{24,8},{28,12},{1,17},{... | collective-permute-start | bytes 3145736 | tf_op jit(solution)/shard_map/ppermute | solution.py:392
  47.9 3.8 %collective-permute-start.4 = (f32[4,1024]{1,0:T(4,128)S(1)}, f32[4,1024]{1,0:T(4,128)S(1)}, u32[]{:S(2)}, u32[]{:S(2)}) collective-permute-start(f32[4,1024]{1,0:T(4,128)S(1)} %pad_maximum_fusion.2), channel_id=1, source_target_pairs={{0,1},{1,0},{2,3},{3,2},{4,5},{5,4},{6,7},{7,6},{8,9},{9,8},{10,11... | collective-permute-start | bytes 49160 | tf_op jit(solution)/shard_map/ppermute | solution.py:392
  51.7 4.7 %collective-permute-start.5 = (f32[4,1024]{1,0:T(4,128)S(1)}, f32[4,1024]{1,0:T(4,128)S(1)}, u32[]{:S(2)}, u32[]{:S(2)}) collective-permute-start(f32[4,1024]{1,0:T(4,128)S(1)} %fusion.20), channel_id=1, source_target_pairs={{0,2},{1,3},{2,0},{3,1},{4,6},{5,7},{6,4},{7,5},{8,10},{9,11},{10,... | collective-permute-start | bytes 49160 | tf_op jit(solution)/shard_map/ppermute | solution.py:392
  65.1 5.5 %collective-permute-start.11 = (f32[2,8,1024]{2,1,0:T(8,128)S(1)}, f32[2,8,1024]{2,1,0:T(8,128)S(1)}, u32[]{:S(2)}, u32[]{:S(2)}) collective-permute-start(f32[2,8,1024]{2,1,0:T(8,128)S(1)} %add.270.refs_8_), channel_id=1, source_target_pairs={{0,24},{4,28},{8,16},{12,20},{16,8},{20,12},{24,0},{28,4},{1,25},{... | collective-permute-start | bytes 196616 | tf_op jit(solution)/shard_map/ppermute | solution.py:392
  66.7 5.0 %collective-permute-start.10 = (f32[2,8,1024]{2,1,0:T(8,128)S(1)}, f32[2,8,1024]{2,1,0:T(8,128)S(1)}, u32[]{:S(2)}, u32[]{:S(2)}) collective-permute-start(f32[2,8,1024]{2,1,0:T(8,128)S(1)} %add.270.refs_8_), channel_id=1, source_target_pairs={{0,16},{4,20},{8,24},{12,28},{16,0},{20,4},{24,8},{28,12},{1,17},{... | collective-permute-start | bytes 196616 | tf_op jit(solution)/shard_map/ppermute | solution.py:392
  67.0 4.7 %collective-permute-start.9 = (f32[2,8,1024]{2,1,0:T(8,128)S(1)}, f32[2,8,1024]{2,1,0:T(8,128)S(1)}, u32[]{:S(2)}, u32[]{:S(2)}) collective-permute-start(f32[2,8,1024]{2,1,0:T(8,128)S(1)} %add.270.refs_8_), channel_id=1, source_target_pairs={{0,8},{4,12},{8,0},{12,4},{16,24},{20,28},{24,16},{28,20},{1,9},{5... | collective-permute-start | bytes 196616 | tf_op jit(solution)/shard_map/ppermute | solution.py:392
  71.7 25.0 %collective-permute-start.14 = (f32[2,512,256]{2,1,0:T(8,128)S(1)}, f32[2,512,256]{2,1,0:T(8,128)S(1)}, u32[]{:S(2)}, u32[]{:S(2)}) collective-permute-start(f32[2,512,256]{2,1,0:T(8,128)S(1)} %get-tuple-element.168.refs_0_), channel_id=1, source_target_pairs={{0,16},{4,20},{8,24},{12,28},{16,0},{20,4},{24,8},{28,12},{1,17},{... | collective-permute-start | bytes 3145736 | tf_op jit(solution)/shard_map/ppermute | solution.py:392
  73.0 24.7 %collective-permute-start.15 = (f32[2,512,256]{2,1,0:T(8,128)S(1)}, f32[2,512,256]{2,1,0:T(8,128)S(1)}, u32[]{:S(2)}, u32[]{:S(2)}) collective-permute-start(f32[2,512,256]{2,1,0:T(8,128)S(1)} %get-tuple-element.169.refs_1_), channel_id=1, source_target_pairs={{0,8},{4,12},{8,0},{12,4},{16,24},{20,28},{24,16},{28,20},{1,9},{5... | collective-permute-start | bytes 3145736 | tf_op jit(solution)/shard_map/ppermute | solution.py:392
  81.2 3.7 %collective-permute-start.12 = (f32[2,1024]{1,0:T(2,128)S(1)}, f32[2,1024]{1,0:T(2,128)S(1)}, u32[]{:S(2)}, u32[]{:S(2)}) collective-permute-start(f32[2,1024]{1,0:T(2,128)S(1)} %row_pass.3), channel_id=1, source_target_pairs={{0,1},{1,0},{2,3},{3,2},{4,5},{5,4},{6,7},{7,6},{8,9},{9,8},{10,11... | collective-permute-start | bytes 24584 | tf_op jit(solution)/shard_map/ppermute | solution.py:392
  85.0 4.5 %collective-permute-start.13 = (f32[2,1024]{1,0:T(2,128)S(1)}, f32[2,1024]{1,0:T(2,128)S(1)}, u32[]{:S(2)}, u32[]{:S(2)}) collective-permute-start(f32[2,1024]{1,0:T(2,128)S(1)} %add.271), channel_id=1, source_target_pairs={{0,2},{1,3},{2,0},{3,1},{4,6},{5,7},{6,4},{7,5},{8,10},{9,11},{10,... | collective-permute-start | bytes 24584 | tf_op jit(solution)/shard_map/ppermute | solution.py:392
  99.9 5.3 %collective-permute-start.19 = (f32[2,8,1024]{2,1,0:T(8,128)S(1)}, f32[2,8,1024]{2,1,0:T(8,128)S(1)}, u32[]{:S(2)}, u32[]{:S(2)}) collective-permute-start(f32[2,8,1024]{2,1,0:T(8,128)S(1)} %add.273.refs_0_), channel_id=1, source_target_pairs={{0,24},{4,28},{8,16},{12,20},{16,8},{20,12},{24,0},{28,4},{1,25},{... | collective-permute-start | bytes 196616 | tf_op jit(solution)/shard_map/ppermute | solution.py:392
  101.5 5.0 %collective-permute-start.18 = (f32[2,8,1024]{2,1,0:T(8,128)S(1)}, f32[2,8,1024]{2,1,0:T(8,128)S(1)}, u32[]{:S(2)}, u32[]{:S(2)}) collective-permute-start(f32[2,8,1024]{2,1,0:T(8,128)S(1)} %add.273.refs_0_), channel_id=1, source_target_pairs={{0,16},{4,20},{8,24},{12,28},{16,0},{20,4},{24,8},{28,12},{1,17},{... | collective-permute-start | bytes 196616 | tf_op jit(solution)/shard_map/ppermute | solution.py:392
  102.2 4.3 %collective-permute-start.17 = (f32[2,8,1024]{2,1,0:T(8,128)S(1)}, f32[2,8,1024]{2,1,0:T(8,128)S(1)}, u32[]{:S(2)}, u32[]{:S(2)}) collective-permute-start(f32[2,8,1024]{2,1,0:T(8,128)S(1)} %add.273.refs_0_), channel_id=1, source_target_pairs={{0,8},{4,12},{8,0},{12,4},{16,24},{20,28},{24,16},{28,20},{1,9},{5... | collective-permute-start | bytes 196616 | tf_op jit(solution)/shard_map/ppermute | solution.py:392
  106.5 29.7 %collective-permute-start.22 = (f32[2,512,256]{2,1,0:T(8,128)}, f32[2,512,256]{2,1,0:T(8,128)}, u32[]{:S(2)}, u32[]{:S(2)}) collective-permute-start(f32[2,512,256]{2,1,0:T(8,128)} %collective-permute-done.6.refs_2_), channel_id=1, source_target_pairs={{0,16},{4,20},{8,24},{12,28},{16,0},{20,4},{24,8},{28,12},{1,17},{... | collective-permute-start | bytes 3145736 | tf_op jit(solution)/shard_map/ppermute | solution.py:392
  107.8 28.5 %collective-permute-start.23 = (f32[2,512,256]{2,1,0:T(8,128)}, f32[2,512,256]{2,1,0:T(8,128)}, u32[]{:S(2)}, u32[]{:S(2)}) collective-permute-start(f32[2,512,256]{2,1,0:T(8,128)} %collective-permute-done.7.refs_5_), channel_id=1, source_target_pairs={{0,8},{4,12},{8,0},{12,4},{16,24},{20,28},{24,16},{28,20},{1,9},{5... | collective-permute-start | bytes 3145736 | tf_op jit(solution)/shard_map/ppermute | solution.py:392
  128.0 3.7 %collective-permute-start.20 = (f32[2,1024]{1,0:T(2,128)S(1)}, f32[2,1024]{1,0:T(2,128)S(1)}, u32[]{:S(2)}, u32[]{:S(2)}) collective-permute-start(f32[2,1024]{1,0:T(2,128)S(1)} %get-tuple-element.160), channel_id=1, source_target_pairs={{0,1},{1,0},{2,3},{3,2},{4,5},{5,4},{6,7},{7,6},{8,9},{9,8},{10,11... | collective-permute-start | bytes 24584 | tf_op jit(solution)/shard_map/ppermute | solution.py:392
  131.7 4.5 %collective-permute-start.21 = (f32[2,1024]{1,0:T(2,128)S(1)}, f32[2,1024]{1,0:T(2,128)S(1)}, u32[]{:S(2)}, u32[]{:S(2)}) collective-permute-start(f32[2,1024]{1,0:T(2,128)S(1)} %add.274), channel_id=1, source_target_pairs={{0,2},{1,3},{2,0},{3,1},{4,6},{5,7},{6,4},{7,5},{8,10},{9,11},{10,... | collective-permute-start | bytes 24584 | tf_op jit(solution)/shard_map/ppermute | solution.py:392
  136.3 12.1 %collective-permute-start.26 = (f32[4,1024]{1,0:T(4,128)S(1)}, f32[4,1024]{1,0:T(4,128)S(1)}, u32[]{:S(2)}, u32[]{:S(2)}) collective-permute-start(f32[4,1024]{1,0:T(4,128)S(1)} %pad_maximum_fusion.3.refs_0_), channel_id=1, source_target_pairs={{0,24},{4,28},{8,16},{12,20},{16,8},{20,12},{24,0},{28,4},{1,25},{... | collective-permute-start | bytes 49160 | tf_op jit(solution)/shard_map/ppermute | solution.py:392
  137.8 10.5 %collective-permute-start.25 = (f32[4,1024]{1,0:T(4,128)S(1)}, f32[4,1024]{1,0:T(4,128)S(1)}, u32[]{:S(2)}, u32[]{:S(2)}) collective-permute-start(f32[4,1024]{1,0:T(4,128)S(1)} %pad_maximum_fusion.3.refs_0_), channel_id=1, source_target_pairs={{0,16},{4,20},{8,24},{12,28},{16,0},{20,4},{24,8},{28,12},{1,17},{... | collective-permute-start | bytes 49160 | tf_op jit(solution)/shard_map/ppermute | solution.py:392
  139.1 9.3 %collective-permute-start.24 = (f32[4,1024]{1,0:T(4,128)S(1)}, f32[4,1024]{1,0:T(4,128)S(1)}, u32[]{:S(2)}, u32[]{:S(2)}) collective-permute-start(f32[4,1024]{1,0:T(4,128)S(1)} %pad_maximum_fusion.3.refs_0_), channel_id=1, source_target_pairs={{0,8},{4,12},{8,0},{12,4},{16,24},{20,28},{24,16},{28,20},{1,9},{5... | collective-permute-start | bytes 49160 | tf_op jit(solution)/shard_map/ppermute | solution.py:392
  144.2 14.3 %collective-permute-start.27 = (f32[512,256]{1,0:T(8,128)S(1)}, f32[512,256]{1,0:T(8,128)S(1)}, u32[]{:S(2)}, u32[]{:S(2)}) collective-permute-start(f32[512,256]{1,0:T(8,128)S(1)} %get-tuple-element.246), channel_id=1, source_target_pairs={{0,1},{1,0},{2,3},{3,2},{4,5},{5,4},{6,7},{7,6},{8,9},{9,8},{10,11... | collective-permute-start | bytes 1572872 | tf_op jit(solution)/shard_map/ppermute | solution.py:392
  158.7 14.8 %collective-permute-start.29 = (f32[256,256]{1,0:T(8,128)S(1)}, f32[256,256]{1,0:T(8,128)S(1)}, u32[]{:S(2)}, u32[]{:S(2)}) collective-permute-start(f32[256,256]{1,0:T(8,128)S(1)} %get-tuple-element.185), channel_id=1, source_target_pairs={{0,2},{1,3},{2,0},{3,1},{4,6},{5,7},{6,4},{7,5},{8,10},{9,11},{10,... | collective-permute-start | bytes 786440 | tf_op jit(solution)/shard_map/ppermute | solution.py:392
  161.4 15.4 %collective-permute-start.30 = (f32[512,256]{1,0:T(8,128)S(1)}, f32[512,256]{1,0:T(8,128)S(1)}, u32[]{:S(2)}, u32[]{:S(2)}) collective-permute-start(f32[512,256]{1,0:T(8,128)S(1)} %get-tuple-element.186), channel_id=1, source_target_pairs={{0,1},{1,0},{2,3},{3,2},{4,5},{5,4},{6,7},{7,6},{8,9},{9,8},{10,11... | collective-permute-start | bytes 1572872 | tf_op jit(solution)/shard_map/ppermute | solution.py:392
  161.8 15.0 %collective-permute-start.28 = (f32[1024,256]{1,0:T(8,128)S(1)}, f32[1024,256]{1,0:T(8,128)S(1)}, u32[]{:S(2)}, u32[]{:S(2)}) collective-permute-start(f32[1024,256]{1,0:T(8,128)S(1)} %grad_pass.2), channel_id=1, source_target_pairs={{0,4},{4,0},{8,12},{12,8},{16,20},{20,16},{24,28},{28,24},{1,5},{5... | collective-permute-start | bytes 3145736 | tf_op jit(solution)/shard_map/ppermute | solution.py:392
  179.7 25.6 %collective-permute-start.32 = (f32[512,256]{1,0:T(8,128)S(1)}, f32[512,256]{1,0:T(8,128)}, u32[]{:S(2)}, u32[]{:S(2)}) collective-permute-start(f32[512,256]{1,0:T(8,128)S(1)} %get-tuple-element.222.refs_2_), channel_id=1, source_target_pairs={{0,16},{4,20},{8,24},{12,28},{16,0},{20,4},{24,8},{28,12},{1,17},{... | collective-permute-start | bytes 1572872 | tf_op jit(solution)/shard_map/ppermute | solution.py:392
  180.5 24.8 %collective-permute-start.31 = (f32[512,256]{1,0:T(8,128)S(1)}, f32[512,256]{1,0:T(8,128)S(1)}, u32[]{:S(2)}, u32[]{:S(2)}) collective-permute-start(f32[512,256]{1,0:T(8,128)S(1)} %get-tuple-element.220.refs_0_), channel_id=1, source_target_pairs={{0,8},{4,12},{8,0},{12,4},{16,24},{20,28},{24,16},{28,20},{1,9},{5... | collective-permute-start | bytes 1572872 | tf_op jit(solution)/shard_map/ppermute | solution.py:392
  182.1 18.4 %collective-permute-start.33 = (f32[256,256]{1,0:T(8,128)S(1)}, f32[256,256]{1,0:T(8,128)S(1)}, u32[]{:S(2)}, u32[]{:S(2)}) collective-permute-start(f32[256,256]{1,0:T(8,128)S(1)} %fusion.17.refs_0_), channel_id=1, source_target_pairs={{0,2},{1,3},{2,0},{3,1},{4,6},{5,7},{6,4},{7,5},{8,10},{9,11},{10,... | collective-permute-start | bytes 786440 | tf_op jit(solution)/shard_map/ppermute | solution.py:392
  182.3 23.0 %collective-permute-start.34 = (f32[256,256]{1,0:T(8,128)S(1)}, f32[256,256]{1,0:T(8,128)S(1)}, u32[]{:S(2)}, u32[]{:S(2)}) collective-permute-start(f32[256,256]{1,0:T(8,128)S(1)} %get-tuple-element.252), channel_id=1, source_target_pairs={{0,2},{1,3},{2,0},{3,1},{4,6},{5,7},{6,4},{7,5},{8,10},{9,11},{10,... | collective-permute-start | bytes 786440 | tf_op jit(solution)/shard_map/ppermute | solution.py:392
  205.3 18.8 %collective-permute-start.38 = (f32[512,256]{1,0:T(8,128)S(1)}, f32[512,256]{1,0:T(8,128)S(1)}, u32[]{:S(2)}, u32[]{:S(2)}) collective-permute-start(f32[512,256]{1,0:T(8,128)S(1)} %pad_maximum_fusion), channel_id=1, source_target_pairs={{0,1},{1,0},{2,3},{3,2},{4,5},{5,4},{6,7},{7,6},{8,9},{9,8},{10,11... | collective-permute-start | bytes 1572872 | tf_op jit(solution)/shard_map/ppermute | solution.py:392
  205.4 18.8 %collective-permute-start.35 = (f32[512,256]{1,0:T(8,128)S(1)}, f32[512,256]{1,0:T(8,128)}, u32[]{:S(2)}, u32[]{:S(2)}) collective-permute-start(f32[512,256]{1,0:T(8,128)S(1)} %get-tuple-element.220.refs_0_), channel_id=1, source_target_pairs={{0,16},{4,20},{8,24},{12,28},{16,0},{20,4},{24,8},{28,12},{1,17},{... | collective-permute-start | bytes 1572872 | tf_op jit(solution)/shard_map/ppermute | solution.py:392
  206.4 17.9 %collective-permute-start.36 = (f32[512,256]{1,0:T(8,128)S(1)}, f32[512,256]{1,0:T(8,128)}, u32[]{:S(2)}, u32[]{:S(2)}) collective-permute-start(f32[512,256]{1,0:T(8,128)S(1)} %get-tuple-element.222.refs_2_), channel_id=1, source_target_pairs={{0,8},{4,12},{8,0},{12,4},{16,24},{20,28},{24,16},{28,20},{1,9},{5... | collective-permute-start | bytes 1572872 | tf_op jit(solution)/shard_map/ppermute | solution.py:392
  207.9 16.3 %collective-permute-start.37 = (f32[256,256]{1,0:T(8,128)S(1)}, f32[256,256]{1,0:T(8,128)S(1)}, u32[]{:S(2)}, u32[]{:S(2)}) collective-permute-start(f32[256,256]{1,0:T(8,128)S(1)} %fusion.14.refs_4_), channel_id=1, source_target_pairs={{0,2},{1,3},{2,0},{3,1},{4,6},{5,7},{6,4},{7,5},{8,10},{9,11},{10,... | collective-permute-start | bytes 786440 | tf_op jit(solution)/shard_map/ppermute | solution.py:392
  224.3 12.3 %collective-permute-start.43 = (f32[512,256]{1,0:T(8,128)S(1)}, f32[512,256]{1,0:T(8,128)S(1)}, u32[]{:S(2)}, u32[]{:S(2)}) collective-permute-start(f32[512,256]{1,0:T(8,128)S(1)} %pad_maximum_fusion.1), channel_id=1, source_target_pairs={{0,1},{1,0},{2,3},{3,2},{4,5},{5,4},{6,7},{7,6},{8,9},{9,8},{10,11... | collective-permute-start | bytes 1572872 | tf_op jit(solution)/shard_map/ppermute | solution.py:392
  224.5 12.1 %collective-permute-start.41 = (f32[512,256]{1,0:T(8,128)S(1)}, f32[512,256]{1,0:T(8,128)S(1)}, u32[]{:S(2)}, u32[]{:S(2)}) collective-permute-start(f32[512,256]{1,0:T(8,128)S(1)} %get-tuple-element.220.refs_0_), channel_id=1, source_target_pairs={{0,4},{4,0},{8,12},{12,8},{16,20},{20,16},{24,28},{28,24},{1,5},{5... | collective-permute-start | bytes 1572872 | tf_op jit(solution)/shard_map/ppermute | solution.py:392
  224.5 14.4 %collective-permute-start.39 = (f32[512,256]{1,0:T(8,128)S(1)}, f32[512,256]{1,0:T(8,128)}, u32[]{:S(2)}, u32[]{:S(2)}) collective-permute-start(f32[512,256]{1,0:T(8,128)S(1)} %collective-permute-done.31.refs_4_), channel_id=1, source_target_pairs={{0,16},{4,20},{8,24},{12,28},{16,0},{20,4},{24,8},{28,12},{1,17},{... | collective-permute-start | bytes 1572872 | tf_op jit(solution)/shard_map/ppermute | solution.py:392
  225.9 13.1 %collective-permute-start.42 = (f32[512,256]{1,0:T(8,128)S(1)}, f32[512,256]{1,0:T(8,128)S(1)}, u32[]{:S(2)}, u32[]{:S(2)}) collective-permute-start(f32[512,256]{1,0:T(8,128)S(1)} %get-tuple-element.222.refs_2_), channel_id=1, source_target_pairs={{0,4},{4,0},{8,12},{12,8},{16,20},{20,16},{24,28},{28,24},{1,5},{5... | collective-permute-start | bytes 1572872 | tf_op jit(solution)/shard_map/ppermute | solution.py:392
  226.1 14.4 %collective-permute-start.40 = (f32[512,256]{1,0:T(8,128)}, f32[512,256]{1,0:T(8,128)}, u32[]{:S(2)}, u32[]{:S(2)}) collective-permute-start(f32[512,256]{1,0:T(8,128)} %collective-permute-done.32.refs_10_), channel_id=1, source_target_pairs={{0,8},{4,12},{8,0},{12,4},{16,24},{20,28},{24,16},{28,20},{1,9},{5... | collective-permute-start | bytes 1572872 | tf_op jit(solution)/shard_map/ppermute | solution.py:392
  240.6 2.6 %collective-permute-start.44 = (f32[512,256]{1,0:T(8,128)S(1)}, f32[512,256]{1,0:T(8,128)S(1)}, u32[]{:S(2)}, u32[]{:S(2)}) collective-permute-start(f32[512,256]{1,0:T(8,128)S(1)} %collective-permute-done.31.refs_4_), channel_id=1, source_target_pairs={{0,4},{4,0},{8,12},{12,8},{16,20},{20,16},{24,28},{28,24},{1,5},{5... | collective-permute-start | bytes 1572872 | tf_op jit(solution)/shard_map/ppermute | solution.py:392
  240.6 5.7 %collective-permute-start.45 = (f32[512,256]{1,0:T(8,128)}, f32[512,256]{1,0:T(8,128)}, u32[]{:S(2)}, u32[]{:S(2)}) collective-permute-start(f32[512,256]{1,0:T(8,128)} %collective-permute-done.36.refs_6_), channel_id=1, source_target_pairs={{0,4},{4,0},{8,12},{12,8},{16,20},{20,16},{24,28},{28,24},{1,5},{5... | collective-permute-start | bytes 1572872 | tf_op jit(solution)/shard_map/ppermute | solution.py:392
  241.1 5.2 %collective-permute-start.46 = (f32[512,256]{1,0:T(8,128)}, f32[512,256]{1,0:T(8,128)}, u32[]{:S(2)}, u32[]{:S(2)}) collective-permute-start(f32[512,256]{1,0:T(8,128)} %collective-permute-done.35.refs_8_), channel_id=1, source_target_pairs={{0,4},{4,0},{8,12},{12,8},{16,20},{20,16},{24,28},{28,24},{1,5},{5... | collective-permute-start | bytes 1572872 | tf_op jit(solution)/shard_map/ppermute | solution.py:392
  241.1 5.2 %collective-permute-start.47 = (f32[512,256]{1,0:T(8,128)}, f32[512,256]{1,0:T(8,128)}, u32[]{:S(2)}, u32[]{:S(2)}) collective-permute-start(f32[512,256]{1,0:T(8,128)} %collective-permute-done.32.refs_10_), channel_id=1, source_target_pairs={{0,4},{4,0},{8,12},{12,8},{16,20},{20,16},{24,28},{28,24},{1,5},{5... | collective-permute-start | bytes 1572872 | tf_op jit(solution)/shard_map/ppermute | solution.py:392
  241.6 4.7 %collective-permute-start.48 = (f32[512,256]{1,0:T(8,128)}, f32[512,256]{1,0:T(8,128)}, u32[]{:S(2)}, u32[]{:S(2)}) collective-permute-start(f32[512,256]{1,0:T(8,128)} %collective-permute-done.39.refs_12_), channel_id=1, source_target_pairs={{0,4},{4,0},{8,12},{12,8},{16,20},{20,16},{24,28},{28,24},{1,5},{5... | collective-permute-start | bytes 1572872 | tf_op jit(solution)/shard_map/ppermute | solution.py:392
  244.0 2.6 %collective-permute-start.49 = (f32[512,256]{1,0:T(8,128)}, f32[512,256]{1,0:T(8,128)}, u32[]{:S(2)}, u32[]{:S(2)}) collective-permute-start(f32[512,256]{1,0:T(8,128)} %collective-permute-done.40.refs_14_), channel_id=1, source_target_pairs={{0,4},{4,0},{8,12},{12,8},{16,20},{20,16},{24,28},{28,24},{1,5},{5... | collective-permute-start | bytes 1572872 | tf_op jit(solution)/shard_map/ppermute | solution.py:392
  (20 other events, 133.0 us)
